TPU v7x, 256 devices: a whole 4x4x8 slice. The times are simulated.
256 devices in a mesh: path: 4 (over z_lo), tensor: 8 (over y, core), problem: 8 (over x, z_hi).
Axes of the slice: x: 4, y: 4, z: 8 (z_hi: 2, z_lo: 4; z = z_hi * 4 + z_lo), core: 2. Of those that a mesh axis runs over, the one named last changes fastest.
Arguments:
- decode_in: bfloat16 [64, 4, 4096], P(('problem', 'path')), parts along dimension 0, may hold values from -6 to 6
- path_embed: bfloat16 [8, 4096], P('path'), may hold values from -6 to 6
- summary_in: bfloat16 [2048, 4096], P(('problem', 'path', 'tensor')), parts along dimension 0, may hold values from -6 to 6
- norm_gain: bfloat16 [4096], replicated, may hold values from 0.099609375 to 1.8984375
- query_gain: bfloat16 [128], replicated, may hold values from 0.099609375 to 1.8984375
- key_norm_gain: bfloat16 [128], replicated, may hold values from 1 to 4
- w_query: bfloat16 [4096, 4096], P(None, 'tensor'), may hold values from -0.09375 to 0.09375
- key_weight: bfloat16 [4096, 1024], P(None, 'tensor'), may hold values from -0.09375 to 0.09375
- w_value: bfloat16 [4096, 1024], P(None, 'tensor'), may hold values from -0.09375 to 0.09375
- w_out: bfloat16 [4096, 4096], P('tensor'), may hold values from -0.09375 to 0.09375
- key_cache: bfloat16 [64, 2048, 1024], P(('problem', 'path'), None, 'tensor'), parts along dimension 0, may hold values from -240 to 240
- value_cache: bfloat16 [64, 2048, 1024], P(('problem', 'path'), None, 'tensor'), parts along dimension 0, may hold values from -6 to 6
- lengths: int32 [64], P('problem'), parts along dimension 0, may hold values from 512 to 2044, as said below
Outputs:
- decode_out: bfloat16 [64, 4, 4096], P(('problem', 'path'), None, 'tensor'), parts along dimension 0
- summary_out: bfloat16 [2048, 4096], P(('problem', 'path', 'tensor')), parts along dimension 0
There are 8 independent parts, one for each index of `problem`. A program takes and returns all parts, laid end to end along the dimension named above; an argument that names none is the same for every part. Nothing has to cross between parts.
Inputs may be any that keep to these rules, and one draw needn't show every extreme that they name: `lengths`: every path has at least one valid entry; at least one path has exactly 2044 and at least one exactly 512.
All inputs are finite; a program needn't handle non-finite values.
Results may differ from a plain program's by a relative error of at most 0.027.
The roundings to bfloat16 on the way count: a program that leaves them out, or rounds other values in their place, can miss the bound.
Values may be sent and summed in bfloat16 or wider, within the bound.
No kernel may reach another device: no remote copies, remote signals or barrier semaphores. Data moves between devices by JAX's collectives and lax.ppermute only.
A program may use at most 128 MiB of HBM per device.

v0:
```python
import math

import jax
import jax.numpy as jnp
from jax import lax
from jax.sharding import PartitionSpec as P

epsilon = 1e-06
rope_base = 1000000.0


def normalize(rows, gain):
    factor = lax.rsqrt(jnp.mean(rows * rows, axis=-1, keepdims=True) + epsilon)
    return rows * factor * gain.astype(rows.dtype)


def rotate(vectors, positions):
    head_width = vectors.shape[-1]
    half_width = head_width // 2
    exponent = jnp.arange(half_width).astype(vectors.dtype) * (2.0 / head_width)
    freqs = jnp.exp(-math.log(rope_base) * exponent)
    angles = positions.astype(vectors.dtype)[:, None, None] * freqs
    cosine = jnp.cos(angles)
    sine = jnp.sin(angles)
    leading = vectors[..., :half_width]
    trailing = vectors[..., half_width:]
    return jnp.concatenate(
        [leading * cosine - trailing * sine, trailing * cosine + leading * sine], axis=-1
    )


def project_rows(normed, weight, gain, positions):
    projected = jnp.dot(normed, weight, preferred_element_type=jnp.float32)
    projected = projected.reshape(projected.shape[0], -1, gain.shape[0])
    return rotate(normalize(projected, gain), positions).astype(jnp.bfloat16)


def score_parts(query, key_parts):
    result = []
    for key_rows, allowed in key_parts:
        raw_scores = jnp.einsum(
            "rkgd,nkd->rkgn", query, key_rows, preferred_element_type=jnp.float32
        ) / math.sqrt(query.shape[-1])
        result.append(jnp.where(allowed[:, None, None, :], raw_scores, -jnp.inf))
    return result


def part_peak(scored):
    peak = jnp.max(scored[0], axis=-1)
    for scores_part in scored[1:]:
        peak = jnp.maximum(peak, jnp.max(scores_part, axis=-1))
    return peak


def weigh_parts(scored, value_parts, peak):
    totals = jnp.zeros(peak.shape, jnp.float32)
    mixture = None
    for scores_part, values_part in zip(scored, value_parts):
        weights_part = jnp.exp(scores_part - peak[..., None])
        totals = totals + jnp.sum(weights_part, axis=-1)
        term = jnp.einsum(
            "rkgn,nkd->rkgd",
            weights_part.astype(jnp.bfloat16),
            values_part,
            preferred_element_type=jnp.float32,
        )
        mixture = term if mixture is None else mixture + term
    return (mixture, totals)


def body(
    decode_in,
    path_embed,
    summary_in,
    norm_gain,
    query_gain,
    key_norm_gain,
    w_query,
    key_weight,
    w_value,
    w_out,
    key_cache,
    value_cache,
    lengths,
):
    path_rows, step_count, model_width = decode_in.shape
    head_width = query_gain.shape[0]
    kv_local = key_weight.shape[1] // head_width
    group_size = w_query.shape[1] // key_weight.shape[1]
    cache_len = key_cache.shape[1]
    path_at = lax.axis_index("path")
    own_len = lax.dynamic_slice_in_dim(lengths, path_at * path_rows, path_rows, 0)
    hidden = decode_in.astype(jnp.float32) + path_embed.astype(jnp.float32)[:, None, :]
    normed = (
        normalize(hidden, norm_gain)
        .astype(jnp.bfloat16)
        .reshape(path_rows * step_count, model_width)
    )
    positions = (own_len[:, None] + jnp.arange(step_count, dtype=jnp.int32)[None, :]).reshape(-1)
    dquery = project_rows(normed, w_query, query_gain, positions).reshape(
        path_rows, step_count, kv_local, group_size, head_width
    )
    dkey = project_rows(normed, key_weight, key_norm_gain, positions).reshape(
        path_rows, step_count, kv_local, head_width
    )
    dvalue = (
        jnp.dot(normed, w_value, preferred_element_type=jnp.float32)
        .astype(jnp.bfloat16)
        .reshape(path_rows, step_count, kv_local, head_width)
    )
    cache_keys = key_cache.reshape(path_rows, cache_len, kv_local, head_width)
    cache_values = value_cache.reshape(path_rows, cache_len, kv_local, head_width)
    cached = jnp.einsum(
        "pskgd,plkd->pskgl", dquery, cache_keys, preferred_element_type=jnp.float32
    ) / math.sqrt(head_width)
    cache_live = jnp.arange(cache_len, dtype=jnp.int32)[None, :] < own_len[:, None]
    cached = jnp.where(cache_live[:, None, None, None, :], cached, -jnp.inf)
    recent = jnp.einsum(
        "pskgd,ptkd->pskgt", dquery, dkey, preferred_element_type=jnp.float32
    ) / math.sqrt(head_width)
    step_index = jnp.arange(step_count, dtype=jnp.int32)
    causal = step_index[None, :] <= step_index[:, None]
    recent = jnp.where(causal[None, :, None, None, :], recent, -jnp.inf)
    peak = jnp.maximum(jnp.max(cached, axis=-1), jnp.max(recent, axis=-1))[..., None]
    cached_weights = jnp.exp(cached - peak)
    recent_weights = jnp.exp(recent - peak)
    totals = jnp.sum(cached_weights, axis=-1) + jnp.sum(recent_weights, axis=-1)
    mixture = jnp.einsum(
        "pskgl,plkd->pskgd",
        cached_weights.astype(jnp.bfloat16),
        cache_values,
        preferred_element_type=jnp.float32,
    )
    mixture = mixture + jnp.einsum(
        "pskgt,ptkd->pskgd",
        recent_weights.astype(jnp.bfloat16),
        dvalue,
        preferred_element_type=jnp.float32,
    )
    dattn = (mixture / totals[..., None]).astype(jnp.bfloat16).reshape(path_rows * step_count, -1)
    dterms = jnp.dot(dattn, w_out, preferred_element_type=jnp.float32).reshape(
        path_rows, step_count, model_width
    )
    decode_out = lax.psum_scatter(
        dterms.astype(jnp.bfloat16), "tensor", scatter_dimension=2, tiled=True
    )
    own_rows = summary_in.shape[0]
    block_rows = own_rows * lax.axis_size("tensor")
    path_count_axis = lax.axis_size("path")
    all_count = block_rows * path_count_axis
    block_first = path_at * block_rows
    block_positions = cache_len + block_first + jnp.arange(block_rows, dtype=jnp.int32)
    gathered = lax.all_gather(summary_in, ("path", "tensor"), axis=0, tiled=True)
    normed_all = normalize(gathered.astype(jnp.float32), norm_gain).astype(jnp.bfloat16)
    all_pos = cache_len + jnp.arange(all_count, dtype=jnp.int32)
    query_all = project_rows(normed_all, w_query, query_gain, all_pos)
    block_rows_normed = lax.dynamic_slice_in_dim(normed_all, block_first, block_rows, 0)
    query_all = query_all.reshape(all_count, kv_local, group_size, head_width)
    summary_key_rows = project_rows(block_rows_normed, key_weight, key_norm_gain, block_positions)
    svalue = (
        jnp.dot(block_rows_normed, w_value, preferred_element_type=jnp.float32)
        .astype(jnp.bfloat16)
        .reshape(block_rows, kv_local, head_width)
    )
    live_flat = jnp.broadcast_to(cache_live.reshape(1, -1), (all_count, path_rows * cache_len))
    decode_flat = jnp.ones((all_count, path_rows * step_count), dtype=bool)
    query_index = jnp.arange(all_count, dtype=jnp.int32)
    summary_causal_mask = (block_first + jnp.arange(block_rows, dtype=jnp.int32))[
        None, :
    ] <= query_index[:, None]
    key_parts = [
        (cache_keys.reshape(-1, kv_local, head_width), live_flat),
        (dkey.reshape(-1, kv_local, head_width), decode_flat),
        (summary_key_rows, summary_causal_mask),
    ]
    value_parts = [
        cache_values.reshape(-1, kv_local, head_width),
        dvalue.reshape(-1, kv_local, head_width),
        svalue,
    ]
    scored = score_parts(query_all, key_parts)
    local_peak = part_peak(scored)
    peak_all = lax.pmax(local_peak, "path")
    mixture_all, totals_all = weigh_parts(scored, value_parts, peak_all)
    merged_mix, merged_tot = (
        lax.psum_scatter(
            mixture_all.reshape(all_count, -1).astype(jnp.bfloat16),
            "path",
            scatter_dimension=0,
            tiled=True,
        ).astype(jnp.float32),
        lax.psum_scatter(
            totals_all.reshape(all_count, -1).astype(jnp.bfloat16),
            "path",
            scatter_dimension=0,
            tiled=True,
        ).astype(jnp.float32),
    )
    sattn = merged_mix.reshape(block_rows, kv_local, group_size, head_width) / merged_tot.reshape(
        block_rows, kv_local, group_size, 1
    )
    sattn = sattn.astype(jnp.bfloat16).reshape(block_rows, -1)
    summary_out = lax.psum_scatter(
        jnp.dot(sattn, w_out, preferred_element_type=jnp.float32).astype(jnp.bfloat16),
        "tensor",
        scatter_dimension=0,
        tiled=True,
    )
    return (decode_out, summary_out)


def solution(mesh):
    in_specs = (
        P(("problem", "path"), None, None),
        P("path", None),
        P(("problem", "path", "tensor"), None),
        P(),
        P(),
        P(),
        P(None, "tensor"),
        P(None, "tensor"),
        P(None, "tensor"),
        P("tensor", None),
        P(("problem", "path"), None, "tensor"),
        P(("problem", "path"), None, "tensor"),
        P("problem"),
    )
    out_specs = (P(("problem", "path"), None, "tensor"), P(("problem", "path", "tensor"), None))
    return jax.shard_map(body, mesh=mesh, in_specs=in_specs, out_specs=out_specs, check_vma=False)
```

profile of v0, /device:TPU:1, one launch (start us, length us, event | category | flops | bytes accessed | tf_op | source)
XLA Modules:
  0.0 243.7 jit_solution(7208609051839673492)
XLA Ops:
  13.7 6.4 %copy.43 = bf16[512,4096]{1,0:T(8,128)(2,1)} copy(bf16[512,4096]{0,1:T(8,128)(2,1)} %bitcast.196) | data formatting | bytes 8388608 | tf_op jit(solution)/shard_map/dot_general | solution.py:33
  20.1 3.6 %multiply_reduce_fusion.3 = (f32[8,4]{0,1:T(4,128)S(1)}, f32[8,4,128]{2,0,1:T(8,128)S(1)}) fusion(bf16[8,4096,1]{1,0,2:T(8,128)(2,1)S(1)} %reshape.691, bf16[4,128,4096]{2,1,0:T(8,128)(2,1)} %bitcast.194), kind=kOutput, calls=%fused_computation.94 | convolution fusion | flops 33562592 | bytes 4276352 | tf_op jit(solution)/shard_map/dot_general | solution.py:33
  26.2 1.2 multiply_cosine_fusion
  27.6 1.6 convolution_bitcast_fusion
  29.2 45.1 %all-gather.2.cloned.1.call-done = bf16[256,4096]{1,0:T(8,128)(2,1)} async-done(((bf16[8,4096]{1,0:T(8,128)(2,1)}), bf16[256,4096]{1,0:T(8,128)(2,1)}) %all-gather.2.cloned.1.call-update) | async-done | bytes 2097168 | tf_op jit(solution)/shard_map/all_gather | solution.py:153
  74.3 2.2 fusion.8
  76.6 2.2 fusion.10
  78.8 2.0 fusion.91
  83.0 1.3 fusion.29
  85.0 7.1 %fusion.3 = (f32[256,4]{0,1:T(4,128)S(1)}, f32[256,4,4096]{2,0,1:T(8,128)}) fusion(pred[4096]{0:T(1024)(128)(4,1)S(1)} %lt.34, bf16[4096,128,1]{1,0,2:T(8,128)(2,1)S(1)} %bitcast.193, bf16[256,4,64]{2,0,1:T(8,128)(2,1)S(1)} %get-tuple-element.3, bf16[256,4,64]{2,0,1:T(8,128)(2,1)S(1)} %get-tuple-element.2), kind=kOutput, calls=%fused_computation.5 | convolution fusion | flops 1086848000 | bytes 18096128 | tf_op jit(solution)/shard_map/rkgd,nkd->rkgn/dot_general | solution.py:41
  92.4 8.4 %pmax.7 = f32[256,4]{0,1:T(4,128)S(1)} all-reduce(f32[256,4]{0,1:T(4,128)S(1)} %maximum_maximum_fusion), channel_id=1, replica_groups=mesh['path'=4,'tensor'=8,'problem'=8] {'path'}, use_global_device_ids=true, to_apply=%region_14.15 | all-reduce | flops 1024 | bytes 8192 | tf_op jit(solution)/shard_map/pmax | solution.py:183
  101.0 9.0 %fusion.1 = f32[256,4]{0,1:T(4,128)S(1)} fusion(f32[256,4,4096]{2,0,1:T(8,128)} %get-tuple-element.27, f32[256,4]{0,1:T(4,128)S(1)} %pmax.7, pred[4096]{0:T(1024)(128)(4,1)S(1)} %lt.34), kind=kLoop, calls=%fused_computation.3 | loop fusion | flops 16776192 | bytes 16789504 | tf_op jit(solution)/shard_map/reduce_sum | solution.py:60
  109.9 1.7 copy-done.1
  111.6 5.6 %fusion.15 = f32[128,256,4]{1,0,2:T(8,128)} fusion(bf16[4096,128,1]{1,0,2:T(8,128)(2,1)} %bitcast.198, f32[256,4,4096]{2,0,1:T(8,128)S(1)} %copy-done.1, f32[256,4]{0,1:T(4,128)S(1)} %pmax.7, pred[4096]{0:T(1024)(128)(4,1)S(1)} %lt.34), kind=kOutput, calls=%fused_computation.21 | convolution fusion | flops 1090519040 | bytes 18358272 | tf_op jit(solution)/shard_map/rkgn,nkd->rkgd/dot_general | solution.py:61
  118.1 1.3 convolution_add_fusion.1
  119.4 1.6 fusion.18
  122.1 2.9 %convolution_convert_fusion.1 = bf16[2,4,4096]{2,1,0:T(4,128)(2,1)S(1)} fusion(bf16[2,4,512]{2,1,0:T(4,128)(2,1)S(1)} %dot_general.74, bf16[512,4096]{1,0:T(8,128)(2,1)} %param.22), kind=kOutput, calls=%fused_computation.12 | convolution fusion | flops 33587200 | bytes 4268032 | tf_op jit(solution)/shard_map/dot_general | solution.py:141
  125.0 2.9 %copy.45 = bf16[2,4,4096]{1,0,2:T(2,128)(2,1)S(1)} copy(bf16[2,4,4096]{2,1,0:T(4,128)(2,1)S(1)} %convolution_convert_fusion.1) | data formatting | bytes 131072
  127.9 1.8 reshape.704
  129.8 10.8 %reduce-scatter.17.cloned.1.call-done = bf16[64,4]{1,0:T(8,128)(2,1)} async-done(((bf16[256,4]{1,0:T(8,128)(2,1)}), bf16[64,4]{1,0:T(8,128)(2,1)}) %reduce-scatter.17.cloned.1.call-update) | async-done | bytes 528
  141.3 26.0 %reduce-scatter.15.cloned.1.call-done = bf16[64,512]{1,0:T(8,128)(2,1)} async-done(((bf16[256,512]{1,0:T(8,128)(2,1)}), bf16[64,512]{1,0:T(8,128)(2,1)}) %reduce-scatter.15.cloned.1.call-update) | async-done | bytes 65552
  168.4 3.9 %convolution_convert_fusion = bf16[64,4096]{1,0:T(8,128)(2,1)} fusion(bf16[64,512]{0,1:T(8,128)(2,1)S(1)} %fusion.34, bf16[512,4096]{1,0:T(8,128)(2,1)} %param.22), kind=kOutput, calls=%fused_computation.11 | convolution fusion | flops 268697600 | bytes 4784128 | tf_op jit(solution)/shard_map/dot_general | solution.py:204
  172.3 29.6 %reduce-scatter.13.cloned.1.call-done = bf16[512,8]{1,0:T(8,128)(2,1)} async-done(((bf16[4096,8]{1,0:T(8,128)(2,1)}), bf16[512,8]{1,0:T(8,128)(2,1)}) %reduce-scatter.13.cloned.1.call-update) | async-done | bytes 8208
  203.7 33.6 %reduce-scatter.11.cloned.1.call-done = bf16[8,4096]{1,0:T(8,128)(2,1)} async-done(((bf16[64,4096]{1,0:T(8,128)(2,1)}), bf16[8,4096]{1,0:T(8,128)(2,1)}) %reduce-scatter.11.cloned.1.call-update) | async-done | bytes 65552 | tf_op jit(solution)/shard_map/reduce_scatter | solution.py:203
  (90 shorter events, 17.9 us)
Async XLA Ops:
  7.2 17.8 %copy-start = (bf16[2,2048,128]{2,1,0:T(8,128)(2,1)S(1)}, bf16[2,2048,128]{2,1,0:T(8,128)(2,1)}, u32[]{:S(2)}) copy-start(bf16[2,2048,128]{2,1,0:T(8,128)(2,1)} %param.23) | copy-start | bytes 3145732
  7.2 67.1 %all-gather.2.cloned.1.call-start = ((), (), s32[]{:S(2)}) async-start(), calls=%async_computation.4 | async-start | bytes 2162688 | tf_op jit(solution)/shard_map/all_gather | solution.py:153
  7.9 132.6 %reduce-scatter.17.cloned.1.call-start = ((), (), s32[]{:S(2)}) async-start(), calls=%async_computation.8 | async-start | bytes 81920
  20.1 3.9 %copy-start.4 = (bf16[4096,128]{1,0:T(8,128)(2,1)S(1)}, bf16[4096,128]{1,0:T(8,128)(2,1)}, u32[]{:S(2)}) copy-start(bf16[4096,128]{1,0:T(8,128)(2,1)} %param.20) | copy-start | bytes 3145732
  20.1 7.3 %copy-start.5 = (bf16[4096,128]{1,0:T(8,128)(2,1)S(1)}, bf16[4096,128]{1,0:T(8,128)(2,1)}, u32[]{:S(2)}) copy-start(bf16[4096,128]{1,0:T(8,128)(2,1)} %param.21) | copy-start | bytes 3145732
  74.3 4.5 %copy-start.3 = (bf16[4096,512]{1,0:T(8,128)(2,1)S(1)}, bf16[4096,512]{1,0:T(8,128)(2,1)}, u32[]{:S(2)}) copy-start(bf16[4096,512]{1,0:T(8,128)(2,1)} %param.19) | copy-start | bytes 12582916
  78.8 2.5 %copy-start.2 = (bf16[256,4096]{1,0:T(8,128)(2,1)}, bf16[256,4096]{1,0:T(8,128)(2,1)S(1)}, u32[]{:S(2)}) copy-start(bf16[256,4096]{1,0:T(8,128)(2,1)S(1)} %fusion.10) | copy-start | bytes 6291460
  80.9 3.6 %copy-start.6 = (f32[256,64]{1,0:T(8,128)S(1)}, f32[256,64]{1,0:T(8,128)}, u32[]{:S(2)}) copy-start(f32[256,64]{1,0:T(8,128)} %get-tuple-element.12) | copy-start | bytes 196612
  80.9 3.6 %copy-start.7 = (f32[256,64]{1,0:T(8,128)S(1)}, f32[256,64]{1,0:T(8,128)}, u32[]{:S(2)}) copy-start(f32[256,64]{1,0:T(8,128)} %get-tuple-element.13) | copy-start | bytes 196612
  100.9 10.7 %copy-start.1 = (f32[256,4,4096]{2,0,1:T(8,128)S(1)}, f32[256,4,4096]{2,0,1:T(8,128)}, u32[]{:S(2)}) copy-start(f32[256,4,4096]{2,0,1:T(8,128)} %get-tuple-element.27) | copy-start | bytes 50331652
  118.1 49.3 %reduce-scatter.15.cloned.1.call-start = ((), (), s32[]{:S(2)}) async-start(), calls=%async_computation.7 | async-start | bytes 327680
  121.9 79.9 %reduce-scatter.13.cloned.1.call-start = ((), (), s32[]{:S(2)}) async-start(), calls=%async_computation.6 | async-start | bytes 1179648
  129.7 107.5 %reduce-scatter.11.cloned.1.call-start = ((), (), s32[]{:S(2)}) async-start(), calls=%async_computation.5 | async-start | bytes 589824 | tf_op jit(solution)/shard_map/reduce_scatter | solution.py:203
Sparse Core Ops, SparseCore 0:
  9.9 64.4 all-gather.1
  118.2 22.3 reduce-scatter.16
  143.2 24.1 reduce-scatter.14
  169.8 32.0 reduce-scatter.12
  204.8 32.3 reduce-scatter.10
where the time goes:
time: 246 us; the launch traced here: 244 us
  waiting for transfers between devices  146 us (59%)
  matrix products  32.1 us (13%)
  other arithmetic  22.8 us (9%)
  local copies, waits for them, and re-layouts  20.4 us (8%)
  between operations  14.1 us (6%)
  blocking collectives  8.41 us (3%)
    unnamed x8, waiting for transfers between devices  67.1 us
    all_gather x1, waiting for transfers between devices, body(): lax.all_gather(summary_in, ('path', 'tensor'), axis=0, tiled=True)  45.1 us
    reduce_scatter x1, waiting for transfers between devices, body(): lax.psum_scatter(jnp.dot(sattn, w_out, preferred_element_type=jnp.float32...  33.6 us
    unnamed x24, local copies, waits for them, and re-layouts  11.6 us
    reduce_sum x3, other arithmetic, weigh_parts(): totals = totals + jnp.sum(weights_part, axis=-1)  9.08 us
    dot_general x3, matrix products, weigh_parts(): jnp.einsum('rkgn,nkd->rkgd', weights_part.astype(jnp.bfloat16), values_pa...  8.56 us
    pmax x1, blocking collectives, body(): peak_all = lax.pmax(local_peak, 'path')  8.41 us
    dot_general x3, matrix products, score_parts(): jnp.einsum('rkgd,nkd->rkgn', query, key_rows, preferred_element_type=jnp....  7.65 us
  transfers between devices with their start and end apart: 5, of which 5 were waited for; matrix products, arithmetic and copies ran while one was open for 16% of the time, Pallas kernels for 0%

commit v1 on v0

v1 whole, which is shorter than its diff:
```python
import functools
import math

import jax
import jax.numpy as jnp
from jax import lax
from jax.experimental import pallas as pl
from jax.experimental.pallas import tpu as pltpu
from jax.sharding import PartitionSpec as P

EPS = 1e-06
ROPE_BASE = 1000000.0
HEAD = 128
GROUP = 4
STEPS = 4
SCALE2 = math.log2(math.e) / math.sqrt(HEAD)
NEG = -1e30
F32 = jnp.float32
BF16 = jnp.bfloat16
MIB = 1024 * 1024


def dot(a, b):
    return lax.dot_general(a, b, (((1,), (0,)), ((), ())), preferred_element_type=F32)


def dot_t(a, b):
    return lax.dot_general(a, b, (((1,), (1,)), ((), ())), preferred_element_type=F32)


def rms(rows, gain):
    factor = lax.rsqrt(jnp.mean(rows * rows, axis=-1, keepdims=True) + EPS)
    return rows * factor * gain


def rope_tables(positions):
    lane = lax.broadcasted_iota(jnp.int32, positions.shape, 1)
    exponent = (lane % (HEAD // 2)).astype(F32) * (2.0 / HEAD)
    angles = positions * jnp.exp(-math.log(ROPE_BASE) * exponent)
    sine = jnp.sin(angles)
    return jnp.cos(angles), jnp.where(lane < HEAD // 2, -sine, sine)


def rotate(v, cosine, sine):
    return v * cosine + pltpu.roll(v, HEAD // 2, 1) * sine


def decode_kernel(
    lengths, decode_in, embed, norm_gain, query_gain, key_gain, w_query, w_key, w_value, w_out,
    keys, values, dterms, dkey, dvalue, cos_out, sin_out,
):
    path = lax.axis_index("path")
    len0 = lengths[path * 2]
    len1 = lengths[path * 2 + 1]
    hidden = jnp.concatenate(
        [decode_in[i].astype(F32) + embed[i : i + 1, :].astype(F32) for i in range(2)], axis=0
    )
    normed = rms(hidden, norm_gain[...].astype(F32)).astype(BF16)
    row = lax.broadcasted_iota(jnp.int32, (8, HEAD), 0)
    position = jnp.where(row < STEPS, len0 + row, len1 + row - STEPS).astype(F32)
    cosine, sine = rope_tables(position)
    query = dot(normed, w_query[...])
    qgain = query_gain[...].astype(F32)
    heads = [
        rotate(rms(query[:, h * HEAD : (h + 1) * HEAD], qgain), cosine, sine)
        for h in range(GROUP)
    ]
    new_key = rotate(rms(dot(normed, w_key[...]), key_gain[...].astype(F32)), cosine, sine)
    new_key = new_key.astype(BF16)
    new_value = dot(normed, w_value[...]).astype(BF16)
    dkey[...] = new_key.astype(F32)
    dvalue[...] = new_value.astype(F32)
    mixed = []
    for i, length in enumerate((len0, len1)):
        q = jnp.concatenate([x[i * STEPS : (i + 1) * STEPS] for x in heads], axis=0).astype(BF16)
        cached = dot_t(q, keys[i])
        slot = lax.broadcasted_iota(jnp.int32, cached.shape, 1)
        cached = jnp.where(slot < length, cached, NEG)
        recent = dot_t(q, new_key)
        r_row = lax.broadcasted_iota(jnp.int32, recent.shape, 0) % STEPS
        r_col = lax.broadcasted_iota(jnp.int32, recent.shape, 1) - i * STEPS
        recent = jnp.where((r_col >= 0) & (r_col <= r_row), recent, NEG)
        peak = jnp.maximum(
            jnp.max(cached, axis=-1, keepdims=True), jnp.max(recent, axis=-1, keepdims=True)
        )
        wc = jnp.exp2((cached - peak) * SCALE2)
        wr = jnp.exp2((recent - peak) * SCALE2)
        total = jnp.sum(wc, axis=-1, keepdims=True) + jnp.sum(wr, axis=-1, keepdims=True)
        mix = dot(wc.astype(BF16), values[i]) + dot(wr.astype(BF16), new_value)
        mix = mix / total
        mixed.append(
            jnp.concatenate([mix[h * STEPS : (h + 1) * STEPS] for h in range(GROUP)], axis=1)
        )
    attn = jnp.concatenate(mixed, axis=0).astype(BF16)
    width = dterms.shape[2]
    for t in range(dterms.shape[0]):
        dterms[t] = dot(attn, w_out[:, t * width : (t + 1) * width]).astype(BF16)
    rows = cos_out.shape[0]
    row = lax.broadcasted_iota(jnp.int32, (rows, HEAD), 0)
    cosine, sine = rope_tables((keys.shape[1] + path * rows + row).astype(F32))
    cos_out[...] = cosine
    sin_out[...] = sine


def project_kernel(*refs):
    rows_in = refs[:8]
    (
        norm_gain, query_gain, key_gain, w_query, w_key, w_value, cosine, sine, dkey, dvalue,
        query_out, tail_keys, tail_values, normed_f32,
    ) = refs[8:]
    own = lax.axis_index("tensor")
    gain = norm_gain[...].astype(F32)
    for j in range(8):
        at = pl.multiple_of((own ^ j) * 8, 8)
        normed_f32[pl.ds(at, 8), :] = rms(rows_in[j][...].astype(F32), gain)
    normed = normed_f32[...].astype(BF16)
    cos = cosine[...]
    sin = sine[...]
    query = dot(normed, w_query[...])
    qgain = query_gain[...].astype(F32)
    for h in range(GROUP):
        at = slice(h * HEAD, (h + 1) * HEAD)
        query_out[:, at] = rotate(rms(query[:, at], qgain), cos, sin).astype(BF16)
    key = rotate(rms(dot(normed, w_key[...]), key_gain[...].astype(F32)), cos, sin)
    value = dot(normed, w_value[...])
    pad = jnp.zeros((56, HEAD), F32)
    tail_keys[...] = jnp.concatenate([key, dkey[...], pad], axis=0).astype(BF16)
    tail_values[...] = jnp.concatenate([value, dvalue[...], pad], axis=0).astype(BF16)


def attend_kernel(flip, lengths, query, keys, values, tail_keys, tail_values, out):
    path = lax.axis_index("path")
    block = path ^ flip
    rows = query.shape[0]
    q = jnp.concatenate(
        [query[:, h * HEAD : (h + 1) * HEAD] for h in range(GROUP)], axis=0
    )
    total_rows = rows * GROUP
    scores = []
    for i in range(2):
        s = dot_t(q, keys[i])
        slot = lax.broadcasted_iota(jnp.int32, s.shape, 1)
        scores.append(jnp.where(slot < lengths[path * 2 + i], s, NEG))
    s = dot_t(q, tail_keys[...])
    col = lax.broadcasted_iota(jnp.int32, s.shape, 1)
    row = lax.broadcasted_iota(jnp.int32, s.shape, 0) % rows
    causal = (col < rows) & (path * rows + col <= block * rows + row)
    recent = (col >= rows) & (col < rows + 8)
    scores.append(jnp.where(causal | recent, s, NEG))
    peak = scores[0].max(axis=-1, keepdims=True)
    for s in scores[1:]:
        peak = jnp.maximum(peak, s.max(axis=-1, keepdims=True))
    peak = (peak * SCALE2).astype(BF16).astype(F32)
    total = jnp.zeros((total_rows, 1), F32)
    mix = jnp.zeros((total_rows, HEAD), F32)
    for s, v in zip(scores, (values[0], values[1], tail_values[...])):
        w = jnp.exp2(s * SCALE2 - peak)
        total = total + jnp.sum(w, axis=-1, keepdims=True)
        mix = mix + dot(w.astype(BF16), v)
    high = total.astype(BF16).astype(F32)
    low = total - high
    lane = lax.broadcasted_iota(jnp.int32, (rows, HEAD), 1)
    stats = jnp.zeros((rows, HEAD), F32)
    for h in range(GROUP):
        at = slice(h * rows, (h + 1) * rows)
        out[:, h * HEAD : (h + 1) * HEAD] = mix[at].astype(BF16)
        for n, x in enumerate((peak, high, low)):
            stats = jnp.where(lane == n * GROUP + h, x[at], stats)
    out[:, GROUP * HEAD :] = stats.astype(BF16)


def output_kernel(own_part, part1, part2, part3, w_out, dterms, send, keep, attn):
    core = lax.axis_index("tensor") % 2
    parts = (own_part, part1, part2, part3)
    stats = [x[:, GROUP * HEAD :].astype(F32) for x in parts]
    for h in range(GROUP):
        at = slice(h * HEAD, (h + 1) * HEAD)
        peaks = [s[:, h : h + 1] for s in stats]
        peak = functools.reduce(jnp.maximum, peaks)
        mix = 0.0
        total = 0.0
        for s, p, x in zip(stats, peaks, parts):
            w = jnp.exp2(p - peak)
            total = total + w * (s[:, GROUP + h : GROUP + h + 1] + s[:, 2 * GROUP + h : 2 * GROUP + h + 1])
            mix = mix + w * x[:, at].astype(F32)
        attn[:, at] = mix / total
    width = w_out.shape[1]
    for which, ref in ((1 - core, send), (core, keep)):
        lhs = jnp.concatenate(
            [attn[pl.ds(pl.multiple_of((2 * y + which) * 8, 8), 8), :] for y in range(4)], axis=0
        ).astype(BF16)
        res = dot(lhs, w_out[...])
        for y in range(4):
            ref[y, :, :width] = res[y * 8 : (y + 1) * 8].astype(ref.dtype)
            ref[y, :, width:] = dterms[2 * y + which].astype(ref.dtype)


def fold_kernel(keep, received, own_out, out1, out2, out3):
    at = lax.axis_index("tensor") // 2
    for k, ref in enumerate((own_out, out1, out2, out3)):
        block = at ^ k
        ref[...] = (keep[block] + received[block].astype(F32)).astype(ref.dtype)


def final_kernel(own, in1, in2, in3, decode_out, summary_out):
    total = own[...] + in1[...].astype(F32) + in2[...].astype(F32) + in3[...].astype(F32)
    width = summary_out.shape[1]
    summary_out[...] = total[:, :width].astype(BF16)
    decode_out[0] = total[:STEPS, width:].astype(BF16)
    decode_out[1] = total[STEPS:, width:].astype(BF16)


def call(kernel, out_shape, args, scratch=(), limit=32, flops=0, smem=()):
    specs = [
        pl.BlockSpec(memory_space=pltpu.SMEM if i in smem else pltpu.VMEM)
        for i in range(len(args))
    ]
    nbytes = sum(math.prod(a.shape) * a.dtype.itemsize for a in args)
    outs = tuple(jax.ShapeDtypeStruct(s, d) for s, d in out_shape)
    out = pl.pallas_call(
        kernel,
        out_shape=outs,
        in_specs=specs,
        out_specs=tuple(pl.BlockSpec(memory_space=pltpu.VMEM) for _ in outs),
        scratch_shapes=list(scratch),
        compiler_params=pltpu.CompilerParams(vmem_limit_bytes=limit * MIB),
        cost_estimate=pl.CostEstimate(flops=flops, bytes_accessed=nbytes, transcendentals=0),
    )(*args)
    return out


def flip(x, axis, size, k):
    return lax.ppermute(x, axis, [(i, i ^ k) for i in range(size)])


def body(
    decode_in,
    path_embed,
    summary_in,
    norm_gain,
    query_gain,
    key_norm_gain,
    w_query,
    key_weight,
    w_value,
    w_out,
    key_cache,
    value_cache,
    lengths,
):
    width = w_out.shape[1]
    rows = 64
    norm_gain = norm_gain.reshape(1, -1)
    query_gain = query_gain.reshape(1, -1)
    key_gain = key_norm_gain.reshape(1, -1)

    across = {k: flip(summary_in, "tensor", 8, k) for k in (2, 6, 4)}
    across[0] = summary_in
    row_blocks = [None] * 8
    for k in (0, 2, 6, 4):
        row_blocks[k] = across[k]
        row_blocks[k + 1] = flip(across[k], "tensor", 8, 1)

    dterms, dkey, dvalue, cosine, sine = call(
        decode_kernel,
        [((8, 8, width // 8), BF16), ((8, HEAD), F32), ((8, HEAD), F32), ((rows, HEAD), F32), ((rows, HEAD), F32)],
        (lengths, decode_in, path_embed, norm_gain, query_gain, key_gain, w_query, key_weight,
         w_value, w_out, key_cache, value_cache),
        limit=24,
        smem=(0,),
        flops=2 * 8 * 4096 * 5000,
    )

    query, tail_keys, tail_values = call(
        project_kernel,
        [((rows, GROUP * HEAD), BF16), ((128, HEAD), BF16), ((128, HEAD), BF16)],
        (*row_blocks, norm_gain, query_gain, key_gain, w_query, key_weight, w_value, cosine, sine,
         dkey, dvalue),
        scratch=[pltpu.VMEM((rows, width), F32)],
        limit=24,
        flops=2 * 64 * 4096 * 768,
    )

    queries = [query] + [flip(query, "path", 4, k) for k in (1, 2, 3)]
    parts = []
    for k in range(4):
        (part,) = call(
            functools.partial(attend_kernel, k),
            [((rows, (GROUP + 1) * HEAD), BF16)],
            (lengths, queries[k], key_cache, value_cache, tail_keys, tail_values),
            limit=32,
            smem=(0,),
            flops=4 * 256 * 4224 * 128,
        )
        parts.append(part if k == 0 else flip(part, "path", 4, k))

    send, keep = call(
        output_kernel,
        [((4, 8, width + width // 8), BF16), ((4, 8, width + width // 8), F32)],
        (*parts, w_out, dterms),
        scratch=[pltpu.VMEM((rows, GROUP * HEAD), F32)],
        limit=24,
        flops=2 * 64 * 512 * 4096,
    )
    received = flip(send, "tensor", 8, 1)
    own, out1, out2, out3 = call(
        fold_kernel,
        [((8, width + width // 8), F32)] + [((8, width + width // 8), BF16)] * 3,
        (keep, received),
    )
    in1 = flip(out1, "tensor", 8, 2)
    in2 = flip(out2, "tensor", 8, 4)
    in3 = flip(out3, "tensor", 8, 6)
    decode_out, summary_out = call(
        final_kernel,
        [((2, STEPS, width // 8), BF16), ((8, width), BF16)],
        (own, in1, in2, in3),
    )
    return (decode_out, summary_out)


def solution(mesh):
    in_specs = (
        P(("problem", "path"), None, None),
        P("path", None),
        P(("problem", "path", "tensor"), None),
        P(),
        P(),
        P(),
        P(None, "tensor"),
        P(None, "tensor"),
        P(None, "tensor"),
        P("tensor", None),
        P(("problem", "path"), None, "tensor"),
        P(("problem", "path"), None, "tensor"),
        P("problem"),
    )
    out_specs = (P(("problem", "path"), None, "tensor"), P(("problem", "path", "tensor"), None))
    return jax.shard_map(body, mesh=mesh, in_specs=in_specs, out_specs=out_specs, check_vma=False)
```

time: 246 us -> 66.6 us (0.27)
  waiting for transfers between devices: 146 us -> 6.19 us
  matrix products: 32.1 us -> 0 us
  starting transfers between devices: 0.2 us -> 27.5 us
  other arithmetic: 22.8 us -> 0 us
  Pallas kernels: 0 us -> 18 us
  between operations: 14.1 us -> 0.84 us
  blocking collectives: 8.41 us -> 0 us
  local copies, waits for them, and re-layouts: 20.4 us -> 13.5 us
    unnamed x8 -> x0, waiting for transfers between devices: 67.1 us -> none
    all_gather x1 -> x0, waiting for transfers between devices: 45.1 us -> none  [body(): lax.all_gather(summary_in, ('path', 'tensor'), axis=0, tiled=True)]
    reduce_scatter x1 -> x0, waiting for transfers between devices: 33.6 us -> none  [body(): lax.psum_scatter(jnp.dot(sattn, w_out, preferred_element_type=jnp.float32...]
    dot_general x17 -> x0, matrix products: 32.1 us -> none  [the longest x3 8.56 us: weigh_parts(): jnp.einsum('rkgn,nkd->rkgd', weights_part.astype(jnp.bfloat16), values_pa...]
    ppermute x0 -> x17, starting transfers between devices: none -> 27.5 us  [flip(): return lax.ppermute(x, axis, [(i, i ^ k) for i in range(size)])]
    pallas_call x0 -> x9, Pallas kernels: none -> 18 us  [call(): pl.pallas_call(kernel, out_shape=outs, in_specs=specs, out_specs=tuple((p...]
    reduce_sum x8 -> x0, other arithmetic: 13 us -> none  [the longest x3 9.08 us: weigh_parts(): totals = totals + jnp.sum(weights_part, axis=-1)]
    pmax x1 -> x0, blocking collectives: 8.41 us -> none  [body(): peak_all = lax.pmax(local_peak, 'path')]
  transfers between devices with their start and end apart: 5 -> 17, of which waited for: 5 -> 4; matrix products, arithmetic and copies ran while one was open for 16% -> 1% of each run, Pallas kernels for 0% -> 21%
where the time goes in v1:
time: 66.6 us; the launch traced here: 66 us
  starting transfers between devices  27.5 us (41%)
  Pallas kernels  18 us (27%)
  local copies, waits for them, and re-layouts  13.5 us (20%)
  waiting for transfers between devices  6.19 us (9%)
  between operations  0.84 us (1%)
    ppermute x17, starting transfers between devices, flip(): return lax.ppermute(x, axis, [(i, i ^ k) for i in range(size)])  27.5 us
    pallas_call x9, Pallas kernels, call(): pl.pallas_call(kernel, out_shape=outs, in_specs=specs, out_specs=tuple((p...  18 us
    unnamed x38, local copies, waits for them, and re-layouts  12.8 us
    ppermute x17, waiting for transfers between devices, flip(): return lax.ppermute(x, axis, [(i, i ^ k) for i in range(size)])  6.19 us
  transfers between devices with their start and end apart: 17, of which 4 were waited for; matrix products, arithmetic and copies ran while one was open for 1% of the time, Pallas kernels for 21%

profile of v1, /device:TPU:1, one launch (start us, length us, event | category | flops | bytes accessed | tf_op | source)
XLA Modules:
  0.0 66.0 jit_solution(8582227367598252990)
XLA Ops:
  0.6 3.8 %collective-permute-start.3 = (bf16[8,4096]{1,0:T(8,128)(2,1)}, bf16[8,4096]{1,0:T(8,128)(2,1)S(1)}, u32[]{:S(2)}, u32[]{:S(2)}) collective-permute-start(bf16[8,4096]{1,0:T(8,128)(2,1)} %refs_0_.1), channel_id=1, source_target_pairs={{0,32},{8,40},{16,48},{24,56},{32,0},{40,8},{48,16},{56,24},{1,33}... | collective-permute-start | bytes 196616 | tf_op jit(solution)/shard_map/ppermute | solution.py:233
  5.2 2.8 %collective-permute-start = (bf16[8,4096]{1,0:T(8,128)(2,1)}, bf16[8,4096]{1,0:T(8,128)(2,1)S(1)}, u32[]{:S(2)}, u32[]{:S(2)}) collective-permute-start(bf16[8,4096]{1,0:T(8,128)(2,1)} %refs_0_.1), channel_id=1, source_target_pairs={{0,8},{8,0},{16,24},{24,16},{32,40},{40,32},{48,56},{56,48},{1,9},... | collective-permute-start | bytes 196616 | tf_op jit(solution)/shard_map/ppermute | solution.py:233
  8.1 1.9 %collective-permute-start.4 = (bf16[8,4096]{1,0:T(8,128)(2,1)S(1)}, bf16[8,4096]{1,0:T(8,128)(2,1)S(1)}, u32[]{:S(2)}, u32[]{:S(2)}) collective-permute-start(bf16[8,4096]{1,0:T(8,128)(2,1)S(1)} %collective-permute-done.3.refs_4_), channel_id=1, source_target_pairs={{0,8},{8,0},{16,24},{24,16},{32,40},{40,32},{48,56},{56,48},{1,9},... | collective-permute-start | bytes 196616 | tf_op jit(solution)/shard_map/ppermute | solution.py:233
  10.0 1.8 %collective-permute-start.6 = (bf16[8,4096]{1,0:T(8,128)(2,1)S(1)}, bf16[8,4096]{1,0:T(8,128)(2,1)S(1)}, u32[]{:S(2)}, u32[]{:S(2)}) collective-permute-start(bf16[8,4096]{1,0:T(8,128)(2,1)S(1)} %collective-permute-done.5.refs_6_), channel_id=1, source_target_pairs={{0,8},{8,0},{16,24},{24,16},{32,40},{40,32},{48,56},{56,48},{1,9},... | collective-permute-start | bytes 196616 | tf_op jit(solution)/shard_map/ppermute | solution.py:233
  13.7 1.2 %copy-done.2 = bf16[2,2048,128]{2,1,0:T(8,128)(2,1)S(1)} copy-done((bf16[2,2048,128]{2,1,0:T(8,128)(2,1)S(1)}, bf16[2,2048,128]{2,1,0:T(8,128)(2,1)}, u32[]{:S(2)}) %copy-start.2) | copy-done | bytes 1048600
  14.9 2.2 %copy-done.4 = bf16[4096,512]{1,0:T(8,128)(2,1)S(1)} copy-done((bf16[4096,512]{1,0:T(8,128)(2,1)S(1)}, bf16[4096,512]{1,0:T(8,128)(2,1)}, u32[]{:S(2)}) %copy-start.4) | copy-done | bytes 4194328
  17.1 2.2 %copy-done.6 = bf16[512,4096]{1,0:T(8,128)(2,1)S(1)} copy-done((bf16[512,4096]{1,0:T(8,128)(2,1)S(1)}, bf16[512,4096]{1,0:T(8,128)(2,1)}, u32[]{:S(2)}) %copy-start.6) | copy-done | bytes 4194328
  19.3 1.2 %copy-done.8 = bf16[4096,128]{1,0:T(8,128)(2,1)S(1)} copy-done((bf16[4096,128]{1,0:T(8,128)(2,1)S(1)}, bf16[4096,128]{1,0:T(8,128)(2,1)}, u32[]{:S(2)}) %copy-start.8) | copy-done | bytes 1048600
  20.5 1.2 %copy-done.10 = bf16[4096,128]{1,0:T(8,128)(2,1)S(1)} copy-done((bf16[4096,128]{1,0:T(8,128)(2,1)S(1)}, bf16[4096,128]{1,0:T(8,128)(2,1)}, u32[]{:S(2)}) %copy-start.10) | copy-done | bytes 1048600
  25.3 3.1 %shard_map.140 = (bf16[8,8,512]{2,1,0:T(8,128)(2,1)S(1)}, f32[8,128]{1,0:T(8,128)S(1)}, f32[8,128]{1,0:T(8,128)S(1)}, f32[64,128]{1,0:T(8,128)S(1)}, f32[64,128]{1,0:T(8,128)S(1)}) custom-call(s32[8]{0:T(128)S(1)} %copy-done.15, bf16[2,4,4096]{2,1,0:T(4,128)(2,1)S(1)} %copy-done.12, bf16[2,4096]{1,0:T(2,128)(2,1)S(1)} %copy-done.14, ...), custom_call_target="tpu_custom_call" | custom-call | flops 327680000 | bytes 12673568 | tf_op jit(solution)/shard_map/pallas_call | solution.py:220
  28.5 1.5 %shard_map.141 = (bf16[64,512]{1,0:T(8,128)(2,1)S(1)}, bf16[128,128]{1,0:T(8,128)(2,1)S(1)}, bf16[128,128]{1,0:T(8,128)(2,1)S(1)}) custom-call(bf16[8,4096]{1,0:T(8,128)(2,1)S(1)} %copy-done.13, bf16[8,4096]{1,0:T(8,128)(2,1)S(1)} %collective-permute-done.refs_1_, bf16[8,4096]{1,0:T(8,128)(2,1)S(1)} %collective-permute-done.1.refs_2_, ...), custom_call_target="tpu_custom_call" | custom-call | flops 402653184 | bytes 6898176 | tf_op jit(solution)/shard_map/pallas_call | solution.py:220
  30.0 1.7 %collective-permute-start.7 = (bf16[64,512]{1,0:T(8,128)(2,1)S(1)}, bf16[64,512]{1,0:T(8,128)(2,1)S(1)}, u32[]{:S(2)}, u32[]{:S(2)}) collective-permute-start(bf16[64,512]{1,0:T(8,128)(2,1)S(1)} %get-tuple-element.20.query), channel_id=1, source_target_pairs={{0,64},{64,0},{128,192},{192,128},{1,65},{65,1},{129,193},{193,129... | collective-permute-start | bytes 196616 | tf_op jit(solution)/shard_map/ppermute | solution.py:233
  31.7 3.0 %collective-permute-start.9 = (bf16[64,512]{1,0:T(8,128)(2,1)S(1)}, bf16[64,512]{1,0:T(8,128)(2,1)S(1)}, u32[]{:S(2)}, u32[]{:S(2)}) collective-permute-start(bf16[64,512]{1,0:T(8,128)(2,1)S(1)} %get-tuple-element.20.query), channel_id=1, source_target_pairs={{0,128},{64,192},{128,0},{192,64},{1,129},{65,193},{129,1},{193,65... | collective-permute-start | bytes 196616 | tf_op jit(solution)/shard_map/ppermute | solution.py:233
  34.7 2.7 %shard_map.143 = bf16[64,640]{1,0:T(8,128)(2,1)S(1)} custom-call(s32[8]{0:T(128)S(1)} %copy-done.16, bf16[64,512]{1,0:T(8,128)(2,1)S(1)} %collective-permute-done.7.query, bf16[2,2048,128]{2,1,0:T(8,128)(2,1)S(1)} %copy-done.1, bf16[2,2048,128]{2,1,0:T(8,128)(2,1)S(1)} %copy-done.3, bf16[128,128]{1,0:T(8,128)(2,1)S(1)} %get-tuple-element.21.tail_keys, ...), custom_call_target="tpu_custom_call" | custom-call | flops 553648128 | bytes 2228256 | tf_op jit(solution)/shard_map/pallas_call | solution.py:220
  38.4 2.7 %shard_map.144 = bf16[64,640]{1,0:T(8,128)(2,1)S(1)} custom-call(s32[8]{0:T(128)S(1)} %copy-done.16, bf16[64,512]{1,0:T(8,128)(2,1)S(1)} %collective-permute-done.9.query, bf16[2,2048,128]{2,1,0:T(8,128)(2,1)S(1)} %copy-done.1, bf16[2,2048,128]{2,1,0:T(8,128)(2,1)S(1)} %copy-done.3, bf16[128,128]{1,0:T(8,128)(2,1)S(1)} %get-tuple-element.21.tail_keys, ...), custom_call_target="tpu_custom_call" | custom-call | flops 553648128 | bytes 2228256 | tf_op jit(solution)/shard_map/pallas_call | solution.py:220
  41.2 3.1 %collective-permute-start.10 = (bf16[64,640]{1,0:T(8,128)(2,1)S(1)}, bf16[64,640]{1,0:T(8,128)(2,1)S(1)}, u32[]{:S(2)}, u32[]{:S(2)}) collective-permute-start(bf16[64,640]{1,0:T(8,128)(2,1)S(1)} %shard_map.144), channel_id=1, source_target_pairs={{0,128},{64,192},{128,0},{192,64},{1,129},{65,193},{129,1},{193,65... | collective-permute-start | bytes 245768 | tf_op jit(solution)/shard_map/ppermute | solution.py:233
  44.2 2.7 %shard_map.145 = bf16[64,640]{1,0:T(8,128)(2,1)S(1)} custom-call(s32[8]{0:T(128)S(1)} %copy-done.16, bf16[64,512]{1,0:T(8,128)(2,1)S(1)} %collective-permute-done.11.query, bf16[2,2048,128]{2,1,0:T(8,128)(2,1)S(1)} %copy-done.1, bf16[2,2048,128]{2,1,0:T(8,128)(2,1)S(1)} %copy-done.3, bf16[128,128]{1,0:T(8,128)(2,1)S(1)} %get-tuple-element.21.tail_keys, ...), custom_call_target="tpu_custom_call" | custom-call | flops 553648128 | bytes 2228256 | tf_op jit(solution)/shard_map/pallas_call | solution.py:220
  47.1 2.7 %shard_map.142.own_part = bf16[64,640]{1,0:T(8,128)(2,1)S(1)} custom-call(s32[8]{0:T(128)S(1)} %copy-done.16, bf16[64,512]{1,0:T(8,128)(2,1)S(1)} %get-tuple-element.20.query, bf16[2,2048,128]{2,1,0:T(8,128)(2,1)S(1)} %copy-done.1, bf16[2,2048,128]{2,1,0:T(8,128)(2,1)S(1)} %copy-done.3, bf16[128,128]{1,0:T(8,128)(2,1)S(1)} %get-tuple-element.21.tail_keys, ...), custom_call_target="tpu_custom_call" | custom-call | flops 553648128 | bytes 2228256 | tf_op jit(solution)/shard_map/pallas_call | solution.py:220
  49.8 2.3 %collective-permute-done.12.part3 = bf16[64,640]{1,0:T(8,128)(2,1)S(1)} collective-permute-done((bf16[64,640]{1,0:T(8,128)(2,1)S(1)}, bf16[64,640]{1,0:T(8,128)(2,1)S(1)}, u32[]{:S(2)}, u32[]{:S(2)}) %collective-permute-start.12) | collective-permute-done | bytes 81952 | tf_op jit(solution)/shard_map/ppermute | solution.py:233
  52.2 1.8 %shard_map.146 = (bf16[4,8,4608]{2,1,0:T(8,128)(2,1)S(1)}, f32[4,8,4608]{2,1,0:T(8,128)S(1)}) custom-call(bf16[64,640]{1,0:T(8,128)(2,1)S(1)} %shard_map.142.own_part, bf16[64,640]{1,0:T(8,128)(2,1)S(1)} %collective-permute-done.8.part1, bf16[64,640]{1,0:T(8,128)(2,1)S(1)} %collective-permute-done.10.part2, ...), custom_call_target="tpu_custom_call" | custom-call | flops 268435456 | bytes 4587520 | tf_op jit(solution)/shard_map/pallas_call | solution.py:220
  54.0 3.6 %collective-permute-start.13 = (bf16[4,8,4608]{2,1,0:T(8,128)(2,1)S(1)}, bf16[4,8,4608]{2,1,0:T(8,128)(2,1)S(1)}, u32[]{:S(2)}, u32[]{:S(2)}) collective-permute-start(bf16[4,8,4608]{2,1,0:T(8,128)(2,1)S(1)} %get-tuple-element.25), channel_id=1, source_target_pairs={{0,8},{8,0},{16,24},{24,16},{32,40},{40,32},{48,56},{56,48},{1,9},... | collective-permute-start | bytes 884744 | tf_op jit(solution)/shard_map/ppermute | solution.py:233
  58.9 1.5 %collective-permute-start.15 = (bf16[8,4608]{1,0:T(8,128)(2,1)S(1)}, bf16[8,4608]{1,0:T(8,128)(2,1)S(1)}, u32[]{:S(2)}, u32[]{:S(2)}) collective-permute-start(bf16[8,4608]{1,0:T(8,128)(2,1)S(1)} %get-tuple-element.28), channel_id=1, source_target_pairs={{0,32},{8,40},{16,48},{24,56},{32,0},{40,8},{48,16},{56,24},{1,33}... | collective-permute-start | bytes 221192 | tf_op jit(solution)/shard_map/ppermute | solution.py:233
  60.4 2.4 %collective-permute-start.16 = (bf16[8,4608]{1,0:T(8,128)(2,1)S(1)}, bf16[8,4608]{1,0:T(8,128)(2,1)S(1)}, u32[]{:S(2)}, u32[]{:S(2)}) collective-permute-start(bf16[8,4608]{1,0:T(8,128)(2,1)S(1)} %get-tuple-element.29), channel_id=1, source_target_pairs={{0,48},{8,56},{16,32},{24,40},{32,16},{40,24},{48,0},{56,8},{1,49}... | collective-permute-start | bytes 221192 | tf_op jit(solution)/shard_map/ppermute | solution.py:233
  63.8 1.6 %collective-permute-done.16.in3 = bf16[8,4608]{1,0:T(8,128)(2,1)S(1)} collective-permute-done((bf16[8,4608]{1,0:T(8,128)(2,1)S(1)}, bf16[8,4608]{1,0:T(8,128)(2,1)S(1)}, u32[]{:S(2)}, u32[]{:S(2)}) %collective-permute-start.16) | collective-permute-done | bytes 73760 | tf_op jit(solution)/shard_map/ppermute | solution.py:233
  (58 shorter events, 10.4 us)
Async XLA Ops:
  0.6 7.4 %collective-permute-start.3 = (bf16[8,4096]{1,0:T(8,128)(2,1)}, bf16[8,4096]{1,0:T(8,128)(2,1)S(1)}, u32[]{:S(2)}, u32[]{:S(2)}) collective-permute-start(bf16[8,4096]{1,0:T(8,128)(2,1)} %refs_0_.1), channel_id=1, source_target_pairs={{0,32},{8,40},{16,48},{24,56},{32,0},{40,8},{48,16},{56,24},{1,33}... | collective-permute-start | bytes 196616 | tf_op jit(solution)/shard_map/ppermute | solution.py:233
  4.5 5.5 %collective-permute-start.1 = (bf16[8,4096]{1,0:T(8,128)(2,1)}, bf16[8,4096]{1,0:T(8,128)(2,1)S(1)}, u32[]{:S(2)}, u32[]{:S(2)}) collective-permute-start(bf16[8,4096]{1,0:T(8,128)(2,1)} %refs_0_.1), channel_id=1, source_target_pairs={{0,16},{8,24},{16,0},{24,8},{32,48},{40,56},{48,32},{56,40},{1,17}... | collective-permute-start | bytes 196616 | tf_op jit(solution)/shard_map/ppermute | solution.py:233
  4.9 5.2 %collective-permute-start.5 = (bf16[8,4096]{1,0:T(8,128)(2,1)}, bf16[8,4096]{1,0:T(8,128)(2,1)S(1)}, u32[]{:S(2)}, u32[]{:S(2)}) collective-permute-start(bf16[8,4096]{1,0:T(8,128)(2,1)} %refs_0_.1), channel_id=1, source_target_pairs={{0,48},{8,56},{16,32},{24,40},{32,16},{40,24},{48,0},{56,8},{1,49}... | collective-permute-start | bytes 196616 | tf_op jit(solution)/shard_map/ppermute | solution.py:233
  5.2 23.2 %collective-permute-start = (bf16[8,4096]{1,0:T(8,128)(2,1)}, bf16[8,4096]{1,0:T(8,128)(2,1)S(1)}, u32[]{:S(2)}, u32[]{:S(2)}) collective-permute-start(bf16[8,4096]{1,0:T(8,128)(2,1)} %refs_0_.1), channel_id=1, source_target_pairs={{0,8},{8,0},{16,24},{24,16},{32,40},{40,32},{48,56},{56,48},{1,9},... | collective-permute-start | bytes 196616 | tf_op jit(solution)/shard_map/ppermute | solution.py:233
  8.1 20.4 %collective-permute-start.4 = (bf16[8,4096]{1,0:T(8,128)(2,1)S(1)}, bf16[8,4096]{1,0:T(8,128)(2,1)S(1)}, u32[]{:S(2)}, u32[]{:S(2)}) collective-permute-start(bf16[8,4096]{1,0:T(8,128)(2,1)S(1)} %collective-permute-done.3.refs_4_), channel_id=1, source_target_pairs={{0,8},{8,0},{16,24},{24,16},{32,40},{40,32},{48,56},{56,48},{1,9},... | collective-permute-start | bytes 196616 | tf_op jit(solution)/shard_map/ppermute | solution.py:233
  10.0 18.4 %collective-permute-start.2 = (bf16[8,4096]{1,0:T(8,128)(2,1)S(1)}, bf16[8,4096]{1,0:T(8,128)(2,1)S(1)}, u32[]{:S(2)}, u32[]{:S(2)}) collective-permute-start(bf16[8,4096]{1,0:T(8,128)(2,1)S(1)} %collective-permute-done.1.refs_2_), channel_id=1, source_target_pairs={{0,8},{8,0},{16,24},{24,16},{32,40},{40,32},{48,56},{56,48},{1,9},... | collective-permute-start | bytes 196616 | tf_op jit(solution)/shard_map/ppermute | solution.py:233
  10.0 18.4 %collective-permute-start.6 = (bf16[8,4096]{1,0:T(8,128)(2,1)S(1)}, bf16[8,4096]{1,0:T(8,128)(2,1)S(1)}, u32[]{:S(2)}, u32[]{:S(2)}) collective-permute-start(bf16[8,4096]{1,0:T(8,128)(2,1)S(1)} %collective-permute-done.5.refs_6_), channel_id=1, source_target_pairs={{0,8},{8,0},{16,24},{24,16},{32,40},{40,32},{48,56},{56,48},{1,9},... | collective-permute-start | bytes 196616 | tf_op jit(solution)/shard_map/ppermute | solution.py:233
  25.3 3.2 %copy-start.9 = (bf16[4096,128]{1,0:T(8,128)(2,1)S(1)}, bf16[4096,128]{1,0:T(8,128)(2,1)}, u32[]{:S(2)}) copy-start(bf16[4096,128]{1,0:T(8,128)(2,1)} %refs_12_.1) | copy-start | bytes 3145732
  25.3 3.2 %copy-start.11 = (bf16[4096,128]{1,0:T(8,128)(2,1)S(1)}, bf16[4096,128]{1,0:T(8,128)(2,1)}, u32[]{:S(2)}) copy-start(bf16[4096,128]{1,0:T(8,128)(2,1)} %refs_13_.1) | copy-start | bytes 3145732
  25.3 3.2 %copy-start.13 = (bf16[8,4096]{1,0:T(8,128)(2,1)S(1)}, bf16[8,4096]{1,0:T(8,128)(2,1)}, u32[]{:S(2)}) copy-start(bf16[8,4096]{1,0:T(8,128)(2,1)} %refs_0_.1) | copy-start | bytes 196612
  28.4 6.3 %copy-start.1 = (bf16[2,2048,128]{2,1,0:T(8,128)(2,1)S(1)}, bf16[2,2048,128]{2,1,0:T(8,128)(2,1)}, u32[]{:S(2)}) copy-start(bf16[2,2048,128]{2,1,0:T(8,128)(2,1)} %keys.9) | copy-start | bytes 3145732
  28.4 6.3 %copy-start.3 = (bf16[2,2048,128]{2,1,0:T(8,128)(2,1)S(1)}, bf16[2,2048,128]{2,1,0:T(8,128)(2,1)}, u32[]{:S(2)}) copy-start(bf16[2,2048,128]{2,1,0:T(8,128)(2,1)} %values.9) | copy-start | bytes 3145732
  28.4 6.3 %copy-start.16 = (s32[8]{0:T(128)S(1)}, s32[8]{0:T(128)}, u32[]{:S(2)}) copy-start(s32[8]{0:T(128)} %lengths.9) | copy-start | bytes 100
  30.0 4.7 %collective-permute-start.7 = (bf16[64,512]{1,0:T(8,128)(2,1)S(1)}, bf16[64,512]{1,0:T(8,128)(2,1)S(1)}, u32[]{:S(2)}, u32[]{:S(2)}) collective-permute-start(bf16[64,512]{1,0:T(8,128)(2,1)S(1)} %get-tuple-element.20.query), channel_id=1, source_target_pairs={{0,64},{64,0},{128,192},{192,128},{1,65},{65,1},{129,193},{193,129... | collective-permute-start | bytes 196616 | tf_op jit(solution)/shard_map/ppermute | solution.py:233
  31.7 6.7 %collective-permute-start.9 = (bf16[64,512]{1,0:T(8,128)(2,1)S(1)}, bf16[64,512]{1,0:T(8,128)(2,1)S(1)}, u32[]{:S(2)}, u32[]{:S(2)}) collective-permute-start(bf16[64,512]{1,0:T(8,128)(2,1)S(1)} %get-tuple-element.20.query), channel_id=1, source_target_pairs={{0,128},{64,192},{128,0},{192,64},{1,129},{65,193},{129,1},{193,65... | collective-permute-start | bytes 196616 | tf_op jit(solution)/shard_map/ppermute | solution.py:233
  34.7 9.6 %collective-permute-start.11 = (bf16[64,512]{1,0:T(8,128)(2,1)S(1)}, bf16[64,512]{1,0:T(8,128)(2,1)S(1)}, u32[]{:S(2)}, u32[]{:S(2)}) collective-permute-start(bf16[64,512]{1,0:T(8,128)(2,1)S(1)} %get-tuple-element.20.query), channel_id=1, source_target_pairs={{0,192},{64,128},{128,64},{192,0},{1,193},{65,129},{129,65},{193,1... | collective-permute-start | bytes 196616 | tf_op jit(solution)/shard_map/ppermute | solution.py:233
  34.7 17.4 %copy-start.7 = (bf16[512,4096]{1,0:T(8,128)(2,1)S(1)}, bf16[512,4096]{1,0:T(8,128)(2,1)}, u32[]{:S(2)}) copy-start(bf16[512,4096]{1,0:T(8,128)(2,1)} %w_out.3) | copy-start | bytes 12582916
  37.4 12.3 %collective-permute-start.8 = (bf16[64,640]{1,0:T(8,128)(2,1)S(1)}, bf16[64,640]{1,0:T(8,128)(2,1)S(1)}, u32[]{:S(2)}, u32[]{:S(2)}) collective-permute-start(bf16[64,640]{1,0:T(8,128)(2,1)S(1)} %shard_map.143), channel_id=1, source_target_pairs={{0,64},{64,0},{128,192},{192,128},{1,65},{65,1},{129,193},{193,129... | collective-permute-start | bytes 245768 | tf_op jit(solution)/shard_map/ppermute | solution.py:233
  41.2 8.6 %collective-permute-start.10 = (bf16[64,640]{1,0:T(8,128)(2,1)S(1)}, bf16[64,640]{1,0:T(8,128)(2,1)S(1)}, u32[]{:S(2)}, u32[]{:S(2)}) collective-permute-start(bf16[64,640]{1,0:T(8,128)(2,1)S(1)} %shard_map.144), channel_id=1, source_target_pairs={{0,128},{64,192},{128,0},{192,64},{1,129},{65,193},{129,1},{193,65... | collective-permute-start | bytes 245768 | tf_op jit(solution)/shard_map/ppermute | solution.py:233
  47.0 5.2 %collective-permute-start.12 = (bf16[64,640]{1,0:T(8,128)(2,1)S(1)}, bf16[64,640]{1,0:T(8,128)(2,1)S(1)}, u32[]{:S(2)}, u32[]{:S(2)}) collective-permute-start(bf16[64,640]{1,0:T(8,128)(2,1)S(1)} %shard_map.145), channel_id=1, source_target_pairs={{0,192},{64,128},{128,64},{192,0},{1,193},{65,129},{129,65},{193,1... | collective-permute-start | bytes 245768 | tf_op jit(solution)/shard_map/ppermute | solution.py:233
  54.0 4.8 %collective-permute-start.13 = (bf16[4,8,4608]{2,1,0:T(8,128)(2,1)S(1)}, bf16[4,8,4608]{2,1,0:T(8,128)(2,1)S(1)}, u32[]{:S(2)}, u32[]{:S(2)}) collective-permute-start(bf16[4,8,4608]{2,1,0:T(8,128)(2,1)S(1)} %get-tuple-element.25), channel_id=1, source_target_pairs={{0,8},{8,0},{16,24},{24,16},{32,40},{40,32},{48,56},{56,48},{1,9},... | collective-permute-start | bytes 884744 | tf_op jit(solution)/shard_map/ppermute | solution.py:233
  58.8 3.9 %collective-permute-start.14 = (bf16[8,4608]{1,0:T(8,128)(2,1)S(1)}, bf16[8,4608]{1,0:T(8,128)(2,1)S(1)}, u32[]{:S(2)}, u32[]{:S(2)}) collective-permute-start(bf16[8,4608]{1,0:T(8,128)(2,1)S(1)} %get-tuple-element.27), channel_id=1, source_target_pairs={{0,16},{8,24},{16,0},{24,8},{32,48},{40,56},{48,32},{56,40},{1,17}... | collective-permute-start | bytes 221192 | tf_op jit(solution)/shard_map/ppermute | solution.py:233
  58.9 4.8 %collective-permute-start.15 = (bf16[8,4608]{1,0:T(8,128)(2,1)S(1)}, bf16[8,4608]{1,0:T(8,128)(2,1)S(1)}, u32[]{:S(2)}, u32[]{:S(2)}) collective-permute-start(bf16[8,4608]{1,0:T(8,128)(2,1)S(1)} %get-tuple-element.28), channel_id=1, source_target_pairs={{0,32},{8,40},{16,48},{24,56},{32,0},{40,8},{48,16},{56,24},{1,33}... | collective-permute-start | bytes 221192 | tf_op jit(solution)/shard_map/ppermute | solution.py:233
  60.4 5.0 %collective-permute-start.16 = (bf16[8,4608]{1,0:T(8,128)(2,1)S(1)}, bf16[8,4608]{1,0:T(8,128)(2,1)S(1)}, u32[]{:S(2)}, u32[]{:S(2)}) collective-permute-start(bf16[8,4608]{1,0:T(8,128)(2,1)S(1)} %get-tuple-element.29), channel_id=1, source_target_pairs={{0,48},{8,56},{16,32},{24,40},{32,16},{40,24},{48,0},{56,8},{1,49}... | collective-permute-start | bytes 221192 | tf_op jit(solution)/shard_map/ppermute | solution.py:233
  (12 other events, 16.0 us)

commit v2 on v1

--- a/solution.py
+++ b/solution.py
@@ -59,6 +59,11 @@
     row = lax.broadcasted_iota(jnp.int32, (8, HEAD), 0)
     position = jnp.where(row < STEPS, len0 + row, len1 + row - STEPS).astype(F32)
     cosine, sine = rope_tables(position)
+    rows = cos_out.shape[0]
+    row = lax.broadcasted_iota(jnp.int32, (rows, HEAD), 0)
+    cos_all, sin_all = rope_tables((keys.shape[1] + path * rows + row).astype(F32))
+    cos_out[...] = cos_all
+    sin_out[...] = sin_all
     query = dot(normed, w_query[...])
     qgain = query_gain[...].astype(F32)
     heads = [
@@ -95,24 +100,28 @@
     width = dterms.shape[2]
     for t in range(dterms.shape[0]):
         dterms[t] = dot(attn, w_out[:, t * width : (t + 1) * width]).astype(BF16)
-    rows = cos_out.shape[0]
-    row = lax.broadcasted_iota(jnp.int32, (rows, HEAD), 0)
-    cosine, sine = rope_tables((keys.shape[1] + path * rows + row).astype(F32))
-    cos_out[...] = cosine
-    sin_out[...] = sine
-
-
-def project_kernel(*refs):
-    rows_in = refs[:8]
-    (
-        norm_gain, query_gain, key_gain, w_query, w_key, w_value, cosine, sine, dkey, dvalue,
-        query_out, tail_keys, tail_values, normed_f32,
-    ) = refs[8:]
+
+
+def hold_kernel(rows, out):
+    out[...] = rows[...]
+
+
+def norm_kernel(rows0, rows1, rows2, rows3, gain, dkey, dvalue, out, tail_key, tail_value):
+    for k, ref in enumerate((rows0, rows1, rows2, rows3)):
+        out[k] = rms(ref[...].astype(F32), gain[...].astype(F32)).astype(BF16)
+    tail_key[...] = dkey[...]
+    tail_value[...] = dvalue[...]
+
+
+def project_kernel(
+    mine, other, query_gain, key_gain, w_query, w_key, w_value, cosine, sine, dkey, dvalue,
+    query_out, tail_keys, tail_values, normed_f32,
+):
     own = lax.axis_index("tensor")
-    gain = norm_gain[...].astype(F32)
-    for j in range(8):
-        at = pl.multiple_of((own ^ j) * 8, 8)
-        normed_f32[pl.ds(at, 8), :] = rms(rows_in[j][...].astype(F32), gain)
+    for k in range(4):
+        for flipped, ref in ((0, mine), (1, other)):
+            at = pl.multiple_of((own ^ (2 * k + flipped)) * 8, 8)
+            normed_f32[pl.ds(at, 8), :] = ref[k].astype(F32)
     normed = normed_f32[...].astype(BF16)
     cos = cosine[...]
     sin = sine[...]
@@ -210,12 +219,15 @@
     decode_out[1] = total[STEPS:, width:].astype(BF16)
 
 
-def call(kernel, out_shape, args, scratch=(), limit=32, flops=0, smem=()):
+def call(kernel, out_shape, args, scratch=(), limit=32, flops=0, smem=(), far=(), nbytes=None):
     specs = [
-        pl.BlockSpec(memory_space=pltpu.SMEM if i in smem else pltpu.VMEM)
+        pl.BlockSpec(
+            memory_space=pltpu.SMEM if i in smem else pltpu.HBM if i in far else pltpu.VMEM
+        )
         for i in range(len(args))
     ]
-    nbytes = sum(math.prod(a.shape) * a.dtype.itemsize for a in args)
+    if nbytes is None:
+        nbytes = sum(math.prod(a.shape) * a.dtype.itemsize for a in args)
     outs = tuple(jax.ShapeDtypeStruct(s, d) for s, d in out_shape)
     out = pl.pallas_call(
         kernel,
@@ -254,12 +266,8 @@
     query_gain = query_gain.reshape(1, -1)
     key_gain = key_norm_gain.reshape(1, -1)
 
-    across = {k: flip(summary_in, "tensor", 8, k) for k in (2, 6, 4)}
-    across[0] = summary_in
-    row_blocks = [None] * 8
-    for k in (0, 2, 6, 4):
-        row_blocks[k] = across[k]
-        row_blocks[k + 1] = flip(across[k], "tensor", 8, 1)
+    (own_rows,) = call(hold_kernel, [(summary_in.shape, BF16)], (summary_in,), flops=10**10)
+    across = [own_rows] + [flip(own_rows, "tensor", 8, k) for k in (2, 4, 6)]
 
     dterms, dkey, dvalue, cosine, sine = call(
         decode_kernel,
@@ -268,13 +276,19 @@
          w_value, w_out, key_cache, value_cache),
         limit=24,
         smem=(0,),
-        flops=2 * 8 * 4096 * 5000,
-    )
-
+        flops=6 * 10**9,
+    )
+
+    mine, dkey, dvalue = call(
+        norm_kernel,
+        [((4, 8, width), BF16), ((8, HEAD), F32), ((8, HEAD), F32)],
+        (*across, norm_gain, dkey, dvalue),
+    )
+    other = flip(mine, "tensor", 8, 1)
     query, tail_keys, tail_values = call(
         project_kernel,
         [((rows, GROUP * HEAD), BF16), ((128, HEAD), BF16), ((128, HEAD), BF16)],
-        (*row_blocks, norm_gain, query_gain, key_gain, w_query, key_weight, w_value, cosine, sine,
+        (mine, other, query_gain, key_gain, w_query, key_weight, w_value, cosine, sine,
          dkey, dvalue),
         scratch=[pltpu.VMEM((rows, width), F32)],
         limit=24,

time: 66.6 us -> 51.9 us (0.78)
  local copies, waits for them, and re-layouts: 13.5 us -> 1.04 us
  starting transfers between devices: 27.5 us -> 22.8 us
  waiting for transfers between devices: 6.19 us -> 9.05 us
    unnamed x38 -> x26, local copies, waits for them, and re-layouts: 12.8 us -> 1.03 us
    ppermute x17 -> x14, starting transfers between devices: 27.5 us -> 22.8 us  [flip(): return lax.ppermute(x, axis, [(i, i ^ k) for i in range(size)])]
    ppermute x17 -> x14, waiting for transfers between devices: 6.19 us -> 9.05 us  [flip(): return lax.ppermute(x, axis, [(i, i ^ k) for i in range(size)])]
    reshape x1, local copies, waits for them, and re-layouts: 0.71 us -> 0.01 us  [body(): norm_gain = norm_gain.reshape(1, -1)]
    pallas_call x9 -> x11, Pallas kernels: 18 us -> 18 us  [call(): pl.pallas_call(kernel, out_shape=outs, in_specs=specs, out_specs=tuple((p...]
  transfers between devices with their start and end apart: 17 -> 14, of which waited for: 4 -> 6; matrix products, arithmetic and copies ran while one was open for 1% -> 0% of each run, Pallas kernels for 21% -> 27%
where the time goes in v2:
time: 51.9 us; the launch traced here: 51.7 us
  starting transfers between devices  22.8 us (44%)
  Pallas kernels  18 us (35%)
  waiting for transfers between devices  9.05 us (17%)
  local copies, waits for them, and re-layouts  1.04 us (2%)
  between operations  0.89 us (2%)
    ppermute x14, starting transfers between devices, flip(): return lax.ppermute(x, axis, [(i, i ^ k) for i in range(size)])  22.8 us
    pallas_call x11, Pallas kernels, call(): pl.pallas_call(kernel, out_shape=outs, in_specs=specs, out_specs=tuple((p...  18 us
    ppermute x14, waiting for transfers between devices, flip(): return lax.ppermute(x, axis, [(i, i ^ k) for i in range(size)])  9.05 us
  transfers between devices with their start and end apart: 14, of which 6 were waited for; matrix products, arithmetic and copies ran while one was open for 0% of the time, Pallas kernels for 27%

profile of v2, /device:TPU:1, one launch (start us, length us, event | category | flops | bytes accessed | tf_op | source)
XLA Modules:
  0.0 51.7 jit_solution(12609496146510534049)
XLA Ops:
  0.7 1.0 %copy-done.9 = bf16[8,4096]{1,0:T(8,128)(2,1)S(1)} copy-done((bf16[8,4096]{1,0:T(8,128)(2,1)S(1)}, bf16[8,4096]{1,0:T(8,128)(2,1)}, u32[]{:S(2)}) %copy-start.9) | copy-done | bytes 65560
  1.7 3.7 %collective-permute-start.2 = (bf16[8,4096]{1,0:T(8,128)(2,1)S(1)}, bf16[8,4096]{1,0:T(8,128)(2,1)S(1)}, u32[]{:S(2)}, u32[]{:S(2)}) collective-permute-start(bf16[8,4096]{1,0:T(8,128)(2,1)S(1)} %shard_map.140.rows0), channel_id=1, source_target_pairs={{0,48},{8,56},{16,32},{24,40},{32,16},{40,24},{48,0},{56,8},{1,49}... | collective-permute-start | bytes 196616 | tf_op jit(solution)/shard_map/ppermute | solution.py:245
  6.2 3.1 %shard_map.141 = (bf16[8,8,512]{2,1,0:T(8,128)(2,1)S(1)}, f32[8,128]{1,0:T(8,128)S(1)}, f32[8,128]{1,0:T(8,128)S(1)}, f32[64,128]{1,0:T(8,128)S(1)}, f32[64,128]{1,0:T(8,128)S(1)}) custom-call(s32[8]{0:T(128)S(1)} %copy-done.6, bf16[2,4,4096]{2,1,0:T(4,128)(2,1)S(1)} %copy-done.10, bf16[2,4096]{1,0:T(2,128)(2,1)S(1)} %copy-done.11, ...), custom_call_target="tpu_custom_call" | custom-call | flops 6000000000 | bytes 12673568 | tf_op jit(solution)/shard_map/pallas_call | solution.py:232
  9.3 0.8 %collective-permute-done.1.rows2 = bf16[8,4096]{1,0:T(8,128)(2,1)S(1)} collective-permute-done((bf16[8,4096]{1,0:T(8,128)(2,1)S(1)}, bf16[8,4096]{1,0:T(8,128)(2,1)S(1)}, u32[]{:S(2)}, u32[]{:S(2)}) %collective-permute-start.1) | collective-permute-done | bytes 65568 | tf_op jit(solution)/shard_map/ppermute | solution.py:245
  10.3 2.4 %collective-permute-start.3 = (bf16[4,8,4096]{2,1,0:T(8,128)(2,1)S(1)}, bf16[4,8,4096]{2,1,0:T(8,128)(2,1)S(1)}, u32[]{:S(2)}, u32[]{:S(2)}) collective-permute-start(bf16[4,8,4096]{2,1,0:T(8,128)(2,1)S(1)} %get-tuple-element.21.mine), channel_id=1, source_target_pairs={{0,8},{8,0},{16,24},{24,16},{32,40},{40,32},{48,56},{56,48},{1,9},... | collective-permute-start | bytes 786440 | tf_op jit(solution)/shard_map/ppermute | solution.py:245
  12.7 1.2 %collective-permute-done.3.other = bf16[4,8,4096]{2,1,0:T(8,128)(2,1)S(1)} collective-permute-done((bf16[4,8,4096]{2,1,0:T(8,128)(2,1)S(1)}, bf16[4,8,4096]{2,1,0:T(8,128)(2,1)S(1)}, u32[]{:S(2)}, u32[]{:S(2)}) %collective-permute-start.3) | collective-permute-done | bytes 262176 | tf_op jit(solution)/shard_map/ppermute | solution.py:245
  13.9 1.3 %shard_map.143 = (bf16[64,512]{1,0:T(8,128)(2,1)S(1)}, bf16[128,128]{1,0:T(8,128)(2,1)S(1)}, bf16[128,128]{1,0:T(8,128)(2,1)S(1)}) custom-call(bf16[4,8,4096]{2,1,0:T(8,128)(2,1)S(1)} %get-tuple-element.21.mine, bf16[4,8,4096]{2,1,0:T(8,128)(2,1)S(1)} %collective-permute-done.3.other, bf16[1,128]{1,0:T(2,128)(2,1)S(1)} %bitcast.3, ...), custom_call_target="tpu_custom_call" | custom-call | flops 402653184 | bytes 6889984 | tf_op jit(solution)/shard_map/pallas_call | solution.py:232
  15.1 1.4 %collective-permute-start.4 = (bf16[64,512]{1,0:T(8,128)(2,1)S(1)}, bf16[64,512]{1,0:T(8,128)(2,1)S(1)}, u32[]{:S(2)}, u32[]{:S(2)}) collective-permute-start(bf16[64,512]{1,0:T(8,128)(2,1)S(1)} %get-tuple-element.26.query), channel_id=1, source_target_pairs={{0,64},{64,0},{128,192},{192,128},{1,65},{65,1},{129,193},{193,129... | collective-permute-start | bytes 196616 | tf_op jit(solution)/shard_map/ppermute | solution.py:245
  16.6 3.0 %collective-permute-start.6 = (bf16[64,512]{1,0:T(8,128)(2,1)S(1)}, bf16[64,512]{1,0:T(8,128)(2,1)S(1)}, u32[]{:S(2)}, u32[]{:S(2)}) collective-permute-start(bf16[64,512]{1,0:T(8,128)(2,1)S(1)} %get-tuple-element.26.query), channel_id=1, source_target_pairs={{0,128},{64,192},{128,0},{192,64},{1,129},{65,193},{129,1},{193,65... | collective-permute-start | bytes 196616 | tf_op jit(solution)/shard_map/ppermute | solution.py:245
  19.6 2.7 %shard_map.145 = bf16[64,640]{1,0:T(8,128)(2,1)S(1)} custom-call(s32[8]{0:T(128)S(1)} %copy-done.6, bf16[64,512]{1,0:T(8,128)(2,1)S(1)} %collective-permute-done.4.query, bf16[2,2048,128]{2,1,0:T(8,128)(2,1)S(1)} %copy-done, bf16[2,2048,128]{2,1,0:T(8,128)(2,1)S(1)} %copy-done.1, bf16[128,128]{1,0:T(8,128)(2,1)S(1)} %get-tuple-element.27.tail_keys, ...), custom_call_target="tpu_custom_call" | custom-call | flops 553648128 | bytes 2228256 | tf_op jit(solution)/shard_map/pallas_call | solution.py:232
  22.3 0.4 collective-permute-start.5
  22.7 2.7 %shard_map.146 = bf16[64,640]{1,0:T(8,128)(2,1)S(1)} custom-call(s32[8]{0:T(128)S(1)} %copy-done.6, bf16[64,512]{1,0:T(8,128)(2,1)S(1)} %collective-permute-done.6.query, bf16[2,2048,128]{2,1,0:T(8,128)(2,1)S(1)} %copy-done, bf16[2,2048,128]{2,1,0:T(8,128)(2,1)S(1)} %copy-done.1, bf16[128,128]{1,0:T(8,128)(2,1)S(1)} %get-tuple-element.27.tail_keys, ...), custom_call_target="tpu_custom_call" | custom-call | flops 553648128 | bytes 2228256 | tf_op jit(solution)/shard_map/pallas_call | solution.py:232
  25.4 3.5 %collective-permute-start.7 = (bf16[64,640]{1,0:T(8,128)(2,1)S(1)}, bf16[64,640]{1,0:T(8,128)(2,1)S(1)}, u32[]{:S(2)}, u32[]{:S(2)}) collective-permute-start(bf16[64,640]{1,0:T(8,128)(2,1)S(1)} %shard_map.146), channel_id=1, source_target_pairs={{0,128},{64,192},{128,0},{192,64},{1,129},{65,193},{129,1},{193,65... | collective-permute-start | bytes 245768 | tf_op jit(solution)/shard_map/ppermute | solution.py:245
  28.9 2.7 %shard_map.147 = bf16[64,640]{1,0:T(8,128)(2,1)S(1)} custom-call(s32[8]{0:T(128)S(1)} %copy-done.6, bf16[64,512]{1,0:T(8,128)(2,1)S(1)} %collective-permute-done.8.query, bf16[2,2048,128]{2,1,0:T(8,128)(2,1)S(1)} %copy-done, bf16[2,2048,128]{2,1,0:T(8,128)(2,1)S(1)} %copy-done.1, bf16[128,128]{1,0:T(8,128)(2,1)S(1)} %get-tuple-element.27.tail_keys, ...), custom_call_target="tpu_custom_call" | custom-call | flops 553648128 | bytes 2228256 | tf_op jit(solution)/shard_map/pallas_call | solution.py:232
  31.7 2.7 %shard_map.144.own_part = bf16[64,640]{1,0:T(8,128)(2,1)S(1)} custom-call(s32[8]{0:T(128)S(1)} %copy-done.6, bf16[64,512]{1,0:T(8,128)(2,1)S(1)} %get-tuple-element.26.query, bf16[2,2048,128]{2,1,0:T(8,128)(2,1)S(1)} %copy-done, bf16[2,2048,128]{2,1,0:T(8,128)(2,1)S(1)} %copy-done.1, bf16[128,128]{1,0:T(8,128)(2,1)S(1)} %get-tuple-element.27.tail_keys, ...), custom_call_target="tpu_custom_call" | custom-call | flops 553648128 | bytes 2228256 | tf_op jit(solution)/shard_map/pallas_call | solution.py:232
  34.5 2.3 %collective-permute-done.9.part3 = bf16[64,640]{1,0:T(8,128)(2,1)S(1)} collective-permute-done((bf16[64,640]{1,0:T(8,128)(2,1)S(1)}, bf16[64,640]{1,0:T(8,128)(2,1)S(1)}, u32[]{:S(2)}, u32[]{:S(2)}) %collective-permute-start.9) | collective-permute-done | bytes 81952 | tf_op jit(solution)/shard_map/ppermute | solution.py:245
  36.8 1.8 %shard_map.148 = (bf16[4,8,4608]{2,1,0:T(8,128)(2,1)S(1)}, f32[4,8,4608]{2,1,0:T(8,128)S(1)}) custom-call(bf16[64,640]{1,0:T(8,128)(2,1)S(1)} %shard_map.144.own_part, bf16[64,640]{1,0:T(8,128)(2,1)S(1)} %collective-permute-done.5.part1, bf16[64,640]{1,0:T(8,128)(2,1)S(1)} %collective-permute-done.7.part2, bf16[64,640]{1,0:T(8,128)(2,1)S(1)} %collective-permute-done.9.part3, ...), custom_call_target="tpu_custom_call" | custom-call | flops 268435456 | bytes 4587520 | tf_op jit(solution)/shard_map/pallas_call | solution.py:232
  38.6 3.7 %collective-permute-start.10 = (bf16[4,8,4608]{2,1,0:T(8,128)(2,1)S(1)}, bf16[4,8,4608]{2,1,0:T(8,128)(2,1)S(1)}, u32[]{:S(2)}, u32[]{:S(2)}) collective-permute-start(bf16[4,8,4608]{2,1,0:T(8,128)(2,1)S(1)} %get-tuple-element.31), channel_id=1, source_target_pairs={{0,8},{8,0},{16,24},{24,16},{32,40},{40,32},{48,56},{56,48},{1,9},... | collective-permute-start | bytes 884744 | tf_op jit(solution)/shard_map/ppermute | solution.py:245
  42.3 1.2 %collective-permute-done.10.received = bf16[4,8,4608]{2,1,0:T(8,128)(2,1)S(1)} collective-permute-done((bf16[4,8,4608]{2,1,0:T(8,128)(2,1)S(1)}, bf16[4,8,4608]{2,1,0:T(8,128)(2,1)S(1)}, u32[]{:S(2)}, u32[]{:S(2)}) %collective-permute-start.10) | collective-permute-done | bytes 294944 | tf_op jit(solution)/shard_map/ppermute | solution.py:245
  43.9 2.3 %collective-permute-start.12 = (bf16[8,4608]{1,0:T(8,128)(2,1)S(1)}, bf16[8,4608]{1,0:T(8,128)(2,1)S(1)}, u32[]{:S(2)}, u32[]{:S(2)}) collective-permute-start(bf16[8,4608]{1,0:T(8,128)(2,1)S(1)} %get-tuple-element.34), channel_id=1, source_target_pairs={{0,32},{8,40},{16,48},{24,56},{32,0},{40,8},{48,16},{56,24},{1,33}... | collective-permute-start | bytes 221192 | tf_op jit(solution)/shard_map/ppermute | solution.py:245
  46.2 1.4 %collective-permute-start.13 = (bf16[8,4608]{1,0:T(8,128)(2,1)S(1)}, bf16[8,4608]{1,0:T(8,128)(2,1)S(1)}, u32[]{:S(2)}, u32[]{:S(2)}) collective-permute-start(bf16[8,4608]{1,0:T(8,128)(2,1)S(1)} %get-tuple-element.35), channel_id=1, source_target_pairs={{0,48},{8,56},{16,32},{24,40},{32,16},{40,24},{48,0},{56,8},{1,49}... | collective-permute-start | bytes 221192 | tf_op jit(solution)/shard_map/ppermute | solution.py:245
  47.6 1.9 %collective-permute-done.12.in2 = bf16[8,4608]{1,0:T(8,128)(2,1)S(1)} collective-permute-done((bf16[8,4608]{1,0:T(8,128)(2,1)S(1)}, bf16[8,4608]{1,0:T(8,128)(2,1)S(1)}, u32[]{:S(2)}, u32[]{:S(2)}) %collective-permute-start.12) | collective-permute-done | bytes 73760 | tf_op jit(solution)/shard_map/ppermute | solution.py:245
  49.5 1.6 %collective-permute-done.13.in3 = bf16[8,4608]{1,0:T(8,128)(2,1)S(1)} collective-permute-done((bf16[8,4608]{1,0:T(8,128)(2,1)S(1)}, bf16[8,4608]{1,0:T(8,128)(2,1)S(1)}, u32[]{:S(2)}, u32[]{:S(2)}) %collective-permute-start.13) | collective-permute-done | bytes 73760 | tf_op jit(solution)/shard_map/ppermute | solution.py:245
  51.1 0.7 %shard_map.150 = (bf16[2,4,512]{2,1,0:T(4,128)(2,1)}, bf16[8,4096]{1,0:T(8,128)(2,1)}) custom-call(f32[8,4608]{1,0:T(8,128)S(1)} %get-tuple-element.32.own, bf16[8,4608]{1,0:T(8,128)(2,1)S(1)} %collective-permute-done.11.in1, bf16[8,4608]{1,0:T(8,128)(2,1)S(1)} %collective-permute-done.12.in2, bf16[8,4608]{1,0:T(8,128)(2,1)S(1)} %collective-permute-done.13.in3), custom_call_target="tpu_custom_call" | custom-call | bytes 368640 | tf_op jit(solution)/shard_map/pallas_call | solution.py:232
  (42 shorter events, 1.4 us)
Async XLA Ops:
  0.6 5.4 %copy-start.6 = (s32[8]{0:T(128)S(1)}, s32[8]{0:T(128)}, u32[]{:S(2)}) copy-start(s32[8]{0:T(128)} %lengths.9) | copy-start | bytes 100
  0.6 5.4 %copy-start.1 = (bf16[2,2048,128]{2,1,0:T(8,128)(2,1)S(1)}, bf16[2,2048,128]{2,1,0:T(8,128)(2,1)}, u32[]{:S(2)}) copy-start(bf16[2,2048,128]{2,1,0:T(8,128)(2,1)} %values.9) | copy-start | bytes 3145732
  0.7 5.4 %copy-start = (bf16[2,2048,128]{2,1,0:T(8,128)(2,1)S(1)}, bf16[2,2048,128]{2,1,0:T(8,128)(2,1)}, u32[]{:S(2)}) copy-start(bf16[2,2048,128]{2,1,0:T(8,128)(2,1)} %keys.9) | copy-start | bytes 3145732
  0.7 5.4 %copy-start.3 = (bf16[512,4096]{1,0:T(8,128)(2,1)S(1)}, bf16[512,4096]{1,0:T(8,128)(2,1)}, u32[]{:S(2)}) copy-start(bf16[512,4096]{1,0:T(8,128)(2,1)} %w_out.3) | copy-start | bytes 12582916
  0.7 5.4 %copy-start.5 = (bf16[4096,128]{1,0:T(8,128)(2,1)S(1)}, bf16[4096,128]{1,0:T(8,128)(2,1)}, u32[]{:S(2)}) copy-start(bf16[4096,128]{1,0:T(8,128)(2,1)} %w_value.3) | copy-start | bytes 3145732
  0.7 5.4 %copy-start.4 = (bf16[4096,128]{1,0:T(8,128)(2,1)S(1)}, bf16[4096,128]{1,0:T(8,128)(2,1)}, u32[]{:S(2)}) copy-start(bf16[4096,128]{1,0:T(8,128)(2,1)} %w_key.3) | copy-start | bytes 3145732
  0.7 5.4 %copy-start.2 = (bf16[4096,512]{1,0:T(8,128)(2,1)S(1)}, bf16[4096,512]{1,0:T(8,128)(2,1)}, u32[]{:S(2)}) copy-start(bf16[4096,512]{1,0:T(8,128)(2,1)} %w_query.3) | copy-start | bytes 12582916
  0.7 5.4 %copy-start.8 = (bf16[128]{0:T(256)(128)(2,1)S(1)}, bf16[128]{0:T(256)(128)(2,1)}, u32[]{:S(2)}) copy-start(bf16[128]{0:T(256)(128)(2,1)} %param.18) | copy-start | bytes 772
  0.7 5.4 %copy-start.7 = (bf16[128]{0:T(256)(128)(2,1)S(1)}, bf16[128]{0:T(256)(128)(2,1)}, u32[]{:S(2)}) copy-start(bf16[128]{0:T(256)(128)(2,1)} %param.17) | copy-start | bytes 772
  1.7 4.5 %copy-start.11 = (bf16[2,4096]{1,0:T(2,128)(2,1)S(1)}, bf16[2,4096]{1,0:T(2,128)(2,1)}, u32[]{:S(2)}) copy-start(bf16[2,4096]{1,0:T(2,128)(2,1)} %embed.1) | copy-start | bytes 49156
  1.7 7.6 %collective-permute-start.2 = (bf16[8,4096]{1,0:T(8,128)(2,1)S(1)}, bf16[8,4096]{1,0:T(8,128)(2,1)S(1)}, u32[]{:S(2)}, u32[]{:S(2)}) collective-permute-start(bf16[8,4096]{1,0:T(8,128)(2,1)S(1)} %shard_map.140.rows0), channel_id=1, source_target_pairs={{0,48},{8,56},{16,32},{24,40},{32,16},{40,24},{48,0},{56,8},{1,49}... | collective-permute-start | bytes 196616 | tf_op jit(solution)/shard_map/ppermute | solution.py:245
  5.4 4.7 %collective-permute-start.1 = (bf16[8,4096]{1,0:T(8,128)(2,1)S(1)}, bf16[8,4096]{1,0:T(8,128)(2,1)S(1)}, u32[]{:S(2)}, u32[]{:S(2)}) collective-permute-start(bf16[8,4096]{1,0:T(8,128)(2,1)S(1)} %shard_map.140.rows0), channel_id=1, source_target_pairs={{0,32},{8,40},{16,48},{24,56},{32,0},{40,8},{48,16},{56,24},{1,33}... | collective-permute-start | bytes 196616 | tf_op jit(solution)/shard_map/ppermute | solution.py:245
  5.7 4.4 %collective-permute-start = (bf16[8,4096]{1,0:T(8,128)(2,1)S(1)}, bf16[8,4096]{1,0:T(8,128)(2,1)S(1)}, u32[]{:S(2)}, u32[]{:S(2)}) collective-permute-start(bf16[8,4096]{1,0:T(8,128)(2,1)S(1)} %shard_map.140.rows0), channel_id=1, source_target_pairs={{0,16},{8,24},{16,0},{24,8},{32,48},{40,56},{48,32},{56,40},{1,17}... | collective-permute-start | bytes 196616 | tf_op jit(solution)/shard_map/ppermute | solution.py:245
  10.3 3.5 %collective-permute-start.3 = (bf16[4,8,4096]{2,1,0:T(8,128)(2,1)S(1)}, bf16[4,8,4096]{2,1,0:T(8,128)(2,1)S(1)}, u32[]{:S(2)}, u32[]{:S(2)}) collective-permute-start(bf16[4,8,4096]{2,1,0:T(8,128)(2,1)S(1)} %get-tuple-element.21.mine), channel_id=1, source_target_pairs={{0,8},{8,0},{16,24},{24,16},{32,40},{40,32},{48,56},{56,48},{1,9},... | collective-permute-start | bytes 786440 | tf_op jit(solution)/shard_map/ppermute | solution.py:245
  15.1 4.4 %collective-permute-start.4 = (bf16[64,512]{1,0:T(8,128)(2,1)S(1)}, bf16[64,512]{1,0:T(8,128)(2,1)S(1)}, u32[]{:S(2)}, u32[]{:S(2)}) collective-permute-start(bf16[64,512]{1,0:T(8,128)(2,1)S(1)} %get-tuple-element.26.query), channel_id=1, source_target_pairs={{0,64},{64,0},{128,192},{192,128},{1,65},{65,1},{129,193},{193,129... | collective-permute-start | bytes 196616 | tf_op jit(solution)/shard_map/ppermute | solution.py:245
  16.6 6.1 %collective-permute-start.6 = (bf16[64,512]{1,0:T(8,128)(2,1)S(1)}, bf16[64,512]{1,0:T(8,128)(2,1)S(1)}, u32[]{:S(2)}, u32[]{:S(2)}) collective-permute-start(bf16[64,512]{1,0:T(8,128)(2,1)S(1)} %get-tuple-element.26.query), channel_id=1, source_target_pairs={{0,128},{64,192},{128,0},{192,64},{1,129},{65,193},{129,1},{193,65... | collective-permute-start | bytes 196616 | tf_op jit(solution)/shard_map/ppermute | solution.py:245
  19.5 9.4 %collective-permute-start.8 = (bf16[64,512]{1,0:T(8,128)(2,1)S(1)}, bf16[64,512]{1,0:T(8,128)(2,1)S(1)}, u32[]{:S(2)}, u32[]{:S(2)}) collective-permute-start(bf16[64,512]{1,0:T(8,128)(2,1)S(1)} %get-tuple-element.26.query), channel_id=1, source_target_pairs={{0,192},{64,128},{128,64},{192,0},{1,193},{65,129},{129,65},{193,1... | collective-permute-start | bytes 196616 | tf_op jit(solution)/shard_map/ppermute | solution.py:245
  22.3 12.2 %collective-permute-start.5 = (bf16[64,640]{1,0:T(8,128)(2,1)S(1)}, bf16[64,640]{1,0:T(8,128)(2,1)S(1)}, u32[]{:S(2)}, u32[]{:S(2)}) collective-permute-start(bf16[64,640]{1,0:T(8,128)(2,1)S(1)} %shard_map.145), channel_id=1, source_target_pairs={{0,64},{64,0},{128,192},{192,128},{1,65},{65,1},{129,193},{193,129... | collective-permute-start | bytes 245768 | tf_op jit(solution)/shard_map/ppermute | solution.py:245
  25.4 9.1 %collective-permute-start.7 = (bf16[64,640]{1,0:T(8,128)(2,1)S(1)}, bf16[64,640]{1,0:T(8,128)(2,1)S(1)}, u32[]{:S(2)}, u32[]{:S(2)}) collective-permute-start(bf16[64,640]{1,0:T(8,128)(2,1)S(1)} %shard_map.146), channel_id=1, source_target_pairs={{0,128},{64,192},{128,0},{192,64},{1,129},{65,193},{129,1},{193,65... | collective-permute-start | bytes 245768 | tf_op jit(solution)/shard_map/ppermute | solution.py:245
  31.6 5.2 %collective-permute-start.9 = (bf16[64,640]{1,0:T(8,128)(2,1)S(1)}, bf16[64,640]{1,0:T(8,128)(2,1)S(1)}, u32[]{:S(2)}, u32[]{:S(2)}) collective-permute-start(bf16[64,640]{1,0:T(8,128)(2,1)S(1)} %shard_map.147), channel_id=1, source_target_pairs={{0,192},{64,128},{128,64},{192,0},{1,193},{65,129},{129,65},{193,1... | collective-permute-start | bytes 245768 | tf_op jit(solution)/shard_map/ppermute | solution.py:245
  38.6 4.9 %collective-permute-start.10 = (bf16[4,8,4608]{2,1,0:T(8,128)(2,1)S(1)}, bf16[4,8,4608]{2,1,0:T(8,128)(2,1)S(1)}, u32[]{:S(2)}, u32[]{:S(2)}) collective-permute-start(bf16[4,8,4608]{2,1,0:T(8,128)(2,1)S(1)} %get-tuple-element.31), channel_id=1, source_target_pairs={{0,8},{8,0},{16,24},{24,16},{32,40},{40,32},{48,56},{56,48},{1,9},... | collective-permute-start | bytes 884744 | tf_op jit(solution)/shard_map/ppermute | solution.py:245
  43.6 3.9 %collective-permute-start.11 = (bf16[8,4608]{1,0:T(8,128)(2,1)S(1)}, bf16[8,4608]{1,0:T(8,128)(2,1)S(1)}, u32[]{:S(2)}, u32[]{:S(2)}) collective-permute-start(bf16[8,4608]{1,0:T(8,128)(2,1)S(1)} %get-tuple-element.33), channel_id=1, source_target_pairs={{0,16},{8,24},{16,0},{24,8},{32,48},{40,56},{48,32},{56,40},{1,17}... | collective-permute-start | bytes 221192 | tf_op jit(solution)/shard_map/ppermute | solution.py:245
  43.9 5.6 %collective-permute-start.12 = (bf16[8,4608]{1,0:T(8,128)(2,1)S(1)}, bf16[8,4608]{1,0:T(8,128)(2,1)S(1)}, u32[]{:S(2)}, u32[]{:S(2)}) collective-permute-start(bf16[8,4608]{1,0:T(8,128)(2,1)S(1)} %get-tuple-element.34), channel_id=1, source_target_pairs={{0,32},{8,40},{16,48},{24,56},{32,0},{40,8},{48,16},{56,24},{1,33}... | collective-permute-start | bytes 221192 | tf_op jit(solution)/shard_map/ppermute | solution.py:245
  46.2 4.9 %collective-permute-start.13 = (bf16[8,4608]{1,0:T(8,128)(2,1)S(1)}, bf16[8,4608]{1,0:T(8,128)(2,1)S(1)}, u32[]{:S(2)}, u32[]{:S(2)}) collective-permute-start(bf16[8,4608]{1,0:T(8,128)(2,1)S(1)} %get-tuple-element.35), channel_id=1, source_target_pairs={{0,48},{8,56},{16,32},{24,40},{32,16},{40,24},{48,0},{56,8},{1,49}... | collective-permute-start | bytes 221192 | tf_op jit(solution)/shard_map/ppermute | solution.py:245
  (3 other events, 9.8 us)

commit v3 on v2

--- a/solution.py
+++ b/solution.py
@@ -15,6 +15,7 @@
 STEPS = 4
 SCALE2 = math.log2(math.e) / math.sqrt(HEAD)
 NEG = -1e30
+CHUNK = 1024
 F32 = jnp.float32
 BF16 = jnp.bfloat16
 MIB = 1024 * 1024
@@ -137,35 +138,50 @@
     tail_values[...] = jnp.concatenate([value, dvalue[...], pad], axis=0).astype(BF16)
 
 
-def attend_kernel(flip, lengths, query, keys, values, tail_keys, tail_values, out):
+def attend_kernel(
+    flip, lengths, query, keys, values, tail_keys, tail_values, _, out
+):
     path = lax.axis_index("path")
     block = path ^ flip
-    rows = query.shape[0]
-    q = jnp.concatenate(
-        [query[:, h * HEAD : (h + 1) * HEAD] for h in range(GROUP)], axis=0
-    )
-    total_rows = rows * GROUP
-    scores = []
-    for i in range(2):
-        s = dot_t(q, keys[i])
-        slot = lax.broadcasted_iota(jnp.int32, s.shape, 1)
-        scores.append(jnp.where(slot < lengths[path * 2 + i], s, NEG))
-    s = dot_t(q, tail_keys[...])
-    col = lax.broadcasted_iota(jnp.int32, s.shape, 1)
-    row = lax.broadcasted_iota(jnp.int32, s.shape, 0) % rows
-    causal = (col < rows) & (path * rows + col <= block * rows + row)
-    recent = (col >= rows) & (col < rows + 8)
-    scores.append(jnp.where(causal | recent, s, NEG))
-    peak = scores[0].max(axis=-1, keepdims=True)
-    for s in scores[1:]:
-        peak = jnp.maximum(peak, s.max(axis=-1, keepdims=True))
-    peak = (peak * SCALE2).astype(BF16).astype(F32)
-    total = jnp.zeros((total_rows, 1), F32)
-    mix = jnp.zeros((total_rows, HEAD), F32)
-    for s, v in zip(scores, (values[0], values[1], tail_values[...])):
-        w = jnp.exp2(s * SCALE2 - peak)
-        total = total + jnp.sum(w, axis=-1, keepdims=True)
-        mix = mix + dot(w.astype(BF16), v)
+    rows = out.shape[0]
+    q = jnp.concatenate([query[:, h * HEAD : (h + 1) * HEAD] for h in range(GROUP)], axis=0)
+    chunks = [(i, c) for i in range(2) for c in range(0, keys.shape[1], CHUNK)]
+
+    def tail_scores():
+        s = dot_t(q, tail_keys[...])
+        col = lax.broadcasted_iota(jnp.int32, s.shape, 1)
+        row = lax.broadcasted_iota(jnp.int32, s.shape, 0) % rows
+        causal = (col < rows) & (path * rows + col <= block * rows + row)
+        recent = (col >= rows) & (col < rows + 8)
+        return jnp.where(causal | recent, s, NEG)
+
+    def chunk_scores(i, c):
+        s = dot_t(q, keys[i, c : c + CHUNK, :])
+        slot = lax.broadcasted_iota(jnp.int32, (1, CHUNK), 1) + c
+        return s + jnp.where(slot < lengths[path * 2 + i], 0.0, NEG)
+
+    scores = tail_scores()
+    peak = jnp.max(scores, axis=-1, keepdims=True) * SCALE2
+    coming = chunk_scores(*chunks[0])
+    w = jnp.exp2(scores * SCALE2 - peak)
+    total = jnp.sum(w, axis=-1, keepdims=True)
+    mix = dot(w.astype(BF16), tail_values[...])
+    for n, (i, c) in enumerate(chunks):
+        scores = coming
+        if n + 1 < len(chunks):
+            coming = chunk_scores(*chunks[n + 1])
+        higher = jnp.maximum(peak, jnp.max(scores, axis=-1, keepdims=True) * SCALE2)
+        fade = jnp.exp2(peak - higher)
+        w = jnp.exp2(scores * SCALE2 - higher)
+        total = total * fade + jnp.sum(w, axis=-1, keepdims=True)
+        mix = mix * fade + dot(w.astype(BF16), values[i, c : c + CHUNK, :])
+        peak = higher
+    rounded = peak.astype(BF16).astype(F32)
+    fade = jnp.exp2(peak - rounded)
+    write_part(out, rows, mix * fade, rounded, total * fade)
+
+
+def write_part(out, rows, mix, peak, total):
     high = total.astype(BF16).astype(F32)
     low = total - high
     lane = lax.broadcasted_iota(jnp.int32, (rows, HEAD), 1)
@@ -178,30 +194,57 @@
     out[:, GROUP * HEAD :] = stats.astype(BF16)
 
 
-def output_kernel(own_part, part1, part2, part3, w_out, dterms, send, keep, attn):
-    core = lax.axis_index("tensor") % 2
-    parts = (own_part, part1, part2, part3)
-    stats = [x[:, GROUP * HEAD :].astype(F32) for x in parts]
+def merge(parts):
+    mixes = []
+    totals = []
+    peak = functools.reduce(jnp.maximum, [p for _, p, _ in parts])
+    scales = [jnp.exp2(p - peak) for _, p, _ in parts]
+    total = sum(w * t for w, (_, _, t) in zip(scales, parts))
     for h in range(GROUP):
         at = slice(h * HEAD, (h + 1) * HEAD)
-        peaks = [s[:, h : h + 1] for s in stats]
-        peak = functools.reduce(jnp.maximum, peaks)
-        mix = 0.0
-        total = 0.0
-        for s, p, x in zip(stats, peaks, parts):
-            w = jnp.exp2(p - peak)
-            total = total + w * (s[:, GROUP + h : GROUP + h + 1] + s[:, 2 * GROUP + h : 2 * GROUP + h + 1])
-            mix = mix + w * x[:, at].astype(F32)
-        attn[:, at] = mix / total
+        mixes.append(sum(w[:, h : h + 1] * x[:, at] for w, (x, _, _) in zip(scales, parts)))
+    return mixes, peak, total
+
+
+def read_part(part):
+    width = GROUP * HEAD
+    stats = part[:, width:].astype(F32)
+    total = stats[:, GROUP : 2 * GROUP] + stats[:, 2 * GROUP : 3 * GROUP]
+    return part[:, :width].astype(F32), stats[:, :GROUP], total
+
+
+def merge_kernel(part, received, out):
+    rows = part.shape[0]
+    mixes, peak, total = merge([read_part(part[...]), read_part(received[...])])
+    mix = jnp.concatenate(mixes, axis=0)
+    peak, total = (
+        jnp.concatenate([x[:, h : h + 1] for h in range(GROUP)], axis=0) for x in (peak, total)
+    )
+    write_part(out, rows, mix, peak, total)
+
+
+def project_half(attn, which, w_out, dterms, ref):
     width = w_out.shape[1]
-    for which, ref in ((1 - core, send), (core, keep)):
-        lhs = jnp.concatenate(
-            [attn[pl.ds(pl.multiple_of((2 * y + which) * 8, 8), 8), :] for y in range(4)], axis=0
-        ).astype(BF16)
-        res = dot(lhs, w_out[...])
-        for y in range(4):
-            ref[y, :, :width] = res[y * 8 : (y + 1) * 8].astype(ref.dtype)
-            ref[y, :, width:] = dterms[2 * y + which].astype(ref.dtype)
+    lhs = jnp.concatenate(
+        [attn[pl.ds(pl.multiple_of((2 * y + which) * 8, 8), 8), :] for y in range(4)], axis=0
+    ).astype(BF16)
+    res = dot(lhs, w_out[...])
+    for y in range(4):
+        ref[y, :, :width] = res[y * 8 : (y + 1) * 8].astype(ref.dtype)
+        ref[y, :, width:] = dterms[2 * y + which].astype(ref.dtype)
+
+
+def send_kernel(own_part, part1, part2, w_out, dterms, send, attn):
+    core = lax.axis_index("tensor") % 2
+    parts = (own_part[...], part1[...], part2[...])
+    mixes, _, total = merge([read_part(x) for x in parts])
+    for h in range(GROUP):
+        attn[:, h * HEAD : (h + 1) * HEAD] = mixes[h] / total[:, h : h + 1]
+    project_half(attn, 1 - core, w_out, dterms, send)
+
+
+def keep_kernel(attn, w_out, dterms, keep):
+    project_half(attn, lax.axis_index("tensor") % 2, w_out, dterms, keep)
 
 
 def fold_kernel(keep, received, own_out, out1, out2, out3):
@@ -285,38 +328,54 @@
         (*across, norm_gain, dkey, dvalue),
     )
     other = flip(mine, "tensor", 8, 1)
-    query, tail_keys, tail_values = call(
+    query, *tails = call(
         project_kernel,
         [((rows, GROUP * HEAD), BF16), ((128, HEAD), BF16), ((128, HEAD), BF16)],
-        (mine, other, query_gain, key_gain, w_query, key_weight, w_value, cosine, sine,
-         dkey, dvalue),
+        (mine, other, query_gain, key_gain, w_query, key_weight, w_value, cosine, sine, dkey, dvalue),
         scratch=[pltpu.VMEM((rows, width), F32)],
         limit=24,
         flops=2 * 64 * 4096 * 768,
     )
-
-    queries = [query] + [flip(query, "path", 4, k) for k in (1, 2, 3)]
-    parts = []
-    for k in range(4):
+    queries = {0: query}
+    for k in (3, 2, 1):
+        queries[k] = flip(query, "path", 4, k)
+
+    def attend(k, after):
         (part,) = call(
             functools.partial(attend_kernel, k),
             [((rows, (GROUP + 1) * HEAD), BF16)],
-            (lengths, queries[k], key_cache, value_cache, tail_keys, tail_values),
-            limit=32,
+            (lengths, queries[k], key_cache, value_cache, *tails, after),
+            limit=24,
             smem=(0,),
-            flops=4 * 256 * 4224 * 128,
+            flops=3 * 10**9,
         )
-        parts.append(part if k == 0 else flip(part, "path", 4, k))
-
-    send, keep = call(
-        output_kernel,
-        [((4, 8, width + width // 8), BF16), ((4, 8, width + width // 8), F32)],
-        (*parts, w_out, dterms),
-        scratch=[pltpu.VMEM((rows, GROUP * HEAD), F32)],
+        return part
+
+    part3 = attend(3, query)
+    received3 = flip(part3, "path", 4, 1)
+    part2 = attend(2, part3)
+    (merged2,) = call(
+        merge_kernel, [(part2.shape, BF16)], (part2, received3), limit=24, flops=10**8
+    )
+    received2 = flip(merged2, "path", 4, 2)
+    part1 = attend(1, merged2)
+    received1 = flip(part1, "path", 4, 1)
+    own_part = attend(0, part1)
+    send, attn = call(
+        send_kernel,
+        [((4, 8, width + width // 8), BF16), ((rows, GROUP * HEAD), F32)],
+        (own_part, received1, received2, w_out, dterms),
         limit=24,
-        flops=2 * 64 * 512 * 4096,
+        flops=64 * 512 * 4096,
     )
     received = flip(send, "tensor", 8, 1)
+    (keep,) = call(
+        keep_kernel,
+        [((4, 8, width + width // 8), F32)],
+        (attn, w_out, dterms),
+        limit=24,
+        flops=64 * 512 * 4096,
+    )
     own, out1, out2, out3 = call(
         fold_kernel,
         [((8, width + width // 8), F32)] + [((8, width + width // 8), BF16)] * 3,

time: 51.9 us -> 50.3 us (0.969)
  Pallas kernels: 18 us -> 16.7 us
    pallas_call x11 -> x13, Pallas kernels: 18 us -> 16.7 us  [call(): pl.pallas_call(kernel, out_shape=outs, in_specs=specs, out_specs=tuple((p...]
  transfers between devices with their start and end apart: 14 -> 14, of which waited for: 6 -> 9; matrix products, arithmetic and copies ran while one was open for 0% -> 0% of each run, Pallas kernels for 27% -> 27%
where the time goes in v3:
time: 50.3 us; the launch traced here: 50.1 us
  starting transfers between devices  22.6 us (45%)
  Pallas kernels  16.7 us (33%)
  waiting for transfers between devices  8.82 us (18%)
  local copies, waits for them, and re-layouts  1.04 us (2%)
  between operations  0.89 us (2%)
    ppermute x14, starting transfers between devices, flip(): return lax.ppermute(x, axis, [(i, i ^ k) for i in range(size)])  22.6 us
    pallas_call x13, Pallas kernels, call(): pl.pallas_call(kernel, out_shape=outs, in_specs=specs, out_specs=tuple((p...  16.7 us
    ppermute x14, waiting for transfers between devices, flip(): return lax.ppermute(x, axis, [(i, i ^ k) for i in range(size)])  8.82 us
    unnamed x26, local copies, waits for them, and re-layouts  1.03 us
  transfers between devices with their start and end apart: 14, of which 9 were waited for; matrix products, arithmetic and copies ran while one was open for 0% of the time, Pallas kernels for 27%

profile of v3, /device:TPU:1, one launch (start us, length us, event | category | flops | bytes accessed | tf_op | source)
XLA Modules:
  0.0 50.1 jit_solution(9923146412471771839)
XLA Ops:
  0.7 1.0 %copy-done.8 = bf16[8,4096]{1,0:T(8,128)(2,1)S(1)} copy-done((bf16[8,4096]{1,0:T(8,128)(2,1)S(1)}, bf16[8,4096]{1,0:T(8,128)(2,1)}, u32[]{:S(2)}) %copy-start.8) | copy-done | bytes 65560
  1.7 3.7 %collective-permute-start.2 = (bf16[8,4096]{1,0:T(8,128)(2,1)S(1)}, bf16[8,4096]{1,0:T(8,128)(2,1)S(1)}, u32[]{:S(2)}, u32[]{:S(2)}) collective-permute-start(bf16[8,4096]{1,0:T(8,128)(2,1)S(1)} %shard_map.140.rows0), channel_id=1, source_target_pairs={{0,48},{8,56},{16,32},{24,40},{32,16},{40,24},{48,0},{56,8},{1,49}... | collective-permute-start | bytes 196616 | tf_op jit(solution)/shard_map/ppermute | solution.py:288
  6.2 3.1 %shard_map.141 = (bf16[8,8,512]{2,1,0:T(8,128)(2,1)S(1)}, f32[8,128]{1,0:T(8,128)S(1)}, f32[8,128]{1,0:T(8,128)S(1)}, f32[64,128]{1,0:T(8,128)S(1)}, f32[64,128]{1,0:T(8,128)S(1)}) custom-call(s32[8]{0:T(128)S(1)} %copy-done.11, bf16[2,4,4096]{2,1,0:T(4,128)(2,1)S(1)} %copy-done.9, bf16[2,4096]{1,0:T(2,128)(2,1)S(1)} %copy-done.10, ...), custom_call_target="tpu_custom_call" | custom-call | flops 6000000000 | bytes 12673568 | tf_op jit(solution)/shard_map/pallas_call | solution.py:275
  9.3 0.8 %collective-permute-done.1.rows2 = bf16[8,4096]{1,0:T(8,128)(2,1)S(1)} collective-permute-done((bf16[8,4096]{1,0:T(8,128)(2,1)S(1)}, bf16[8,4096]{1,0:T(8,128)(2,1)S(1)}, u32[]{:S(2)}, u32[]{:S(2)}) %collective-permute-start.1) | collective-permute-done | bytes 65568 | tf_op jit(solution)/shard_map/ppermute | solution.py:288
  10.3 2.4 %collective-permute-start.3 = (bf16[4,8,4096]{2,1,0:T(8,128)(2,1)S(1)}, bf16[4,8,4096]{2,1,0:T(8,128)(2,1)S(1)}, u32[]{:S(2)}, u32[]{:S(2)}) collective-permute-start(bf16[4,8,4096]{2,1,0:T(8,128)(2,1)S(1)} %get-tuple-element.21.mine), channel_id=1, source_target_pairs={{0,8},{8,0},{16,24},{24,16},{32,40},{40,32},{48,56},{56,48},{1,9},... | collective-permute-start | bytes 786440 | tf_op jit(solution)/shard_map/ppermute | solution.py:288
  12.7 1.2 %collective-permute-done.3.other = bf16[4,8,4096]{2,1,0:T(8,128)(2,1)S(1)} collective-permute-done((bf16[4,8,4096]{2,1,0:T(8,128)(2,1)S(1)}, bf16[4,8,4096]{2,1,0:T(8,128)(2,1)S(1)}, u32[]{:S(2)}, u32[]{:S(2)}) %collective-permute-start.3) | collective-permute-done | bytes 262176 | tf_op jit(solution)/shard_map/ppermute | solution.py:288
  13.9 1.3 %shard_map.143 = (bf16[64,512]{1,0:T(8,128)(2,1)S(1)}, bf16[128,128]{1,0:T(8,128)(2,1)S(1)}, bf16[128,128]{1,0:T(8,128)(2,1)S(1)}) custom-call(bf16[4,8,4096]{2,1,0:T(8,128)(2,1)S(1)} %get-tuple-element.21.mine, bf16[4,8,4096]{2,1,0:T(8,128)(2,1)S(1)} %collective-permute-done.3.other, bf16[1,128]{1,0:T(2,128)(2,1)S(1)} %bitcast.3, ...), custom_call_target="tpu_custom_call" | custom-call | flops 402653184 | bytes 6889984 | tf_op jit(solution)/shard_map/pallas_call | solution.py:275
  15.1 4.1 %collective-permute-start.6 = (bf16[64,512]{1,0:T(8,128)(2,1)S(1)}, bf16[64,512]{1,0:T(8,128)(2,1)S(1)}, u32[]{:S(2)}, u32[]{:S(2)}) collective-permute-start(bf16[64,512]{1,0:T(8,128)(2,1)S(1)} %get-tuple-element.26._.query), channel_id=1, source_target_pairs={{0,192},{64,128},{128,64},{192,0},{1,193},{65,129},{129,65},{193,1... | collective-permute-start | bytes 196616 | tf_op jit(solution)/shard_map/ppermute | solution.py:288
  19.6 1.8 %collective-permute-done.6.query = bf16[64,512]{1,0:T(8,128)(2,1)S(1)} collective-permute-done((bf16[64,512]{1,0:T(8,128)(2,1)S(1)}, bf16[64,512]{1,0:T(8,128)(2,1)S(1)}, u32[]{:S(2)}, u32[]{:S(2)}) %collective-permute-start.6) | collective-permute-done | bytes 65568 | tf_op jit(solution)/shard_map/ppermute | solution.py:288
  21.4 2.3 %shard_map.144._ = bf16[64,640]{1,0:T(8,128)(2,1)S(1)} custom-call(s32[8]{0:T(128)S(1)} %copy-done.11, bf16[64,512]{1,0:T(8,128)(2,1)S(1)} %collective-permute-done.6.query, bf16[2,2048,128]{2,1,0:T(8,128)(2,1)S(1)} %copy-done.6, bf16[2,2048,128]{2,1,0:T(8,128)(2,1)S(1)} %copy-done.7, bf16[128,128]{1,0:T(8,128)(2,1)S(1)} %get-tuple-element.27.tail_keys, ...), custom_call_target="tpu_custom_call" | custom-call | flops 3000000000 | bytes 2293792 | tf_op jit(solution)/shard_map/pallas_call | solution.py:275
  24.2 2.3 %shard_map.145.part = bf16[64,640]{1,0:T(8,128)(2,1)S(1)} custom-call(s32[8]{0:T(128)S(1)} %copy-done.11, bf16[64,512]{1,0:T(8,128)(2,1)S(1)} %collective-permute-done.5.query, bf16[2,2048,128]{2,1,0:T(8,128)(2,1)S(1)} %copy-done.6, bf16[2,2048,128]{2,1,0:T(8,128)(2,1)S(1)} %copy-done.7, bf16[128,128]{1,0:T(8,128)(2,1)S(1)} %get-tuple-element.27.tail_keys, ...), custom_call_target="tpu_custom_call" | custom-call | flops 3000000000 | bytes 2310176 | tf_op jit(solution)/shard_map/pallas_call | solution.py:275
  26.4 0.7 %collective-permute-done.7.received = bf16[64,640]{1,0:T(8,128)(2,1)S(1)} collective-permute-done((bf16[64,640]{1,0:T(8,128)(2,1)S(1)}, bf16[64,640]{1,0:T(8,128)(2,1)S(1)}, u32[]{:S(2)}, u32[]{:S(2)}) %collective-permute-start.7) | collective-permute-done | bytes 81952 | tf_op jit(solution)/shard_map/ppermute | solution.py:288
  27.4 2.4 %collective-permute-start.9 = (bf16[64,640]{1,0:T(8,128)(2,1)S(1)}, bf16[64,640]{1,0:T(8,128)(2,1)S(1)}, u32[]{:S(2)}, u32[]{:S(2)}) collective-permute-start(bf16[64,640]{1,0:T(8,128)(2,1)S(1)} %shard_map.146._), channel_id=1, source_target_pairs={{0,128},{64,192},{128,0},{192,64},{1,129},{65,193},{129,1},{193,65... | collective-permute-start | bytes 245768 | tf_op jit(solution)/shard_map/ppermute | solution.py:288
  29.9 2.3 %shard_map.147._ = bf16[64,640]{1,0:T(8,128)(2,1)S(1)} custom-call(s32[8]{0:T(128)S(1)} %copy-done.11, bf16[64,512]{1,0:T(8,128)(2,1)S(1)} %collective-permute-done.4.query, bf16[2,2048,128]{2,1,0:T(8,128)(2,1)S(1)} %copy-done.6, bf16[2,2048,128]{2,1,0:T(8,128)(2,1)S(1)} %copy-done.7, bf16[128,128]{1,0:T(8,128)(2,1)S(1)} %get-tuple-element.27.tail_keys, ...), custom_call_target="tpu_custom_call" | custom-call | flops 3000000000 | bytes 2310176 | tf_op jit(solution)/shard_map/pallas_call | solution.py:275
  32.2 1.1 %collective-permute-start.8 = (bf16[64,640]{1,0:T(8,128)(2,1)S(1)}, bf16[64,640]{1,0:T(8,128)(2,1)S(1)}, u32[]{:S(2)}, u32[]{:S(2)}) collective-permute-start(bf16[64,640]{1,0:T(8,128)(2,1)S(1)} %shard_map.147._), channel_id=1, source_target_pairs={{0,64},{64,0},{128,192},{192,128},{1,65},{65,1},{129,193},{193,129... | collective-permute-start | bytes 245768 | tf_op jit(solution)/shard_map/ppermute | solution.py:288
  33.3 2.3 %shard_map.148.own_part = bf16[64,640]{1,0:T(8,128)(2,1)S(1)} custom-call(s32[8]{0:T(128)S(1)} %copy-done.11, bf16[64,512]{1,0:T(8,128)(2,1)S(1)} %get-tuple-element.26._.query, bf16[2,2048,128]{2,1,0:T(8,128)(2,1)S(1)} %copy-done.6, bf16[2,2048,128]{2,1,0:T(8,128)(2,1)S(1)} %copy-done.7, bf16[128,128]{1,0:T(8,128)(2,1)S(1)} %get-tuple-element.27.tail_keys, ...), custom_call_target="tpu_custom_call" | custom-call | flops 3000000000 | bytes 2310176 | tf_op jit(solution)/shard_map/pallas_call | solution.py:275
  35.7 1.0 %shard_map.149 = (bf16[4,8,4608]{2,1,0:T(8,128)(2,1)S(1)}, f32[64,512]{1,0:T(8,128)S(1)}) custom-call(bf16[64,640]{1,0:T(8,128)(2,1)S(1)} %shard_map.148.own_part, bf16[64,640]{1,0:T(8,128)(2,1)S(1)} %collective-permute-done.8.part1, bf16[64,640]{1,0:T(8,128)(2,1)S(1)} %collective-permute-done.9.part2, bf16[512,4096]{1,0:T(8,128)(2,1)S(1)} %copy-done, ...), custom_call_target="tpu_custom_call" | custom-call | flops 134217728 | bytes 4505600 | tf_op jit(solution)/shard_map/pallas_call | solution.py:275
  36.7 3.9 %collective-permute-start.10 = (bf16[4,8,4608]{2,1,0:T(8,128)(2,1)S(1)}, bf16[4,8,4608]{2,1,0:T(8,128)(2,1)S(1)}, u32[]{:S(2)}, u32[]{:S(2)}) collective-permute-start(bf16[4,8,4608]{2,1,0:T(8,128)(2,1)S(1)} %get-tuple-element.31), channel_id=1, source_target_pairs={{0,8},{8,0},{16,24},{24,16},{32,40},{40,32},{48,56},{56,48},{1,9},... | collective-permute-start | bytes 884744 | tf_op jit(solution)/shard_map/ppermute | solution.py:288
  40.6 0.8 %shard_map.150.keep = f32[4,8,4608]{2,1,0:T(8,128)S(1)} custom-call(f32[64,512]{1,0:T(8,128)S(1)} %get-tuple-element.30.attn, bf16[512,4096]{1,0:T(8,128)(2,1)S(1)} %copy-done, bf16[8,8,512]{2,1,0:T(8,128)(2,1)S(1)} %get-tuple-element.29.dterms), custom_call_target="tpu_custom_call" | custom-call | flops 134217728 | bytes 4390912 | tf_op jit(solution)/shard_map/pallas_call | solution.py:275
  42.2 2.3 %collective-permute-start.12 = (bf16[8,4608]{1,0:T(8,128)(2,1)S(1)}, bf16[8,4608]{1,0:T(8,128)(2,1)S(1)}, u32[]{:S(2)}, u32[]{:S(2)}) collective-permute-start(bf16[8,4608]{1,0:T(8,128)(2,1)S(1)} %get-tuple-element.34), channel_id=1, source_target_pairs={{0,32},{8,40},{16,48},{24,56},{32,0},{40,8},{48,16},{56,24},{1,33}... | collective-permute-start | bytes 221192 | tf_op jit(solution)/shard_map/ppermute | solution.py:288
  44.5 1.4 %collective-permute-start.13 = (bf16[8,4608]{1,0:T(8,128)(2,1)S(1)}, bf16[8,4608]{1,0:T(8,128)(2,1)S(1)}, u32[]{:S(2)}, u32[]{:S(2)}) collective-permute-start(bf16[8,4608]{1,0:T(8,128)(2,1)S(1)} %get-tuple-element.35), channel_id=1, source_target_pairs={{0,48},{8,56},{16,32},{24,40},{32,16},{40,24},{48,0},{56,8},{1,49}... | collective-permute-start | bytes 221192 | tf_op jit(solution)/shard_map/ppermute | solution.py:288
  45.9 1.9 %collective-permute-done.12.in2 = bf16[8,4608]{1,0:T(8,128)(2,1)S(1)} collective-permute-done((bf16[8,4608]{1,0:T(8,128)(2,1)S(1)}, bf16[8,4608]{1,0:T(8,128)(2,1)S(1)}, u32[]{:S(2)}, u32[]{:S(2)}) %collective-permute-start.12) | collective-permute-done | bytes 73760 | tf_op jit(solution)/shard_map/ppermute | solution.py:288
  47.8 1.6 %collective-permute-done.13.in3 = bf16[8,4608]{1,0:T(8,128)(2,1)S(1)} collective-permute-done((bf16[8,4608]{1,0:T(8,128)(2,1)S(1)}, bf16[8,4608]{1,0:T(8,128)(2,1)S(1)}, u32[]{:S(2)}, u32[]{:S(2)}) %collective-permute-start.13) | collective-permute-done | bytes 73760 | tf_op jit(solution)/shard_map/ppermute | solution.py:288
  49.4 0.7 %shard_map.152 = (bf16[2,4,512]{2,1,0:T(4,128)(2,1)}, bf16[8,4096]{1,0:T(8,128)(2,1)}) custom-call(f32[8,4608]{1,0:T(8,128)S(1)} %get-tuple-element.32.own, bf16[8,4608]{1,0:T(8,128)(2,1)S(1)} %collective-permute-done.11.in1, bf16[8,4608]{1,0:T(8,128)(2,1)S(1)} %collective-permute-done.12.in2, bf16[8,4608]{1,0:T(8,128)(2,1)S(1)} %collective-permute-done.13.in3), custom_call_target="tpu_custom_call" | custom-call | bytes 368640 | tf_op jit(solution)/shard_map/pallas_call | solution.py:275
  (44 shorter events, 2.9 us)
Async XLA Ops:
  0.6 5.4 %copy-start.7 = (bf16[2,2048,128]{2,1,0:T(8,128)(2,1)S(1)}, bf16[2,2048,128]{2,1,0:T(8,128)(2,1)}, u32[]{:S(2)}) copy-start(bf16[2,2048,128]{2,1,0:T(8,128)(2,1)} %values.9) | copy-start | bytes 3145732
  0.6 5.4 %copy-start.6 = (bf16[2,2048,128]{2,1,0:T(8,128)(2,1)S(1)}, bf16[2,2048,128]{2,1,0:T(8,128)(2,1)}, u32[]{:S(2)}) copy-start(bf16[2,2048,128]{2,1,0:T(8,128)(2,1)} %keys.9) | copy-start | bytes 3145732
  0.7 5.4 %copy-start = (bf16[512,4096]{1,0:T(8,128)(2,1)S(1)}, bf16[512,4096]{1,0:T(8,128)(2,1)}, u32[]{:S(2)}) copy-start(bf16[512,4096]{1,0:T(8,128)(2,1)} %w_out.5) | copy-start | bytes 12582916
  0.7 5.4 %copy-start.3 = (bf16[4096,128]{1,0:T(8,128)(2,1)S(1)}, bf16[4096,128]{1,0:T(8,128)(2,1)}, u32[]{:S(2)}) copy-start(bf16[4096,128]{1,0:T(8,128)(2,1)} %w_value.3) | copy-start | bytes 3145732
  0.7 5.4 %copy-start.2 = (bf16[4096,128]{1,0:T(8,128)(2,1)S(1)}, bf16[4096,128]{1,0:T(8,128)(2,1)}, u32[]{:S(2)}) copy-start(bf16[4096,128]{1,0:T(8,128)(2,1)} %w_key.3) | copy-start | bytes 3145732
  0.7 5.4 %copy-start.1 = (bf16[4096,512]{1,0:T(8,128)(2,1)S(1)}, bf16[4096,512]{1,0:T(8,128)(2,1)}, u32[]{:S(2)}) copy-start(bf16[4096,512]{1,0:T(8,128)(2,1)} %w_query.3) | copy-start | bytes 12582916
  0.7 5.4 %copy-start.5 = (bf16[128]{0:T(256)(128)(2,1)S(1)}, bf16[128]{0:T(256)(128)(2,1)}, u32[]{:S(2)}) copy-start(bf16[128]{0:T(256)(128)(2,1)} %param.18) | copy-start | bytes 772
  0.7 5.4 %copy-start.4 = (bf16[128]{0:T(256)(128)(2,1)S(1)}, bf16[128]{0:T(256)(128)(2,1)}, u32[]{:S(2)}) copy-start(bf16[128]{0:T(256)(128)(2,1)} %param.17) | copy-start | bytes 772
  1.7 4.5 %copy-start.10 = (bf16[2,4096]{1,0:T(2,128)(2,1)S(1)}, bf16[2,4096]{1,0:T(2,128)(2,1)}, u32[]{:S(2)}) copy-start(bf16[2,4096]{1,0:T(2,128)(2,1)} %embed.1) | copy-start | bytes 49156
  1.7 4.5 %copy-start.11 = (s32[8]{0:T(128)S(1)}, s32[8]{0:T(128)}, u32[]{:S(2)}) copy-start(s32[8]{0:T(128)} %lengths.9) | copy-start | bytes 100
  1.7 7.6 %collective-permute-start.2 = (bf16[8,4096]{1,0:T(8,128)(2,1)S(1)}, bf16[8,4096]{1,0:T(8,128)(2,1)S(1)}, u32[]{:S(2)}, u32[]{:S(2)}) collective-permute-start(bf16[8,4096]{1,0:T(8,128)(2,1)S(1)} %shard_map.140.rows0), channel_id=1, source_target_pairs={{0,48},{8,56},{16,32},{24,40},{32,16},{40,24},{48,0},{56,8},{1,49}... | collective-permute-start | bytes 196616 | tf_op jit(solution)/shard_map/ppermute | solution.py:288
  5.4 4.7 %collective-permute-start.1 = (bf16[8,4096]{1,0:T(8,128)(2,1)S(1)}, bf16[8,4096]{1,0:T(8,128)(2,1)S(1)}, u32[]{:S(2)}, u32[]{:S(2)}) collective-permute-start(bf16[8,4096]{1,0:T(8,128)(2,1)S(1)} %shard_map.140.rows0), channel_id=1, source_target_pairs={{0,32},{8,40},{16,48},{24,56},{32,0},{40,8},{48,16},{56,24},{1,33}... | collective-permute-start | bytes 196616 | tf_op jit(solution)/shard_map/ppermute | solution.py:288
  5.7 4.4 %collective-permute-start = (bf16[8,4096]{1,0:T(8,128)(2,1)S(1)}, bf16[8,4096]{1,0:T(8,128)(2,1)S(1)}, u32[]{:S(2)}, u32[]{:S(2)}) collective-permute-start(bf16[8,4096]{1,0:T(8,128)(2,1)S(1)} %shard_map.140.rows0), channel_id=1, source_target_pairs={{0,16},{8,24},{16,0},{24,8},{32,48},{40,56},{48,32},{56,40},{1,17}... | collective-permute-start | bytes 196616 | tf_op jit(solution)/shard_map/ppermute | solution.py:288
  10.3 3.6 %collective-permute-start.3 = (bf16[4,8,4096]{2,1,0:T(8,128)(2,1)S(1)}, bf16[4,8,4096]{2,1,0:T(8,128)(2,1)S(1)}, u32[]{:S(2)}, u32[]{:S(2)}) collective-permute-start(bf16[4,8,4096]{2,1,0:T(8,128)(2,1)S(1)} %get-tuple-element.21.mine), channel_id=1, source_target_pairs={{0,8},{8,0},{16,24},{24,16},{32,40},{40,32},{48,56},{56,48},{1,9},... | collective-permute-start | bytes 786440 | tf_op jit(solution)/shard_map/ppermute | solution.py:288
  15.1 6.3 %collective-permute-start.6 = (bf16[64,512]{1,0:T(8,128)(2,1)S(1)}, bf16[64,512]{1,0:T(8,128)(2,1)S(1)}, u32[]{:S(2)}, u32[]{:S(2)}) collective-permute-start(bf16[64,512]{1,0:T(8,128)(2,1)S(1)} %get-tuple-element.26._.query), channel_id=1, source_target_pairs={{0,192},{64,128},{128,64},{192,0},{1,193},{65,129},{129,65},{193,1... | collective-permute-start | bytes 196616 | tf_op jit(solution)/shard_map/ppermute | solution.py:288
  19.3 4.9 %collective-permute-start.5 = (bf16[64,512]{1,0:T(8,128)(2,1)S(1)}, bf16[64,512]{1,0:T(8,128)(2,1)S(1)}, u32[]{:S(2)}, u32[]{:S(2)}) collective-permute-start(bf16[64,512]{1,0:T(8,128)(2,1)S(1)} %get-tuple-element.26._.query), channel_id=1, source_target_pairs={{0,128},{64,192},{128,0},{192,64},{1,129},{65,193},{129,1},{193,65... | collective-permute-start | bytes 196616 | tf_op jit(solution)/shard_map/ppermute | solution.py:288
  19.3 10.6 %collective-permute-start.4 = (bf16[64,512]{1,0:T(8,128)(2,1)S(1)}, bf16[64,512]{1,0:T(8,128)(2,1)S(1)}, u32[]{:S(2)}, u32[]{:S(2)}) collective-permute-start(bf16[64,512]{1,0:T(8,128)(2,1)S(1)} %get-tuple-element.26._.query), channel_id=1, source_target_pairs={{0,64},{64,0},{128,192},{192,128},{1,65},{65,1},{129,193},{193,129... | collective-permute-start | bytes 196616 | tf_op jit(solution)/shard_map/ppermute | solution.py:288
  23.7 3.4 %collective-permute-start.7 = (bf16[64,640]{1,0:T(8,128)(2,1)S(1)}, bf16[64,640]{1,0:T(8,128)(2,1)S(1)}, u32[]{:S(2)}, u32[]{:S(2)}) collective-permute-start(bf16[64,640]{1,0:T(8,128)(2,1)S(1)} %shard_map.144._), channel_id=1, source_target_pairs={{0,64},{64,0},{128,192},{192,128},{1,65},{65,1},{129,193},{193,129... | collective-permute-start | bytes 245768 | tf_op jit(solution)/shard_map/ppermute | solution.py:288
  27.4 8.3 %collective-permute-start.9 = (bf16[64,640]{1,0:T(8,128)(2,1)S(1)}, bf16[64,640]{1,0:T(8,128)(2,1)S(1)}, u32[]{:S(2)}, u32[]{:S(2)}) collective-permute-start(bf16[64,640]{1,0:T(8,128)(2,1)S(1)} %shard_map.146._), channel_id=1, source_target_pairs={{0,128},{64,192},{128,0},{192,64},{1,129},{65,193},{129,1},{193,65... | collective-permute-start | bytes 245768 | tf_op jit(solution)/shard_map/ppermute | solution.py:288
  32.2 3.5 %collective-permute-start.8 = (bf16[64,640]{1,0:T(8,128)(2,1)S(1)}, bf16[64,640]{1,0:T(8,128)(2,1)S(1)}, u32[]{:S(2)}, u32[]{:S(2)}) collective-permute-start(bf16[64,640]{1,0:T(8,128)(2,1)S(1)} %shard_map.147._), channel_id=1, source_target_pairs={{0,64},{64,0},{128,192},{192,128},{1,65},{65,1},{129,193},{193,129... | collective-permute-start | bytes 245768 | tf_op jit(solution)/shard_map/ppermute | solution.py:288
  36.7 5.1 %collective-permute-start.10 = (bf16[4,8,4608]{2,1,0:T(8,128)(2,1)S(1)}, bf16[4,8,4608]{2,1,0:T(8,128)(2,1)S(1)}, u32[]{:S(2)}, u32[]{:S(2)}) collective-permute-start(bf16[4,8,4608]{2,1,0:T(8,128)(2,1)S(1)} %get-tuple-element.31), channel_id=1, source_target_pairs={{0,8},{8,0},{16,24},{24,16},{32,40},{40,32},{48,56},{56,48},{1,9},... | collective-permute-start | bytes 884744 | tf_op jit(solution)/shard_map/ppermute | solution.py:288
  41.9 3.9 %collective-permute-start.11 = (bf16[8,4608]{1,0:T(8,128)(2,1)S(1)}, bf16[8,4608]{1,0:T(8,128)(2,1)S(1)}, u32[]{:S(2)}, u32[]{:S(2)}) collective-permute-start(bf16[8,4608]{1,0:T(8,128)(2,1)S(1)} %get-tuple-element.33), channel_id=1, source_target_pairs={{0,16},{8,24},{16,0},{24,8},{32,48},{40,56},{48,32},{56,40},{1,17}... | collective-permute-start | bytes 221192 | tf_op jit(solution)/shard_map/ppermute | solution.py:288
  42.2 5.6 %collective-permute-start.12 = (bf16[8,4608]{1,0:T(8,128)(2,1)S(1)}, bf16[8,4608]{1,0:T(8,128)(2,1)S(1)}, u32[]{:S(2)}, u32[]{:S(2)}) collective-permute-start(bf16[8,4608]{1,0:T(8,128)(2,1)S(1)} %get-tuple-element.34), channel_id=1, source_target_pairs={{0,32},{8,40},{16,48},{24,56},{32,0},{40,8},{48,16},{56,24},{1,33}... | collective-permute-start | bytes 221192 | tf_op jit(solution)/shard_map/ppermute | solution.py:288
  44.5 4.9 %collective-permute-start.13 = (bf16[8,4608]{1,0:T(8,128)(2,1)S(1)}, bf16[8,4608]{1,0:T(8,128)(2,1)S(1)}, u32[]{:S(2)}, u32[]{:S(2)}) collective-permute-start(bf16[8,4608]{1,0:T(8,128)(2,1)S(1)} %get-tuple-element.35), channel_id=1, source_target_pairs={{0,48},{8,56},{16,32},{24,40},{32,16},{40,24},{48,0},{56,8},{1,49}... | collective-permute-start | bytes 221192 | tf_op jit(solution)/shard_map/ppermute | solution.py:288
  (3 other events, 9.8 us)

commit v4 on v3

--- a/solution.py
+++ b/solution.py
@@ -16,6 +16,12 @@
 SCALE2 = math.log2(math.e) / math.sqrt(HEAD)
 NEG = -1e30
 CHUNK = 1024
+Y_ORDER = (1, 3, 2)
+STEPS_Z = (
+    ((3, 0, 1, 2), (1, 2, 3, 0)),
+    ((2, 3, 0, 1), (2, 3, 0, 1)),
+    ((1, 2, 3, 0), (3, 0, 1, 2)),
+)
 F32 = jnp.float32
 BF16 = jnp.bfloat16
 MIB = 1024 * 1024
@@ -121,7 +127,7 @@
     own = lax.axis_index("tensor")
     for k in range(4):
         for flipped, ref in ((0, mine), (1, other)):
-            at = pl.multiple_of((own ^ (2 * k + flipped)) * 8, 8)
+            at = pl.multiple_of((2 * ((own // 2 + 4 - k) % 4) + (own % 2 ^ flipped)) * 8, 8)
             normed_f32[pl.ds(at, 8), :] = ref[k].astype(F32)
     normed = normed_f32[...].astype(BF16)
     cos = cosine[...]
@@ -139,10 +145,14 @@
 
 
 def attend_kernel(
-    flip, lengths, query, keys, values, tail_keys, tail_values, _, out
+    step, lengths, query, keys, values, tail_keys, tail_values, _, out
 ):
     path = lax.axis_index("path")
-    block = path ^ flip
+    core = lax.axis_index("tensor") % 2
+    block = jnp.int32(0)
+    for c, table in enumerate(STEPS_Z[step] if step >= 0 else (range(4),) * 2):
+        for p, b in enumerate(table):
+            block = jnp.where((path == p) & (core == c), b, block)
     rows = out.shape[0]
     q = jnp.concatenate([query[:, h * HEAD : (h + 1) * HEAD] for h in range(GROUP)], axis=0)
     chunks = [(i, c) for i in range(2) for c in range(0, keys.shape[1], CHUNK)]
@@ -213,16 +223,6 @@
     return part[:, :width].astype(F32), stats[:, :GROUP], total
 
 
-def merge_kernel(part, received, out):
-    rows = part.shape[0]
-    mixes, peak, total = merge([read_part(part[...]), read_part(received[...])])
-    mix = jnp.concatenate(mixes, axis=0)
-    peak, total = (
-        jnp.concatenate([x[:, h : h + 1] for h in range(GROUP)], axis=0) for x in (peak, total)
-    )
-    write_part(out, rows, mix, peak, total)
-
-
 def project_half(attn, which, w_out, dterms, ref):
     width = w_out.shape[1]
     lhs = jnp.concatenate(
@@ -234,9 +234,9 @@
         ref[y, :, width:] = dterms[2 * y + which].astype(ref.dtype)
 
 
-def send_kernel(own_part, part1, part2, w_out, dterms, send, attn):
+def send_kernel(own_part, part1, part2, part3, w_out, dterms, send, attn):
     core = lax.axis_index("tensor") % 2
-    parts = (own_part[...], part1[...], part2[...])
+    parts = (own_part[...], part1[...], part2[...], part3[...])
     mixes, _, total = merge([read_part(x) for x in parts])
     for h in range(GROUP):
         attn[:, h * HEAD : (h + 1) * HEAD] = mixes[h] / total[:, h : h + 1]
@@ -250,7 +250,7 @@
 def fold_kernel(keep, received, own_out, out1, out2, out3):
     at = lax.axis_index("tensor") // 2
     for k, ref in enumerate((own_out, out1, out2, out3)):
-        block = at ^ k
+        block = (at + k) % 4
         ref[...] = (keep[block] + received[block].astype(F32)).astype(ref.dtype)
 
 
@@ -288,6 +288,24 @@
     return lax.ppermute(x, axis, [(i, i ^ k) for i in range(size)])
 
 
+def shift(x, axis, size, k):
+    return lax.ppermute(x, axis, [(i, (i + k) % size) for i in range(size)])
+
+
+def routes(step):
+    return [
+        (p * 8 + t, STEPS_Z[step][t % 2][p] * 8 + t) for p in range(4) for t in range(8)
+    ]
+
+
+def fetch(x, step):
+    return lax.ppermute(x, ("path", "tensor"), [(b, a) for a, b in routes(step)])
+
+
+def give_back(x, step):
+    return lax.ppermute(x, ("path", "tensor"), routes(step))
+
+
 def body(
     decode_in,
     path_embed,
@@ -310,7 +328,10 @@
     key_gain = key_norm_gain.reshape(1, -1)
 
     (own_rows,) = call(hold_kernel, [(summary_in.shape, BF16)], (summary_in,), flops=10**10)
-    across = [own_rows] + [flip(own_rows, "tensor", 8, k) for k in (2, 4, 6)]
+    across = {0: own_rows}
+    for k in Y_ORDER:
+        across[k] = shift(own_rows, "tensor", 8, 2 * k)
+    across = [across[k] for k in range(4)]
 
     dterms, dkey, dvalue, cosine, sine = call(
         decode_kernel,
@@ -336,9 +357,9 @@
         limit=24,
         flops=2 * 64 * 4096 * 768,
     )
-    queries = {0: query}
-    for k in (3, 2, 1):
-        queries[k] = flip(query, "path", 4, k)
+    queries = {-1: query}
+    for n in range(3):
+        queries[n] = fetch(query, n)
 
     def attend(k, after):
         (part,) = call(
@@ -351,20 +372,17 @@
         )
         return part
 
-    part3 = attend(3, query)
-    received3 = flip(part3, "path", 4, 1)
-    part2 = attend(2, part3)
-    (merged2,) = call(
-        merge_kernel, [(part2.shape, BF16)], (part2, received3), limit=24, flops=10**8
-    )
-    received2 = flip(merged2, "path", 4, 2)
-    part1 = attend(1, merged2)
-    received1 = flip(part1, "path", 4, 1)
-    own_part = attend(0, part1)
+    parts = []
+    last = query
+    for n in range(3):
+        last = attend(n, last)
+        parts.append(give_back(last, n))
+    parts.append(attend(-1, last))
+
     send, attn = call(
         send_kernel,
         [((4, 8, width + width // 8), BF16), ((rows, GROUP * HEAD), F32)],
-        (own_part, received1, received2, w_out, dterms),
+        (*parts, w_out, dterms),
         limit=24,
         flops=64 * 512 * 4096,
     )
@@ -381,13 +399,12 @@
         [((8, width + width // 8), F32)] + [((8, width + width // 8), BF16)] * 3,
         (keep, received),
     )
-    in1 = flip(out1, "tensor", 8, 2)
-    in2 = flip(out2, "tensor", 8, 4)
-    in3 = flip(out3, "tensor", 8, 6)
+    outs = {1: out1, 2: out2, 3: out3}
+    ins = {k: shift(outs[k], "tensor", 8, 2 * k) for k in Y_ORDER}
     decode_out, summary_out = call(
         final_kernel,
         [((2, STEPS, width // 8), BF16), ((8, width), BF16)],
-        (own, in1, in2, in3),
+        (own, ins[1], ins[2], ins[3]),
     )
     return (decode_out, summary_out)
 

time: 50.3 us -> 48.9 us (0.972)
  waiting for transfers between devices: 8.82 us -> 7.04 us
  starting transfers between devices: 22.6 us -> 23.4 us
    ppermute x0 -> x12, starting transfers between devices: none -> 18.6 us  [the longest x6 7.87 us: shift(): return lax.ppermute(x, axis, [(i, (i + k) % size) for i in range(size)])]
    ppermute x14 -> x2, starting transfers between devices: 22.6 us -> 4.77 us  [flip(): return lax.ppermute(x, axis, [(i, i ^ k) for i in range(size)])]
    ppermute x14 -> x2, waiting for transfers between devices: 8.82 us -> 1.56 us  [flip(): return lax.ppermute(x, axis, [(i, i ^ k) for i in range(size)])]
    ppermute x0 -> x12, waiting for transfers between devices: none -> 5.49 us  [the longest x6 4.52 us: shift(): return lax.ppermute(x, axis, [(i, (i + k) % size) for i in range(size)])]
    pallas_call x13 -> x12, Pallas kernels: 16.7 us -> 16.4 us  [call(): pl.pallas_call(kernel, out_shape=outs, in_specs=specs, out_specs=tuple((p...]
  transfers between devices with their start and end apart: 14 -> 14, of which waited for: 9 -> 6; matrix products, arithmetic and copies ran while one was open for 0% -> 0% of each run, Pallas kernels for 27% -> 27%
where the time goes in v4:
time: 48.9 us; the launch traced here: 48.8 us
  starting transfers between devices  23.4 us (48%)
  Pallas kernels  16.4 us (34%)
  waiting for transfers between devices  7.04 us (14%)
  local copies, waits for them, and re-layouts  1.04 us (2%)
  between operations  0.9 us (2%)
    pallas_call x12, Pallas kernels, call(): pl.pallas_call(kernel, out_shape=outs, in_specs=specs, out_specs=tuple((p...  16.4 us
    ppermute x6, starting transfers between devices, shift(): return lax.ppermute(x, axis, [(i, (i + k) % size) for i in range(size)])  7.87 us
    ppermute x3, starting transfers between devices, give_back(): return lax.ppermute(x, ('path', 'tensor'), routes(step))  5.94 us
    ppermute x3, starting transfers between devices, fetch(): lax.ppermute(x, ('path', 'tensor'), [(b, a) for a, b in routes(step)])  4.79 us
    ppermute x2, starting transfers between devices, flip(): return lax.ppermute(x, axis, [(i, i ^ k) for i in range(size)])  4.77 us
    ppermute x6, waiting for transfers between devices, shift(): return lax.ppermute(x, axis, [(i, (i + k) % size) for i in range(size)])  4.52 us
    ppermute x2, waiting for transfers between devices, flip(): return lax.ppermute(x, axis, [(i, i ^ k) for i in range(size)])  1.56 us
    unnamed x26, local copies, waits for them, and re-layouts  1.03 us
  transfers between devices with their start and end apart: 14, of which 6 were waited for; matrix products, arithmetic and copies ran while one was open for 0% of the time, Pallas kernels for 27%

profile of v4, /device:TPU:1, one launch (start us, length us, event | category | flops | bytes accessed | tf_op | source)
XLA Modules:
  0.0 48.8 jit_solution(13412700696978743068)
XLA Ops:
  0.7 1.0 %copy-done.8 = bf16[8,4096]{1,0:T(8,128)(2,1)S(1)} copy-done((bf16[8,4096]{1,0:T(8,128)(2,1)S(1)}, bf16[8,4096]{1,0:T(8,128)(2,1)}, u32[]{:S(2)}) %copy-start.8) | copy-done | bytes 65560
  1.7 3.6 %collective-permute-start.2 = (bf16[8,4096]{1,0:T(8,128)(2,1)S(1)}, bf16[8,4096]{1,0:T(8,128)(2,1)S(1)}, u32[]{:S(2)}, u32[]{:S(2)}) collective-permute-start(bf16[8,4096]{1,0:T(8,128)(2,1)S(1)} %shard_map.140.rows0), channel_id=1, source_target_pairs={{0,48},{8,56},{16,0},{24,8},{32,16},{40,24},{48,32},{56,40},{1,49}... | collective-permute-start | bytes 196616 | tf_op jit(solution)/shard_map/ppermute | solution.py:292
  5.7 0.7 %collective-permute-start = (bf16[8,4096]{1,0:T(8,128)(2,1)S(1)}, bf16[8,4096]{1,0:T(8,128)(2,1)S(1)}, u32[]{:S(2)}, u32[]{:S(2)}) collective-permute-start(bf16[8,4096]{1,0:T(8,128)(2,1)S(1)} %shard_map.140.rows0), channel_id=1, source_target_pairs={{0,16},{8,24},{16,32},{24,40},{32,48},{40,56},{48,0},{56,8},{1,17}... | collective-permute-start | bytes 196616 | tf_op jit(solution)/shard_map/ppermute | solution.py:292
  6.5 3.1 %shard_map.141 = (bf16[8,8,512]{2,1,0:T(8,128)(2,1)S(1)}, f32[8,128]{1,0:T(8,128)S(1)}, f32[8,128]{1,0:T(8,128)S(1)}, f32[64,128]{1,0:T(8,128)S(1)}, f32[64,128]{1,0:T(8,128)S(1)}) custom-call(s32[8]{0:T(128)S(1)} %copy-done.11, bf16[2,4,4096]{2,1,0:T(4,128)(2,1)S(1)} %copy-done.9, bf16[2,4096]{1,0:T(2,128)(2,1)S(1)} %copy-done.10, ...), custom_call_target="tpu_custom_call" | custom-call | flops 6000000000 | bytes 12673568 | tf_op jit(solution)/shard_map/pallas_call | solution.py:275
  10.1 0.6 %collective-permute-done.rows1 = bf16[8,4096]{1,0:T(8,128)(2,1)S(1)} collective-permute-done((bf16[8,4096]{1,0:T(8,128)(2,1)S(1)}, bf16[8,4096]{1,0:T(8,128)(2,1)S(1)}, u32[]{:S(2)}, u32[]{:S(2)}) %collective-permute-start) | collective-permute-done | bytes 65568 | tf_op jit(solution)/shard_map/ppermute | solution.py:292
  10.9 2.2 %collective-permute-start.3 = (bf16[4,8,4096]{2,1,0:T(8,128)(2,1)S(1)}, bf16[4,8,4096]{2,1,0:T(8,128)(2,1)S(1)}, u32[]{:S(2)}, u32[]{:S(2)}) collective-permute-start(bf16[4,8,4096]{2,1,0:T(8,128)(2,1)S(1)} %get-tuple-element.21.mine), channel_id=1, source_target_pairs={{0,8},{8,0},{16,24},{24,16},{32,40},{40,32},{48,56},{56,48},{1,9},... | collective-permute-start | bytes 786440 | tf_op jit(solution)/shard_map/ppermute | solution.py:288
  13.1 1.2 %collective-permute-done.3.other = bf16[4,8,4096]{2,1,0:T(8,128)(2,1)S(1)} collective-permute-done((bf16[4,8,4096]{2,1,0:T(8,128)(2,1)S(1)}, bf16[4,8,4096]{2,1,0:T(8,128)(2,1)S(1)}, u32[]{:S(2)}, u32[]{:S(2)}) %collective-permute-start.3) | collective-permute-done | bytes 262176 | tf_op jit(solution)/shard_map/ppermute | solution.py:288
  14.2 1.3 %shard_map.143 = (bf16[64,512]{1,0:T(8,128)(2,1)S(1)}, bf16[128,128]{1,0:T(8,128)(2,1)S(1)}, bf16[128,128]{1,0:T(8,128)(2,1)S(1)}) custom-call(bf16[4,8,4096]{2,1,0:T(8,128)(2,1)S(1)} %get-tuple-element.21.mine, bf16[4,8,4096]{2,1,0:T(8,128)(2,1)S(1)} %collective-permute-done.3.other, bf16[1,128]{1,0:T(2,128)(2,1)S(1)} %bitcast.3, ...), custom_call_target="tpu_custom_call" | custom-call | flops 402653184 | bytes 6889984 | tf_op jit(solution)/shard_map/pallas_call | solution.py:275
  15.5 4.4 %collective-permute-start.4 = (bf16[64,512]{1,0:T(8,128)(2,1)S(1)}, bf16[64,512]{1,0:T(8,128)(2,1)S(1)}, u32[]{:S(2)}, u32[]{:S(2)}) collective-permute-start(bf16[64,512]{1,0:T(8,128)(2,1)S(1)} %get-tuple-element.26._.query), channel_id=1, source_target_pairs={{192,0},{72,8},{208,16},{88,24},{224,32},{104,40},{240,48},{120,56... | collective-permute-start | bytes 196616 | tf_op jit(solution)/shard_map/ppermute | solution.py:302
  20.3 1.0 %collective-permute-done.4.query = bf16[64,512]{1,0:T(8,128)(2,1)S(1)} collective-permute-done((bf16[64,512]{1,0:T(8,128)(2,1)S(1)}, bf16[64,512]{1,0:T(8,128)(2,1)S(1)}, u32[]{:S(2)}, u32[]{:S(2)}) %collective-permute-start.4) | collective-permute-done | bytes 65568 | tf_op jit(solution)/shard_map/ppermute | solution.py:302
  21.3 2.3 %shard_map.144._ = bf16[64,640]{1,0:T(8,128)(2,1)S(1)} custom-call(s32[8]{0:T(128)S(1)} %copy-done.11, bf16[64,512]{1,0:T(8,128)(2,1)S(1)} %collective-permute-done.4.query, bf16[2,2048,128]{2,1,0:T(8,128)(2,1)S(1)} %copy-done.6, bf16[2,2048,128]{2,1,0:T(8,128)(2,1)S(1)} %copy-done.7, bf16[128,128]{1,0:T(8,128)(2,1)S(1)} %get-tuple-element.27.tail_keys, ...), custom_call_target="tpu_custom_call" | custom-call | flops 3000000000 | bytes 2293792 | tf_op jit(solution)/shard_map/pallas_call | solution.py:275
  23.6 2.5 %collective-permute-start.5 = (bf16[64,640]{1,0:T(8,128)(2,1)S(1)}, bf16[64,640]{1,0:T(8,128)(2,1)S(1)}, u32[]{:S(2)}, u32[]{:S(2)}) collective-permute-start(bf16[64,640]{1,0:T(8,128)(2,1)S(1)} %shard_map.144._), channel_id=1, source_target_pairs={{0,192},{8,72},{16,208},{24,88},{32,224},{40,104},{48,240},{56,120... | collective-permute-start | bytes 245768 | tf_op jit(solution)/shard_map/ppermute | solution.py:306
  26.1 2.3 %shard_map.145._ = bf16[64,640]{1,0:T(8,128)(2,1)S(1)} custom-call(s32[8]{0:T(128)S(1)} %copy-done.11, bf16[64,512]{1,0:T(8,128)(2,1)S(1)} %collective-permute-done.6.query, bf16[2,2048,128]{2,1,0:T(8,128)(2,1)S(1)} %copy-done.6, bf16[2,2048,128]{2,1,0:T(8,128)(2,1)S(1)} %copy-done.7, bf16[128,128]{1,0:T(8,128)(2,1)S(1)} %get-tuple-element.27.tail_keys, ...), custom_call_target="tpu_custom_call" | custom-call | flops 3000000000 | bytes 2310176 | tf_op jit(solution)/shard_map/pallas_call | solution.py:275
  28.4 1.7 %collective-permute-start.7 = (bf16[64,640]{1,0:T(8,128)(2,1)S(1)}, bf16[64,640]{1,0:T(8,128)(2,1)S(1)}, u32[]{:S(2)}, u32[]{:S(2)}) collective-permute-start(bf16[64,640]{1,0:T(8,128)(2,1)S(1)} %shard_map.145._), channel_id=1, source_target_pairs={{0,128},{8,136},{16,144},{24,152},{32,160},{40,168},{48,176},{56,1... | collective-permute-start | bytes 245768 | tf_op jit(solution)/shard_map/ppermute | solution.py:306
  30.1 2.3 %shard_map.146._ = bf16[64,640]{1,0:T(8,128)(2,1)S(1)} custom-call(s32[8]{0:T(128)S(1)} %copy-done.11, bf16[64,512]{1,0:T(8,128)(2,1)S(1)} %collective-permute-done.8.query, bf16[2,2048,128]{2,1,0:T(8,128)(2,1)S(1)} %copy-done.6, bf16[2,2048,128]{2,1,0:T(8,128)(2,1)S(1)} %copy-done.7, bf16[128,128]{1,0:T(8,128)(2,1)S(1)} %get-tuple-element.27.tail_keys, ...), custom_call_target="tpu_custom_call" | custom-call | flops 3000000000 | bytes 2310176 | tf_op jit(solution)/shard_map/pallas_call | solution.py:275
  32.5 1.7 %collective-permute-start.9 = (bf16[64,640]{1,0:T(8,128)(2,1)S(1)}, bf16[64,640]{1,0:T(8,128)(2,1)S(1)}, u32[]{:S(2)}, u32[]{:S(2)}) collective-permute-start(bf16[64,640]{1,0:T(8,128)(2,1)S(1)} %shard_map.146._), channel_id=1, source_target_pairs={{0,64},{8,200},{16,80},{24,216},{32,96},{40,232},{48,112},{56,248}... | collective-permute-start | bytes 245768 | tf_op jit(solution)/shard_map/ppermute | solution.py:306
  34.2 2.3 %shard_map.147.part3 = bf16[64,640]{1,0:T(8,128)(2,1)S(1)} custom-call(s32[8]{0:T(128)S(1)} %copy-done.11, bf16[64,512]{1,0:T(8,128)(2,1)S(1)} %get-tuple-element.26._.query, bf16[2,2048,128]{2,1,0:T(8,128)(2,1)S(1)} %copy-done.6, bf16[2,2048,128]{2,1,0:T(8,128)(2,1)S(1)} %copy-done.7, bf16[128,128]{1,0:T(8,128)(2,1)S(1)} %get-tuple-element.27.tail_keys, ...), custom_call_target="tpu_custom_call" | custom-call | flops 3000000000 | bytes 2310176 | tf_op jit(solution)/shard_map/pallas_call | solution.py:275
  36.5 1.1 %shard_map.148 = (bf16[4,8,4608]{2,1,0:T(8,128)(2,1)S(1)}, f32[64,512]{1,0:T(8,128)S(1)}) custom-call(bf16[64,640]{1,0:T(8,128)(2,1)S(1)} %collective-permute-done.5.own_part, bf16[64,640]{1,0:T(8,128)(2,1)S(1)} %collective-permute-done.7.part1, bf16[64,640]{1,0:T(8,128)(2,1)S(1)} %collective-permute-done.9.part2, bf16[64,640]{1,0:T(8,128)(2,1)S(1)} %shard_map.147.part3, ...), custom_call_target="tpu_custom_call" | custom-call | flops 134217728 | bytes 4587520 | tf_op jit(solution)/shard_map/pallas_call | solution.py:275
  37.6 2.6 %collective-permute-start.10 = (bf16[4,8,4608]{2,1,0:T(8,128)(2,1)S(1)}, bf16[4,8,4608]{2,1,0:T(8,128)(2,1)S(1)}, u32[]{:S(2)}, u32[]{:S(2)}) collective-permute-start(bf16[4,8,4608]{2,1,0:T(8,128)(2,1)S(1)} %get-tuple-element.31), channel_id=1, source_target_pairs={{0,8},{8,0},{16,24},{24,16},{32,40},{40,32},{48,56},{56,48},{1,9},... | collective-permute-start | bytes 884744 | tf_op jit(solution)/shard_map/ppermute | solution.py:288
  40.2 0.8 %shard_map.149.keep = f32[4,8,4608]{2,1,0:T(8,128)S(1)} custom-call(f32[64,512]{1,0:T(8,128)S(1)} %get-tuple-element.30.attn, bf16[512,4096]{1,0:T(8,128)(2,1)S(1)} %copy-done, bf16[8,8,512]{2,1,0:T(8,128)(2,1)S(1)} %get-tuple-element.29.dterms), custom_call_target="tpu_custom_call" | custom-call | flops 134217728 | bytes 4390912 | tf_op jit(solution)/shard_map/pallas_call | solution.py:275
  41.6 1.5 %collective-permute-start.12 = (bf16[8,4608]{1,0:T(8,128)(2,1)S(1)}, bf16[8,4608]{1,0:T(8,128)(2,1)S(1)}, u32[]{:S(2)}, u32[]{:S(2)}) collective-permute-start(bf16[8,4608]{1,0:T(8,128)(2,1)S(1)} %get-tuple-element.34), channel_id=1, source_target_pairs={{0,32},{8,40},{16,48},{24,56},{32,0},{40,8},{48,16},{56,24},{1,33}... | collective-permute-start | bytes 221192 | tf_op jit(solution)/shard_map/ppermute | solution.py:292
  43.1 1.6 %collective-permute-start.13 = (bf16[8,4608]{1,0:T(8,128)(2,1)S(1)}, bf16[8,4608]{1,0:T(8,128)(2,1)S(1)}, u32[]{:S(2)}, u32[]{:S(2)}) collective-permute-start(bf16[8,4608]{1,0:T(8,128)(2,1)S(1)} %get-tuple-element.35), channel_id=1, source_target_pairs={{0,48},{8,56},{16,0},{24,8},{32,16},{40,24},{48,32},{56,40},{1,49}... | collective-permute-start | bytes 221192 | tf_op jit(solution)/shard_map/ppermute | solution.py:292
  44.7 3.5 %collective-permute-done.11.in1 = bf16[8,4608]{1,0:T(8,128)(2,1)S(1)} collective-permute-done((bf16[8,4608]{1,0:T(8,128)(2,1)S(1)}, bf16[8,4608]{1,0:T(8,128)(2,1)S(1)}, u32[]{:S(2)}, u32[]{:S(2)}) %collective-permute-start.11) | collective-permute-done | bytes 73760 | tf_op jit(solution)/shard_map/ppermute | solution.py:292
  48.1 0.7 %shard_map.151 = (bf16[2,4,512]{2,1,0:T(4,128)(2,1)}, bf16[8,4096]{1,0:T(8,128)(2,1)}) custom-call(f32[8,4608]{1,0:T(8,128)S(1)} %get-tuple-element.32.own, bf16[8,4608]{1,0:T(8,128)(2,1)S(1)} %collective-permute-done.11.in1, bf16[8,4608]{1,0:T(8,128)(2,1)S(1)} %collective-permute-done.12.in2, bf16[8,4608]{1,0:T(8,128)(2,1)S(1)} %collective-permute-done.13.in3), custom_call_target="tpu_custom_call" | custom-call | bytes 368640 | tf_op jit(solution)/shard_map/pallas_call | solution.py:275
  (43 shorter events, 1.9 us)
Async XLA Ops:
  0.6 5.8 %copy-start.7 = (bf16[2,2048,128]{2,1,0:T(8,128)(2,1)S(1)}, bf16[2,2048,128]{2,1,0:T(8,128)(2,1)}, u32[]{:S(2)}) copy-start(bf16[2,2048,128]{2,1,0:T(8,128)(2,1)} %values.9) | copy-start | bytes 3145732
  0.6 5.8 %copy-start.6 = (bf16[2,2048,128]{2,1,0:T(8,128)(2,1)S(1)}, bf16[2,2048,128]{2,1,0:T(8,128)(2,1)}, u32[]{:S(2)}) copy-start(bf16[2,2048,128]{2,1,0:T(8,128)(2,1)} %keys.9) | copy-start | bytes 3145732
  0.7 5.8 %copy-start = (bf16[512,4096]{1,0:T(8,128)(2,1)S(1)}, bf16[512,4096]{1,0:T(8,128)(2,1)}, u32[]{:S(2)}) copy-start(bf16[512,4096]{1,0:T(8,128)(2,1)} %w_out.5) | copy-start | bytes 12582916
  0.7 5.8 %copy-start.3 = (bf16[4096,128]{1,0:T(8,128)(2,1)S(1)}, bf16[4096,128]{1,0:T(8,128)(2,1)}, u32[]{:S(2)}) copy-start(bf16[4096,128]{1,0:T(8,128)(2,1)} %w_value.3) | copy-start | bytes 3145732
  0.7 5.8 %copy-start.2 = (bf16[4096,128]{1,0:T(8,128)(2,1)S(1)}, bf16[4096,128]{1,0:T(8,128)(2,1)}, u32[]{:S(2)}) copy-start(bf16[4096,128]{1,0:T(8,128)(2,1)} %w_key.3) | copy-start | bytes 3145732
  0.7 5.8 %copy-start.1 = (bf16[4096,512]{1,0:T(8,128)(2,1)S(1)}, bf16[4096,512]{1,0:T(8,128)(2,1)}, u32[]{:S(2)}) copy-start(bf16[4096,512]{1,0:T(8,128)(2,1)} %w_query.3) | copy-start | bytes 12582916
  0.7 5.8 %copy-start.5 = (bf16[128]{0:T(256)(128)(2,1)S(1)}, bf16[128]{0:T(256)(128)(2,1)}, u32[]{:S(2)}) copy-start(bf16[128]{0:T(256)(128)(2,1)} %param.18) | copy-start | bytes 772
  0.7 5.8 %copy-start.4 = (bf16[128]{0:T(256)(128)(2,1)S(1)}, bf16[128]{0:T(256)(128)(2,1)}, u32[]{:S(2)}) copy-start(bf16[128]{0:T(256)(128)(2,1)} %param.17) | copy-start | bytes 772
  1.7 4.8 %copy-start.10 = (bf16[2,4096]{1,0:T(2,128)(2,1)S(1)}, bf16[2,4096]{1,0:T(2,128)(2,1)}, u32[]{:S(2)}) copy-start(bf16[2,4096]{1,0:T(2,128)(2,1)} %embed.1) | copy-start | bytes 49156
  1.7 4.8 %copy-start.11 = (s32[8]{0:T(128)S(1)}, s32[8]{0:T(128)}, u32[]{:S(2)}) copy-start(s32[8]{0:T(128)} %lengths.9) | copy-start | bytes 100
  1.7 7.9 %collective-permute-start.2 = (bf16[8,4096]{1,0:T(8,128)(2,1)S(1)}, bf16[8,4096]{1,0:T(8,128)(2,1)S(1)}, u32[]{:S(2)}, u32[]{:S(2)}) collective-permute-start(bf16[8,4096]{1,0:T(8,128)(2,1)S(1)} %shard_map.140.rows0), channel_id=1, source_target_pairs={{0,48},{8,56},{16,0},{24,8},{32,16},{40,24},{48,32},{56,40},{1,49}... | collective-permute-start | bytes 196616 | tf_op jit(solution)/shard_map/ppermute | solution.py:292
  5.4 4.7 %collective-permute-start.1 = (bf16[8,4096]{1,0:T(8,128)(2,1)S(1)}, bf16[8,4096]{1,0:T(8,128)(2,1)S(1)}, u32[]{:S(2)}, u32[]{:S(2)}) collective-permute-start(bf16[8,4096]{1,0:T(8,128)(2,1)S(1)} %shard_map.140.rows0), channel_id=1, source_target_pairs={{0,32},{8,40},{16,48},{24,56},{32,0},{40,8},{48,16},{56,24},{1,33}... | collective-permute-start | bytes 196616 | tf_op jit(solution)/shard_map/ppermute | solution.py:292
  5.7 5.0 %collective-permute-start = (bf16[8,4096]{1,0:T(8,128)(2,1)S(1)}, bf16[8,4096]{1,0:T(8,128)(2,1)S(1)}, u32[]{:S(2)}, u32[]{:S(2)}) collective-permute-start(bf16[8,4096]{1,0:T(8,128)(2,1)S(1)} %shard_map.140.rows0), channel_id=1, source_target_pairs={{0,16},{8,24},{16,32},{24,40},{32,48},{40,56},{48,0},{56,8},{1,17}... | collective-permute-start | bytes 196616 | tf_op jit(solution)/shard_map/ppermute | solution.py:292
  10.9 3.4 %collective-permute-start.3 = (bf16[4,8,4096]{2,1,0:T(8,128)(2,1)S(1)}, bf16[4,8,4096]{2,1,0:T(8,128)(2,1)S(1)}, u32[]{:S(2)}, u32[]{:S(2)}) collective-permute-start(bf16[4,8,4096]{2,1,0:T(8,128)(2,1)S(1)} %get-tuple-element.21.mine), channel_id=1, source_target_pairs={{0,8},{8,0},{16,24},{24,16},{32,40},{40,32},{48,56},{56,48},{1,9},... | collective-permute-start | bytes 786440 | tf_op jit(solution)/shard_map/ppermute | solution.py:288
  15.5 5.8 %collective-permute-start.4 = (bf16[64,512]{1,0:T(8,128)(2,1)S(1)}, bf16[64,512]{1,0:T(8,128)(2,1)S(1)}, u32[]{:S(2)}, u32[]{:S(2)}) collective-permute-start(bf16[64,512]{1,0:T(8,128)(2,1)S(1)} %get-tuple-element.26._.query), channel_id=1, source_target_pairs={{192,0},{72,8},{208,16},{88,24},{224,32},{104,40},{240,48},{120,56... | collective-permute-start | bytes 196616 | tf_op jit(solution)/shard_map/ppermute | solution.py:302
  19.9 10.2 %collective-permute-start.8 = (bf16[64,512]{1,0:T(8,128)(2,1)S(1)}, bf16[64,512]{1,0:T(8,128)(2,1)S(1)}, u32[]{:S(2)}, u32[]{:S(2)}) collective-permute-start(bf16[64,512]{1,0:T(8,128)(2,1)S(1)} %get-tuple-element.26._.query), channel_id=1, source_target_pairs={{64,0},{200,8},{80,16},{216,24},{96,32},{232,40},{112,48},{248,56}... | collective-permute-start | bytes 196616 | tf_op jit(solution)/shard_map/ppermute | solution.py:302
  19.9 6.1 %collective-permute-start.6 = (bf16[64,512]{1,0:T(8,128)(2,1)S(1)}, bf16[64,512]{1,0:T(8,128)(2,1)S(1)}, u32[]{:S(2)}, u32[]{:S(2)}) collective-permute-start(bf16[64,512]{1,0:T(8,128)(2,1)S(1)} %get-tuple-element.26._.query), channel_id=1, source_target_pairs={{128,0},{136,8},{144,16},{152,24},{160,32},{168,40},{176,48},{184,... | collective-permute-start | bytes 196616 | tf_op jit(solution)/shard_map/ppermute | solution.py:302
  23.6 12.9 %collective-permute-start.5 = (bf16[64,640]{1,0:T(8,128)(2,1)S(1)}, bf16[64,640]{1,0:T(8,128)(2,1)S(1)}, u32[]{:S(2)}, u32[]{:S(2)}) collective-permute-start(bf16[64,640]{1,0:T(8,128)(2,1)S(1)} %shard_map.144._), channel_id=1, source_target_pairs={{0,192},{8,72},{16,208},{24,88},{32,224},{40,104},{48,240},{56,120... | collective-permute-start | bytes 245768 | tf_op jit(solution)/shard_map/ppermute | solution.py:306
  28.4 8.1 %collective-permute-start.7 = (bf16[64,640]{1,0:T(8,128)(2,1)S(1)}, bf16[64,640]{1,0:T(8,128)(2,1)S(1)}, u32[]{:S(2)}, u32[]{:S(2)}) collective-permute-start(bf16[64,640]{1,0:T(8,128)(2,1)S(1)} %shard_map.145._), channel_id=1, source_target_pairs={{0,128},{8,136},{16,144},{24,152},{32,160},{40,168},{48,176},{56,1... | collective-permute-start | bytes 245768 | tf_op jit(solution)/shard_map/ppermute | solution.py:306
  32.5 4.0 %collective-permute-start.9 = (bf16[64,640]{1,0:T(8,128)(2,1)S(1)}, bf16[64,640]{1,0:T(8,128)(2,1)S(1)}, u32[]{:S(2)}, u32[]{:S(2)}) collective-permute-start(bf16[64,640]{1,0:T(8,128)(2,1)S(1)} %shard_map.146._), channel_id=1, source_target_pairs={{0,64},{8,200},{16,80},{24,216},{32,96},{40,232},{48,112},{56,248}... | collective-permute-start | bytes 245768 | tf_op jit(solution)/shard_map/ppermute | solution.py:306
  37.6 3.8 %collective-permute-start.10 = (bf16[4,8,4608]{2,1,0:T(8,128)(2,1)S(1)}, bf16[4,8,4608]{2,1,0:T(8,128)(2,1)S(1)}, u32[]{:S(2)}, u32[]{:S(2)}) collective-permute-start(bf16[4,8,4608]{2,1,0:T(8,128)(2,1)S(1)} %get-tuple-element.31), channel_id=1, source_target_pairs={{0,8},{8,0},{16,24},{24,16},{32,40},{40,32},{48,56},{56,48},{1,9},... | collective-permute-start | bytes 884744 | tf_op jit(solution)/shard_map/ppermute | solution.py:288
  41.5 6.7 %collective-permute-start.11 = (bf16[8,4608]{1,0:T(8,128)(2,1)S(1)}, bf16[8,4608]{1,0:T(8,128)(2,1)S(1)}, u32[]{:S(2)}, u32[]{:S(2)}) collective-permute-start(bf16[8,4608]{1,0:T(8,128)(2,1)S(1)} %get-tuple-element.33), channel_id=1, source_target_pairs={{0,16},{8,24},{16,32},{24,40},{32,48},{40,56},{48,0},{56,8},{1,17}... | collective-permute-start | bytes 221192 | tf_op jit(solution)/shard_map/ppermute | solution.py:292
  41.6 6.6 %collective-permute-start.12 = (bf16[8,4608]{1,0:T(8,128)(2,1)S(1)}, bf16[8,4608]{1,0:T(8,128)(2,1)S(1)}, u32[]{:S(2)}, u32[]{:S(2)}) collective-permute-start(bf16[8,4608]{1,0:T(8,128)(2,1)S(1)} %get-tuple-element.34), channel_id=1, source_target_pairs={{0,32},{8,40},{16,48},{24,56},{32,0},{40,8},{48,16},{56,24},{1,33}... | collective-permute-start | bytes 221192 | tf_op jit(solution)/shard_map/ppermute | solution.py:292
  43.1 5.0 %collective-permute-start.13 = (bf16[8,4608]{1,0:T(8,128)(2,1)S(1)}, bf16[8,4608]{1,0:T(8,128)(2,1)S(1)}, u32[]{:S(2)}, u32[]{:S(2)}) collective-permute-start(bf16[8,4608]{1,0:T(8,128)(2,1)S(1)} %get-tuple-element.35), channel_id=1, source_target_pairs={{0,48},{8,56},{16,0},{24,8},{32,16},{40,24},{48,32},{56,40},{1,49}... | collective-permute-start | bytes 221192 | tf_op jit(solution)/shard_map/ppermute | solution.py:292
  (3 other events, 10.5 us)

commit v5 on v4

--- a/solution.py
+++ b/solution.py
@@ -109,7 +109,11 @@
         dterms[t] = dot(attn, w_out[:, t * width : (t + 1) * width]).astype(BF16)
 
 
-def hold_kernel(rows, out):
+def begin_kernel(out):
+    out[...] = jnp.zeros_like(out)
+
+
+def hold_kernel(rows, _, out):
     out[...] = rows[...]
 
 
@@ -121,8 +125,7 @@
 
 
 def project_kernel(
-    mine, other, query_gain, key_gain, w_query, w_key, w_value, cosine, sine, dkey, dvalue,
-    query_out, tail_keys, tail_values, normed_f32,
+    mine, other, query_gain, w_query, cosine, sine, query_out, normed_out, normed_f32
 ):
     own = lax.axis_index("tensor")
     for k in range(4):
@@ -130,15 +133,21 @@
             at = pl.multiple_of((2 * ((own // 2 + 4 - k) % 4) + (own % 2 ^ flipped)) * 8, 8)
             normed_f32[pl.ds(at, 8), :] = ref[k].astype(F32)
     normed = normed_f32[...].astype(BF16)
-    cos = cosine[...]
-    sin = sine[...]
+    normed_out[...] = normed
     query = dot(normed, w_query[...])
     qgain = query_gain[...].astype(F32)
     for h in range(GROUP):
         at = slice(h * HEAD, (h + 1) * HEAD)
-        query_out[:, at] = rotate(rms(query[:, at], qgain), cos, sin).astype(BF16)
-    key = rotate(rms(dot(normed, w_key[...]), key_gain[...].astype(F32)), cos, sin)
-    value = dot(normed, w_value[...])
+        query_out[:, at] = rotate(rms(query[:, at], qgain), cosine[...], sine[...]).astype(BF16)
+
+
+def tail_kernel(
+    normed, key_gain, w_key, w_value, cosine, sine, dkey, dvalue, tail_keys, tail_values
+):
+    rows = normed[...]
+    key = rms(dot(rows, w_key[...]), key_gain[...].astype(F32))
+    key = rotate(key, cosine[...], sine[...])
+    value = dot(rows, w_value[...])
     pad = jnp.zeros((56, HEAD), F32)
     tail_keys[...] = jnp.concatenate([key, dkey[...], pad], axis=0).astype(BF16)
     tail_values[...] = jnp.concatenate([value, dvalue[...], pad], axis=0).astype(BF16)
@@ -327,7 +336,8 @@
     query_gain = query_gain.reshape(1, -1)
     key_gain = key_norm_gain.reshape(1, -1)
 
-    (own_rows,) = call(hold_kernel, [(summary_in.shape, BF16)], (summary_in,), flops=10**10)
+    (begun,) = call(begin_kernel, [((8, HEAD), F32)], (), flops=10**10)
+    (own_rows,) = call(hold_kernel, [(summary_in.shape, BF16)], (summary_in, begun))
     across = {0: own_rows}
     for k in Y_ORDER:
         across[k] = shift(own_rows, "tensor", 8, 2 * k)
@@ -349,17 +359,24 @@
         (*across, norm_gain, dkey, dvalue),
     )
     other = flip(mine, "tensor", 8, 1)
-    query, *tails = call(
+    query, normed = call(
         project_kernel,
-        [((rows, GROUP * HEAD), BF16), ((128, HEAD), BF16), ((128, HEAD), BF16)],
-        (mine, other, query_gain, key_gain, w_query, key_weight, w_value, cosine, sine, dkey, dvalue),
+        [((rows, GROUP * HEAD), BF16), ((rows, width), BF16)],
+        (mine, other, query_gain, w_query, cosine, sine),
         scratch=[pltpu.VMEM((rows, width), F32)],
         limit=24,
-        flops=2 * 64 * 4096 * 768,
+        flops=2 * 64 * 4096 * 512,
     )
     queries = {-1: query}
     for n in range(3):
         queries[n] = fetch(query, n)
+    tails = call(
+        tail_kernel,
+        [((128, HEAD), BF16), ((128, HEAD), BF16)],
+        (normed, key_gain, key_weight, w_value, cosine, sine, dkey, dvalue),
+        limit=24,
+        flops=2 * 64 * 4096 * 256,
+    )
 
     def attend(k, after):
         (part,) = call(

time: 48.9 us -> 48.3 us (0.988)
    pallas_call x12 -> x14, Pallas kernels: 16.4 us -> 16.6 us  [call(): pl.pallas_call(kernel, out_shape=outs, in_specs=specs, out_specs=tuple((p...]
  transfers between devices with their start and end apart: 14 -> 14, of which waited for: 6 -> 7; matrix products, arithmetic and copies ran while one was open for 0% -> 0% of each run, Pallas kernels for 27% -> 28%
where the time goes in v5:
time: 48.3 us; the launch traced here: 48.2 us
  starting transfers between devices  23.1 us (48%)
  Pallas kernels  16.6 us (34%)
  waiting for transfers between devices  6.79 us (14%)
  between operations  0.91 us (2%)
  local copies, waits for them, and re-layouts  0.76 us (2%)
    pallas_call x14, Pallas kernels, call(): pl.pallas_call(kernel, out_shape=outs, in_specs=specs, out_specs=tuple((p...  16.6 us
    ppermute x6, starting transfers between devices, shift(): return lax.ppermute(x, axis, [(i, (i + k) % size) for i in range(size)])  7.79 us
    ppermute x3, starting transfers between devices, give_back(): return lax.ppermute(x, ('path', 'tensor'), routes(step))  5.94 us
    ppermute x3, starting transfers between devices, fetch(): lax.ppermute(x, ('path', 'tensor'), [(b, a) for a, b in routes(step)])  4.79 us
    ppermute x2, starting transfers between devices, flip(): return lax.ppermute(x, axis, [(i, i ^ k) for i in range(size)])  4.57 us
    ppermute x6, waiting for transfers between devices, shift(): return lax.ppermute(x, axis, [(i, (i + k) % size) for i in range(size)])  4.52 us
    ppermute x2, waiting for transfers between devices, flip(): return lax.ppermute(x, axis, [(i, i ^ k) for i in range(size)])  1.55 us
  transfers between devices with their start and end apart: 14, of which 7 were waited for; matrix products, arithmetic and copies ran while one was open for 0% of the time, Pallas kernels for 28%

profile of v5, /device:TPU:1, one launch (start us, length us, event | category | flops | bytes accessed | tf_op | source)
XLA Modules:
  0.0 48.2 jit_solution(12636578823410750636)
XLA Ops:
  0.8 0.7 %copy-done.4 = bf16[8,4096]{1,0:T(8,128)(2,1)S(1)} copy-done((bf16[8,4096]{1,0:T(8,128)(2,1)S(1)}, bf16[8,4096]{1,0:T(8,128)(2,1)}, u32[]{:S(2)}) %copy-start.4) | copy-done | bytes 65560
  1.5 3.6 %collective-permute-start.2 = (bf16[8,4096]{1,0:T(8,128)(2,1)S(1)}, bf16[8,4096]{1,0:T(8,128)(2,1)S(1)}, u32[]{:S(2)}, u32[]{:S(2)}) collective-permute-start(bf16[8,4096]{1,0:T(8,128)(2,1)S(1)} %shard_map.141.rows0), channel_id=1, source_target_pairs={{0,48},{8,56},{16,0},{24,8},{32,16},{40,24},{48,32},{56,40},{1,49}... | collective-permute-start | bytes 196616 | tf_op jit(solution)/shard_map/ppermute | solution.py:301
  5.4 0.7 %collective-permute-start = (bf16[8,4096]{1,0:T(8,128)(2,1)S(1)}, bf16[8,4096]{1,0:T(8,128)(2,1)S(1)}, u32[]{:S(2)}, u32[]{:S(2)}) collective-permute-start(bf16[8,4096]{1,0:T(8,128)(2,1)S(1)} %shard_map.141.rows0), channel_id=1, source_target_pairs={{0,16},{8,24},{16,32},{24,40},{32,48},{40,56},{48,0},{56,8},{1,17}... | collective-permute-start | bytes 196616 | tf_op jit(solution)/shard_map/ppermute | solution.py:301
  6.2 3.1 %shard_map.142 = (bf16[8,8,512]{2,1,0:T(8,128)(2,1)S(1)}, f32[8,128]{1,0:T(8,128)S(1)}, f32[8,128]{1,0:T(8,128)S(1)}, f32[64,128]{1,0:T(8,128)S(1)}, f32[64,128]{1,0:T(8,128)S(1)}) custom-call(s32[8]{0:T(128)S(1)} %copy-done.11, bf16[2,4,4096]{2,1,0:T(4,128)(2,1)S(1)} %copy-done.9, bf16[2,4096]{1,0:T(2,128)(2,1)S(1)} %copy-done.10, ...), custom_call_target="tpu_custom_call" | custom-call | flops 6000000000 | bytes 12673568 | tf_op jit(solution)/shard_map/pallas_call | solution.py:284
  9.7 0.6 %collective-permute-done.rows1 = bf16[8,4096]{1,0:T(8,128)(2,1)S(1)} collective-permute-done((bf16[8,4096]{1,0:T(8,128)(2,1)S(1)}, bf16[8,4096]{1,0:T(8,128)(2,1)S(1)}, u32[]{:S(2)}, u32[]{:S(2)}) %collective-permute-start) | collective-permute-done | bytes 65568 | tf_op jit(solution)/shard_map/ppermute | solution.py:301
  10.6 2.2 %collective-permute-start.3 = (bf16[4,8,4096]{2,1,0:T(8,128)(2,1)S(1)}, bf16[4,8,4096]{2,1,0:T(8,128)(2,1)S(1)}, u32[]{:S(2)}, u32[]{:S(2)}) collective-permute-start(bf16[4,8,4096]{2,1,0:T(8,128)(2,1)S(1)} %get-tuple-element.22.mine), channel_id=1, source_target_pairs={{0,8},{8,0},{16,24},{24,16},{32,40},{40,32},{48,56},{56,48},{1,9},... | collective-permute-start | bytes 786440 | tf_op jit(solution)/shard_map/ppermute | solution.py:297
  12.8 1.2 %collective-permute-done.3.other = bf16[4,8,4096]{2,1,0:T(8,128)(2,1)S(1)} collective-permute-done((bf16[4,8,4096]{2,1,0:T(8,128)(2,1)S(1)}, bf16[4,8,4096]{2,1,0:T(8,128)(2,1)S(1)}, u32[]{:S(2)}, u32[]{:S(2)}) %collective-permute-start.3) | collective-permute-done | bytes 262176 | tf_op jit(solution)/shard_map/ppermute | solution.py:297
  13.9 1.1 %shard_map.144 = (bf16[64,512]{1,0:T(8,128)(2,1)S(1)}, bf16[64,4096]{1,0:T(8,128)(2,1)S(1)}) custom-call(bf16[4,8,4096]{2,1,0:T(8,128)(2,1)S(1)} %get-tuple-element.22.mine, bf16[4,8,4096]{2,1,0:T(8,128)(2,1)S(1)} %collective-permute-done.3.other, bf16[1,128]{1,0:T(2,128)(2,1)S(1)} %bitcast.3, bf16[4096,512]{1,0:T(8,128)(2,1)S(1)} %copy-done.1, ...), custom_call_target="tpu_custom_call" | custom-call | flops 268435456 | bytes 4784384 | tf_op jit(solution)/shard_map/pallas_call | solution.py:284
  15.0 4.4 %collective-permute-start.4 = (bf16[64,512]{1,0:T(8,128)(2,1)S(1)}, bf16[64,512]{1,0:T(8,128)(2,1)S(1)}, u32[]{:S(2)}, u32[]{:S(2)}) collective-permute-start(bf16[64,512]{1,0:T(8,128)(2,1)S(1)} %get-tuple-element.25._.query), channel_id=1, source_target_pairs={{192,0},{72,8},{208,16},{88,24},{224,32},{104,40},{240,48},{120,56... | collective-permute-start | bytes 196616 | tf_op jit(solution)/shard_map/ppermute | solution.py:311
  19.8 0.5 shard_map.145
  20.8 2.3 %shard_map.146._ = bf16[64,640]{1,0:T(8,128)(2,1)S(1)} custom-call(s32[8]{0:T(128)S(1)} %copy-done.11, bf16[64,512]{1,0:T(8,128)(2,1)S(1)} %collective-permute-done.4.query, bf16[2,2048,128]{2,1,0:T(8,128)(2,1)S(1)} %copy-done.7, bf16[2,2048,128]{2,1,0:T(8,128)(2,1)S(1)} %copy-done.8, bf16[128,128]{1,0:T(8,128)(2,1)S(1)} %get-tuple-element.29.tail_keys, ...), custom_call_target="tpu_custom_call" | custom-call | flops 3000000000 | bytes 2293792 | tf_op jit(solution)/shard_map/pallas_call | solution.py:284
  23.1 3.0 %collective-permute-start.5 = (bf16[64,640]{1,0:T(8,128)(2,1)S(1)}, bf16[64,640]{1,0:T(8,128)(2,1)S(1)}, u32[]{:S(2)}, u32[]{:S(2)}) collective-permute-start(bf16[64,640]{1,0:T(8,128)(2,1)S(1)} %shard_map.146._), channel_id=1, source_target_pairs={{0,192},{8,72},{16,208},{24,88},{32,224},{40,104},{48,240},{56,120... | collective-permute-start | bytes 245768 | tf_op jit(solution)/shard_map/ppermute | solution.py:315
  26.0 2.3 %shard_map.147._ = bf16[64,640]{1,0:T(8,128)(2,1)S(1)} custom-call(s32[8]{0:T(128)S(1)} %copy-done.11, bf16[64,512]{1,0:T(8,128)(2,1)S(1)} %collective-permute-done.6.query, bf16[2,2048,128]{2,1,0:T(8,128)(2,1)S(1)} %copy-done.7, bf16[2,2048,128]{2,1,0:T(8,128)(2,1)S(1)} %copy-done.8, bf16[128,128]{1,0:T(8,128)(2,1)S(1)} %get-tuple-element.29.tail_keys, ...), custom_call_target="tpu_custom_call" | custom-call | flops 3000000000 | bytes 2310176 | tf_op jit(solution)/shard_map/pallas_call | solution.py:284
  28.3 1.2 %collective-permute-start.7 = (bf16[64,640]{1,0:T(8,128)(2,1)S(1)}, bf16[64,640]{1,0:T(8,128)(2,1)S(1)}, u32[]{:S(2)}, u32[]{:S(2)}) collective-permute-start(bf16[64,640]{1,0:T(8,128)(2,1)S(1)} %shard_map.147._), channel_id=1, source_target_pairs={{0,128},{8,136},{16,144},{24,152},{32,160},{40,168},{48,176},{56,1... | collective-permute-start | bytes 245768 | tf_op jit(solution)/shard_map/ppermute | solution.py:315
  29.6 2.3 %shard_map.148._ = bf16[64,640]{1,0:T(8,128)(2,1)S(1)} custom-call(s32[8]{0:T(128)S(1)} %copy-done.11, bf16[64,512]{1,0:T(8,128)(2,1)S(1)} %collective-permute-done.8.query, bf16[2,2048,128]{2,1,0:T(8,128)(2,1)S(1)} %copy-done.7, bf16[2,2048,128]{2,1,0:T(8,128)(2,1)S(1)} %copy-done.8, bf16[128,128]{1,0:T(8,128)(2,1)S(1)} %get-tuple-element.29.tail_keys, ...), custom_call_target="tpu_custom_call" | custom-call | flops 3000000000 | bytes 2310176 | tf_op jit(solution)/shard_map/pallas_call | solution.py:284
  31.9 1.7 %collective-permute-start.9 = (bf16[64,640]{1,0:T(8,128)(2,1)S(1)}, bf16[64,640]{1,0:T(8,128)(2,1)S(1)}, u32[]{:S(2)}, u32[]{:S(2)}) collective-permute-start(bf16[64,640]{1,0:T(8,128)(2,1)S(1)} %shard_map.148._), channel_id=1, source_target_pairs={{0,64},{8,200},{16,80},{24,216},{32,96},{40,232},{48,112},{56,248}... | collective-permute-start | bytes 245768 | tf_op jit(solution)/shard_map/ppermute | solution.py:315
  33.6 2.3 %shard_map.149.part3 = bf16[64,640]{1,0:T(8,128)(2,1)S(1)} custom-call(s32[8]{0:T(128)S(1)} %copy-done.11, bf16[64,512]{1,0:T(8,128)(2,1)S(1)} %get-tuple-element.25._.query, bf16[2,2048,128]{2,1,0:T(8,128)(2,1)S(1)} %copy-done.7, bf16[2,2048,128]{2,1,0:T(8,128)(2,1)S(1)} %copy-done.8, bf16[128,128]{1,0:T(8,128)(2,1)S(1)} %get-tuple-element.29.tail_keys, ...), custom_call_target="tpu_custom_call" | custom-call | flops 3000000000 | bytes 2310176 | tf_op jit(solution)/shard_map/pallas_call | solution.py:284
  36.1 1.1 %shard_map.150 = (bf16[4,8,4608]{2,1,0:T(8,128)(2,1)S(1)}, f32[64,512]{1,0:T(8,128)S(1)}) custom-call(bf16[64,640]{1,0:T(8,128)(2,1)S(1)} %collective-permute-done.5.own_part, bf16[64,640]{1,0:T(8,128)(2,1)S(1)} %collective-permute-done.7.part1, bf16[64,640]{1,0:T(8,128)(2,1)S(1)} %collective-permute-done.9.part2, bf16[64,640]{1,0:T(8,128)(2,1)S(1)} %shard_map.149.part3, ...), custom_call_target="tpu_custom_call" | custom-call | flops 134217728 | bytes 4587520 | tf_op jit(solution)/shard_map/pallas_call | solution.py:284
  37.2 2.4 %collective-permute-start.10 = (bf16[4,8,4608]{2,1,0:T(8,128)(2,1)S(1)}, bf16[4,8,4608]{2,1,0:T(8,128)(2,1)S(1)}, u32[]{:S(2)}, u32[]{:S(2)}) collective-permute-start(bf16[4,8,4608]{2,1,0:T(8,128)(2,1)S(1)} %get-tuple-element.33), channel_id=1, source_target_pairs={{0,8},{8,0},{16,24},{24,16},{32,40},{40,32},{48,56},{56,48},{1,9},... | collective-permute-start | bytes 884744 | tf_op jit(solution)/shard_map/ppermute | solution.py:297
  39.6 0.8 %shard_map.151.keep = f32[4,8,4608]{2,1,0:T(8,128)S(1)} custom-call(f32[64,512]{1,0:T(8,128)S(1)} %get-tuple-element.32.attn, bf16[512,4096]{1,0:T(8,128)(2,1)S(1)} %copy-done, bf16[8,8,512]{2,1,0:T(8,128)(2,1)S(1)} %get-tuple-element.31.dterms), custom_call_target="tpu_custom_call" | custom-call | flops 134217728 | bytes 4390912 | tf_op jit(solution)/shard_map/pallas_call | solution.py:284
  41.0 1.5 %collective-permute-start.12 = (bf16[8,4608]{1,0:T(8,128)(2,1)S(1)}, bf16[8,4608]{1,0:T(8,128)(2,1)S(1)}, u32[]{:S(2)}, u32[]{:S(2)}) collective-permute-start(bf16[8,4608]{1,0:T(8,128)(2,1)S(1)} %get-tuple-element.36), channel_id=1, source_target_pairs={{0,32},{8,40},{16,48},{24,56},{32,0},{40,8},{48,16},{56,24},{1,33}... | collective-permute-start | bytes 221192 | tf_op jit(solution)/shard_map/ppermute | solution.py:301
  42.5 1.6 %collective-permute-start.13 = (bf16[8,4608]{1,0:T(8,128)(2,1)S(1)}, bf16[8,4608]{1,0:T(8,128)(2,1)S(1)}, u32[]{:S(2)}, u32[]{:S(2)}) collective-permute-start(bf16[8,4608]{1,0:T(8,128)(2,1)S(1)} %get-tuple-element.37), channel_id=1, source_target_pairs={{0,48},{8,56},{16,0},{24,8},{32,16},{40,24},{48,32},{56,40},{1,49}... | collective-permute-start | bytes 221192 | tf_op jit(solution)/shard_map/ppermute | solution.py:301
  44.1 3.5 %collective-permute-done.11.in1 = bf16[8,4608]{1,0:T(8,128)(2,1)S(1)} collective-permute-done((bf16[8,4608]{1,0:T(8,128)(2,1)S(1)}, bf16[8,4608]{1,0:T(8,128)(2,1)S(1)}, u32[]{:S(2)}, u32[]{:S(2)}) %collective-permute-start.11) | collective-permute-done | bytes 73760 | tf_op jit(solution)/shard_map/ppermute | solution.py:301
  47.5 0.7 %shard_map.153 = (bf16[2,4,512]{2,1,0:T(4,128)(2,1)}, bf16[8,4096]{1,0:T(8,128)(2,1)}) custom-call(f32[8,4608]{1,0:T(8,128)S(1)} %get-tuple-element.34.own, bf16[8,4608]{1,0:T(8,128)(2,1)S(1)} %collective-permute-done.11.in1, bf16[8,4608]{1,0:T(8,128)(2,1)S(1)} %collective-permute-done.12.in2, bf16[8,4608]{1,0:T(8,128)(2,1)S(1)} %collective-permute-done.13.in3), custom_call_target="tpu_custom_call" | custom-call | bytes 368640 | tf_op jit(solution)/shard_map/pallas_call | solution.py:284
  (45 shorter events, 2.7 us)
Async XLA Ops:
  0.7 5.5 %copy-start.11 = (s32[8]{0:T(128)S(1)}, s32[8]{0:T(128)}, u32[]{:S(2)}) copy-start(s32[8]{0:T(128)} %lengths.9) | copy-start | bytes 100
  0.7 5.5 %copy-start.8 = (bf16[2,2048,128]{2,1,0:T(8,128)(2,1)S(1)}, bf16[2,2048,128]{2,1,0:T(8,128)(2,1)}, u32[]{:S(2)}) copy-start(bf16[2,2048,128]{2,1,0:T(8,128)(2,1)} %values.9) | copy-start | bytes 3145732
  0.7 5.5 %copy-start.7 = (bf16[2,2048,128]{2,1,0:T(8,128)(2,1)S(1)}, bf16[2,2048,128]{2,1,0:T(8,128)(2,1)}, u32[]{:S(2)}) copy-start(bf16[2,2048,128]{2,1,0:T(8,128)(2,1)} %keys.9) | copy-start | bytes 3145732
  0.7 5.5 %copy-start = (bf16[512,4096]{1,0:T(8,128)(2,1)S(1)}, bf16[512,4096]{1,0:T(8,128)(2,1)}, u32[]{:S(2)}) copy-start(bf16[512,4096]{1,0:T(8,128)(2,1)} %w_out.5) | copy-start | bytes 12582916
  0.7 5.5 %copy-start.3 = (bf16[4096,128]{1,0:T(8,128)(2,1)S(1)}, bf16[4096,128]{1,0:T(8,128)(2,1)}, u32[]{:S(2)}) copy-start(bf16[4096,128]{1,0:T(8,128)(2,1)} %w_value.3) | copy-start | bytes 3145732
  0.7 5.5 %copy-start.2 = (bf16[4096,128]{1,0:T(8,128)(2,1)S(1)}, bf16[4096,128]{1,0:T(8,128)(2,1)}, u32[]{:S(2)}) copy-start(bf16[4096,128]{1,0:T(8,128)(2,1)} %w_key.3) | copy-start | bytes 3145732
  0.7 5.5 %copy-start.1 = (bf16[4096,512]{1,0:T(8,128)(2,1)S(1)}, bf16[4096,512]{1,0:T(8,128)(2,1)}, u32[]{:S(2)}) copy-start(bf16[4096,512]{1,0:T(8,128)(2,1)} %w_query.3) | copy-start | bytes 12582916
  0.7 5.5 %copy-start.6 = (bf16[128]{0:T(256)(128)(2,1)S(1)}, bf16[128]{0:T(256)(128)(2,1)}, u32[]{:S(2)}) copy-start(bf16[128]{0:T(256)(128)(2,1)} %param.18) | copy-start | bytes 772
  0.7 5.5 %copy-start.5 = (bf16[128]{0:T(256)(128)(2,1)S(1)}, bf16[128]{0:T(256)(128)(2,1)}, u32[]{:S(2)}) copy-start(bf16[128]{0:T(256)(128)(2,1)} %param.17) | copy-start | bytes 772
  0.7 5.5 %copy-start.10 = (bf16[2,4096]{1,0:T(2,128)(2,1)S(1)}, bf16[2,4096]{1,0:T(2,128)(2,1)}, u32[]{:S(2)}) copy-start(bf16[2,4096]{1,0:T(2,128)(2,1)} %embed.1) | copy-start | bytes 49156
  1.5 7.8 %collective-permute-start.2 = (bf16[8,4096]{1,0:T(8,128)(2,1)S(1)}, bf16[8,4096]{1,0:T(8,128)(2,1)S(1)}, u32[]{:S(2)}, u32[]{:S(2)}) collective-permute-start(bf16[8,4096]{1,0:T(8,128)(2,1)S(1)} %shard_map.141.rows0), channel_id=1, source_target_pairs={{0,48},{8,56},{16,0},{24,8},{32,16},{40,24},{48,32},{56,40},{1,49}... | collective-permute-start | bytes 196616 | tf_op jit(solution)/shard_map/ppermute | solution.py:301
  5.0 4.7 %collective-permute-start.1 = (bf16[8,4096]{1,0:T(8,128)(2,1)S(1)}, bf16[8,4096]{1,0:T(8,128)(2,1)S(1)}, u32[]{:S(2)}, u32[]{:S(2)}) collective-permute-start(bf16[8,4096]{1,0:T(8,128)(2,1)S(1)} %shard_map.141.rows0), channel_id=1, source_target_pairs={{0,32},{8,40},{16,48},{24,56},{32,0},{40,8},{48,16},{56,24},{1,33}... | collective-permute-start | bytes 196616 | tf_op jit(solution)/shard_map/ppermute | solution.py:301
  5.4 5.0 %collective-permute-start = (bf16[8,4096]{1,0:T(8,128)(2,1)S(1)}, bf16[8,4096]{1,0:T(8,128)(2,1)S(1)}, u32[]{:S(2)}, u32[]{:S(2)}) collective-permute-start(bf16[8,4096]{1,0:T(8,128)(2,1)S(1)} %shard_map.141.rows0), channel_id=1, source_target_pairs={{0,16},{8,24},{16,32},{24,40},{32,48},{40,56},{48,0},{56,8},{1,17}... | collective-permute-start | bytes 196616 | tf_op jit(solution)/shard_map/ppermute | solution.py:301
  10.6 3.4 %collective-permute-start.3 = (bf16[4,8,4096]{2,1,0:T(8,128)(2,1)S(1)}, bf16[4,8,4096]{2,1,0:T(8,128)(2,1)S(1)}, u32[]{:S(2)}, u32[]{:S(2)}) collective-permute-start(bf16[4,8,4096]{2,1,0:T(8,128)(2,1)S(1)} %get-tuple-element.22.mine), channel_id=1, source_target_pairs={{0,8},{8,0},{16,24},{24,16},{32,40},{40,32},{48,56},{56,48},{1,9},... | collective-permute-start | bytes 786440 | tf_op jit(solution)/shard_map/ppermute | solution.py:297
  15.0 5.8 %collective-permute-start.4 = (bf16[64,512]{1,0:T(8,128)(2,1)S(1)}, bf16[64,512]{1,0:T(8,128)(2,1)S(1)}, u32[]{:S(2)}, u32[]{:S(2)}) collective-permute-start(bf16[64,512]{1,0:T(8,128)(2,1)S(1)} %get-tuple-element.25._.query), channel_id=1, source_target_pairs={{192,0},{72,8},{208,16},{88,24},{224,32},{104,40},{240,48},{120,56... | collective-permute-start | bytes 196616 | tf_op jit(solution)/shard_map/ppermute | solution.py:311
  19.4 10.1 %collective-permute-start.8 = (bf16[64,512]{1,0:T(8,128)(2,1)S(1)}, bf16[64,512]{1,0:T(8,128)(2,1)S(1)}, u32[]{:S(2)}, u32[]{:S(2)}) collective-permute-start(bf16[64,512]{1,0:T(8,128)(2,1)S(1)} %get-tuple-element.25._.query), channel_id=1, source_target_pairs={{64,0},{200,8},{80,16},{216,24},{96,32},{232,40},{112,48},{248,56}... | collective-permute-start | bytes 196616 | tf_op jit(solution)/shard_map/ppermute | solution.py:311
  19.4 6.6 %collective-permute-start.6 = (bf16[64,512]{1,0:T(8,128)(2,1)S(1)}, bf16[64,512]{1,0:T(8,128)(2,1)S(1)}, u32[]{:S(2)}, u32[]{:S(2)}) collective-permute-start(bf16[64,512]{1,0:T(8,128)(2,1)S(1)} %get-tuple-element.25._.query), channel_id=1, source_target_pairs={{128,0},{136,8},{144,16},{152,24},{160,32},{168,40},{176,48},{184,... | collective-permute-start | bytes 196616 | tf_op jit(solution)/shard_map/ppermute | solution.py:311
  23.1 13.1 %collective-permute-start.5 = (bf16[64,640]{1,0:T(8,128)(2,1)S(1)}, bf16[64,640]{1,0:T(8,128)(2,1)S(1)}, u32[]{:S(2)}, u32[]{:S(2)}) collective-permute-start(bf16[64,640]{1,0:T(8,128)(2,1)S(1)} %shard_map.146._), channel_id=1, source_target_pairs={{0,192},{8,72},{16,208},{24,88},{32,224},{40,104},{48,240},{56,120... | collective-permute-start | bytes 245768 | tf_op jit(solution)/shard_map/ppermute | solution.py:315
  28.3 7.8 %collective-permute-start.7 = (bf16[64,640]{1,0:T(8,128)(2,1)S(1)}, bf16[64,640]{1,0:T(8,128)(2,1)S(1)}, u32[]{:S(2)}, u32[]{:S(2)}) collective-permute-start(bf16[64,640]{1,0:T(8,128)(2,1)S(1)} %shard_map.147._), channel_id=1, source_target_pairs={{0,128},{8,136},{16,144},{24,152},{32,160},{40,168},{48,176},{56,1... | collective-permute-start | bytes 245768 | tf_op jit(solution)/shard_map/ppermute | solution.py:315
  31.9 4.2 %collective-permute-start.9 = (bf16[64,640]{1,0:T(8,128)(2,1)S(1)}, bf16[64,640]{1,0:T(8,128)(2,1)S(1)}, u32[]{:S(2)}, u32[]{:S(2)}) collective-permute-start(bf16[64,640]{1,0:T(8,128)(2,1)S(1)} %shard_map.148._), channel_id=1, source_target_pairs={{0,64},{8,200},{16,80},{24,216},{32,96},{40,232},{48,112},{56,248}... | collective-permute-start | bytes 245768 | tf_op jit(solution)/shard_map/ppermute | solution.py:315
  37.2 3.6 %collective-permute-start.10 = (bf16[4,8,4608]{2,1,0:T(8,128)(2,1)S(1)}, bf16[4,8,4608]{2,1,0:T(8,128)(2,1)S(1)}, u32[]{:S(2)}, u32[]{:S(2)}) collective-permute-start(bf16[4,8,4608]{2,1,0:T(8,128)(2,1)S(1)} %get-tuple-element.33), channel_id=1, source_target_pairs={{0,8},{8,0},{16,24},{24,16},{32,40},{40,32},{48,56},{56,48},{1,9},... | collective-permute-start | bytes 884744 | tf_op jit(solution)/shard_map/ppermute | solution.py:297
  40.9 6.7 %collective-permute-start.11 = (bf16[8,4608]{1,0:T(8,128)(2,1)S(1)}, bf16[8,4608]{1,0:T(8,128)(2,1)S(1)}, u32[]{:S(2)}, u32[]{:S(2)}) collective-permute-start(bf16[8,4608]{1,0:T(8,128)(2,1)S(1)} %get-tuple-element.35), channel_id=1, source_target_pairs={{0,16},{8,24},{16,32},{24,40},{32,48},{40,56},{48,0},{56,8},{1,17}... | collective-permute-start | bytes 221192 | tf_op jit(solution)/shard_map/ppermute | solution.py:301
  41.0 6.6 %collective-permute-start.12 = (bf16[8,4608]{1,0:T(8,128)(2,1)S(1)}, bf16[8,4608]{1,0:T(8,128)(2,1)S(1)}, u32[]{:S(2)}, u32[]{:S(2)}) collective-permute-start(bf16[8,4608]{1,0:T(8,128)(2,1)S(1)} %get-tuple-element.36), channel_id=1, source_target_pairs={{0,32},{8,40},{16,48},{24,56},{32,0},{40,8},{48,16},{56,24},{1,33}... | collective-permute-start | bytes 221192 | tf_op jit(solution)/shard_map/ppermute | solution.py:301
  42.5 5.0 %collective-permute-start.13 = (bf16[8,4608]{1,0:T(8,128)(2,1)S(1)}, bf16[8,4608]{1,0:T(8,128)(2,1)S(1)}, u32[]{:S(2)}, u32[]{:S(2)}) collective-permute-start(bf16[8,4608]{1,0:T(8,128)(2,1)S(1)} %get-tuple-element.37), channel_id=1, source_target_pairs={{0,48},{8,56},{16,0},{24,8},{32,16},{40,24},{48,32},{56,40},{1,49}... | collective-permute-start | bytes 221192 | tf_op jit(solution)/shard_map/ppermute | solution.py:301
  (3 other events, 11.7 us)

commit v6 on v5

--- a/solution.py
+++ b/solution.py
@@ -183,7 +183,7 @@
     peak = jnp.max(scores, axis=-1, keepdims=True) * SCALE2
     coming = chunk_scores(*chunks[0])
     w = jnp.exp2(scores * SCALE2 - peak)
-    total = jnp.sum(w, axis=-1, keepdims=True)
+    total = w
     mix = dot(w.astype(BF16), tail_values[...])
     for n, (i, c) in enumerate(chunks):
         scores = coming
@@ -192,9 +192,10 @@
         higher = jnp.maximum(peak, jnp.max(scores, axis=-1, keepdims=True) * SCALE2)
         fade = jnp.exp2(peak - higher)
         w = jnp.exp2(scores * SCALE2 - higher)
-        total = total * fade + jnp.sum(w, axis=-1, keepdims=True)
+        total = total * fade + sum(w[:, k : k + HEAD] for k in range(0, CHUNK, HEAD))
         mix = mix * fade + dot(w.astype(BF16), values[i, c : c + CHUNK, :])
         peak = higher
+    total = jnp.sum(total, axis=-1, keepdims=True)
     rounded = peak.astype(BF16).astype(F32)
     fade = jnp.exp2(peak - rounded)
     write_part(out, rows, mix * fade, rounded, total * fade)

time: 48.3 us -> 48.4 us (level)
  no operation moved by 1% of the time
where the time goes in v6:
time: 48.4 us; the launch traced here: 48.3 us
  starting transfers between devices  23.1 us (48%)
  Pallas kernels  16.8 us (35%)
  waiting for transfers between devices  6.75 us (14%)
  between operations  0.89 us (2%)
  local copies, waits for them, and re-layouts  0.76 us (2%)
    pallas_call x14, Pallas kernels, call(): pl.pallas_call(kernel, out_shape=outs, in_specs=specs, out_specs=tuple((p...  16.8 us
    ppermute x6, starting transfers between devices, shift(): return lax.ppermute(x, axis, [(i, (i + k) % size) for i in range(size)])  7.79 us
    ppermute x3, starting transfers between devices, give_back(): return lax.ppermute(x, ('path', 'tensor'), routes(step))  5.91 us
    ppermute x3, starting transfers between devices, fetch(): lax.ppermute(x, ('path', 'tensor'), [(b, a) for a, b in routes(step)])  4.79 us
    ppermute x2, starting transfers between devices, flip(): return lax.ppermute(x, axis, [(i, i ^ k) for i in range(size)])  4.57 us
    ppermute x6, waiting for transfers between devices, shift(): return lax.ppermute(x, axis, [(i, (i + k) % size) for i in range(size)])  4.52 us
    ppermute x2, waiting for transfers between devices, flip(): return lax.ppermute(x, axis, [(i, i ^ k) for i in range(size)])  1.55 us
  transfers between devices with their start and end apart: 14, of which 7 were waited for; matrix products, arithmetic and copies ran while one was open for 0% of the time, Pallas kernels for 28%

profile of v6, /device:TPU:1, one launch (start us, length us, event | category | flops | bytes accessed | tf_op | source)
XLA Modules:
  0.0 48.3 jit_solution(12631887440573693813)
XLA Ops:
  0.8 0.7 %copy-done.4 = bf16[8,4096]{1,0:T(8,128)(2,1)S(1)} copy-done((bf16[8,4096]{1,0:T(8,128)(2,1)S(1)}, bf16[8,4096]{1,0:T(8,128)(2,1)}, u32[]{:S(2)}) %copy-start.4) | copy-done | bytes 65560
  1.5 3.6 %collective-permute-start.2 = (bf16[8,4096]{1,0:T(8,128)(2,1)S(1)}, bf16[8,4096]{1,0:T(8,128)(2,1)S(1)}, u32[]{:S(2)}, u32[]{:S(2)}) collective-permute-start(bf16[8,4096]{1,0:T(8,128)(2,1)S(1)} %shard_map.141.rows0), channel_id=1, source_target_pairs={{0,48},{8,56},{16,0},{24,8},{32,16},{40,24},{48,32},{56,40},{1,49}... | collective-permute-start | bytes 196616 | tf_op jit(solution)/shard_map/ppermute | solution.py:302
  5.4 0.7 %collective-permute-start = (bf16[8,4096]{1,0:T(8,128)(2,1)S(1)}, bf16[8,4096]{1,0:T(8,128)(2,1)S(1)}, u32[]{:S(2)}, u32[]{:S(2)}) collective-permute-start(bf16[8,4096]{1,0:T(8,128)(2,1)S(1)} %shard_map.141.rows0), channel_id=1, source_target_pairs={{0,16},{8,24},{16,32},{24,40},{32,48},{40,56},{48,0},{56,8},{1,17}... | collective-permute-start | bytes 196616 | tf_op jit(solution)/shard_map/ppermute | solution.py:302
  6.2 3.1 %shard_map.142 = (bf16[8,8,512]{2,1,0:T(8,128)(2,1)S(1)}, f32[8,128]{1,0:T(8,128)S(1)}, f32[8,128]{1,0:T(8,128)S(1)}, f32[64,128]{1,0:T(8,128)S(1)}, f32[64,128]{1,0:T(8,128)S(1)}) custom-call(s32[8]{0:T(128)S(1)} %copy-done.11, bf16[2,4,4096]{2,1,0:T(4,128)(2,1)S(1)} %copy-done.9, bf16[2,4096]{1,0:T(2,128)(2,1)S(1)} %copy-done.10, ...), custom_call_target="tpu_custom_call" | custom-call | flops 6000000000 | bytes 12673568 | tf_op jit(solution)/shard_map/pallas_call | solution.py:285
  9.7 0.6 %collective-permute-done.rows1 = bf16[8,4096]{1,0:T(8,128)(2,1)S(1)} collective-permute-done((bf16[8,4096]{1,0:T(8,128)(2,1)S(1)}, bf16[8,4096]{1,0:T(8,128)(2,1)S(1)}, u32[]{:S(2)}, u32[]{:S(2)}) %collective-permute-start) | collective-permute-done | bytes 65568 | tf_op jit(solution)/shard_map/ppermute | solution.py:302
  10.6 2.2 %collective-permute-start.3 = (bf16[4,8,4096]{2,1,0:T(8,128)(2,1)S(1)}, bf16[4,8,4096]{2,1,0:T(8,128)(2,1)S(1)}, u32[]{:S(2)}, u32[]{:S(2)}) collective-permute-start(bf16[4,8,4096]{2,1,0:T(8,128)(2,1)S(1)} %get-tuple-element.22.mine), channel_id=1, source_target_pairs={{0,8},{8,0},{16,24},{24,16},{32,40},{40,32},{48,56},{56,48},{1,9},... | collective-permute-start | bytes 786440 | tf_op jit(solution)/shard_map/ppermute | solution.py:298
  12.8 1.2 %collective-permute-done.3.other = bf16[4,8,4096]{2,1,0:T(8,128)(2,1)S(1)} collective-permute-done((bf16[4,8,4096]{2,1,0:T(8,128)(2,1)S(1)}, bf16[4,8,4096]{2,1,0:T(8,128)(2,1)S(1)}, u32[]{:S(2)}, u32[]{:S(2)}) %collective-permute-start.3) | collective-permute-done | bytes 262176 | tf_op jit(solution)/shard_map/ppermute | solution.py:298
  13.9 1.1 %shard_map.144 = (bf16[64,512]{1,0:T(8,128)(2,1)S(1)}, bf16[64,4096]{1,0:T(8,128)(2,1)S(1)}) custom-call(bf16[4,8,4096]{2,1,0:T(8,128)(2,1)S(1)} %get-tuple-element.22.mine, bf16[4,8,4096]{2,1,0:T(8,128)(2,1)S(1)} %collective-permute-done.3.other, bf16[1,128]{1,0:T(2,128)(2,1)S(1)} %bitcast.3, bf16[4096,512]{1,0:T(8,128)(2,1)S(1)} %copy-done.1, ...), custom_call_target="tpu_custom_call" | custom-call | flops 268435456 | bytes 4784384 | tf_op jit(solution)/shard_map/pallas_call | solution.py:285
  15.0 4.4 %collective-permute-start.4 = (bf16[64,512]{1,0:T(8,128)(2,1)S(1)}, bf16[64,512]{1,0:T(8,128)(2,1)S(1)}, u32[]{:S(2)}, u32[]{:S(2)}) collective-permute-start(bf16[64,512]{1,0:T(8,128)(2,1)S(1)} %get-tuple-element.25._.query), channel_id=1, source_target_pairs={{192,0},{72,8},{208,16},{88,24},{224,32},{104,40},{240,48},{120,56... | collective-permute-start | bytes 196616 | tf_op jit(solution)/shard_map/ppermute | solution.py:312
  19.8 0.5 shard_map.145
  20.8 2.3 %shard_map.146._ = bf16[64,640]{1,0:T(8,128)(2,1)S(1)} custom-call(s32[8]{0:T(128)S(1)} %copy-done.11, bf16[64,512]{1,0:T(8,128)(2,1)S(1)} %collective-permute-done.4.query, bf16[2,2048,128]{2,1,0:T(8,128)(2,1)S(1)} %copy-done.7, bf16[2,2048,128]{2,1,0:T(8,128)(2,1)S(1)} %copy-done.8, bf16[128,128]{1,0:T(8,128)(2,1)S(1)} %get-tuple-element.29.tail_keys, ...), custom_call_target="tpu_custom_call" | custom-call | flops 3000000000 | bytes 2293792 | tf_op jit(solution)/shard_map/pallas_call | solution.py:285
  23.1 3.0 %collective-permute-start.5 = (bf16[64,640]{1,0:T(8,128)(2,1)S(1)}, bf16[64,640]{1,0:T(8,128)(2,1)S(1)}, u32[]{:S(2)}, u32[]{:S(2)}) collective-permute-start(bf16[64,640]{1,0:T(8,128)(2,1)S(1)} %shard_map.146._), channel_id=1, source_target_pairs={{0,192},{8,72},{16,208},{24,88},{32,224},{40,104},{48,240},{56,120... | collective-permute-start | bytes 245768 | tf_op jit(solution)/shard_map/ppermute | solution.py:316
  26.1 2.3 %shard_map.147._ = bf16[64,640]{1,0:T(8,128)(2,1)S(1)} custom-call(s32[8]{0:T(128)S(1)} %copy-done.11, bf16[64,512]{1,0:T(8,128)(2,1)S(1)} %collective-permute-done.6.query, bf16[2,2048,128]{2,1,0:T(8,128)(2,1)S(1)} %copy-done.7, bf16[2,2048,128]{2,1,0:T(8,128)(2,1)S(1)} %copy-done.8, bf16[128,128]{1,0:T(8,128)(2,1)S(1)} %get-tuple-element.29.tail_keys, ...), custom_call_target="tpu_custom_call" | custom-call | flops 3000000000 | bytes 2310176 | tf_op jit(solution)/shard_map/pallas_call | solution.py:285
  28.4 1.2 %collective-permute-start.7 = (bf16[64,640]{1,0:T(8,128)(2,1)S(1)}, bf16[64,640]{1,0:T(8,128)(2,1)S(1)}, u32[]{:S(2)}, u32[]{:S(2)}) collective-permute-start(bf16[64,640]{1,0:T(8,128)(2,1)S(1)} %shard_map.147._), channel_id=1, source_target_pairs={{0,128},{8,136},{16,144},{24,152},{32,160},{40,168},{48,176},{56,1... | collective-permute-start | bytes 245768 | tf_op jit(solution)/shard_map/ppermute | solution.py:316
  29.6 2.3 %shard_map.148._ = bf16[64,640]{1,0:T(8,128)(2,1)S(1)} custom-call(s32[8]{0:T(128)S(1)} %copy-done.11, bf16[64,512]{1,0:T(8,128)(2,1)S(1)} %collective-permute-done.8.query, bf16[2,2048,128]{2,1,0:T(8,128)(2,1)S(1)} %copy-done.7, bf16[2,2048,128]{2,1,0:T(8,128)(2,1)S(1)} %copy-done.8, bf16[128,128]{1,0:T(8,128)(2,1)S(1)} %get-tuple-element.29.tail_keys, ...), custom_call_target="tpu_custom_call" | custom-call | flops 3000000000 | bytes 2310176 | tf_op jit(solution)/shard_map/pallas_call | solution.py:285
  32.0 1.7 %collective-permute-start.9 = (bf16[64,640]{1,0:T(8,128)(2,1)S(1)}, bf16[64,640]{1,0:T(8,128)(2,1)S(1)}, u32[]{:S(2)}, u32[]{:S(2)}) collective-permute-start(bf16[64,640]{1,0:T(8,128)(2,1)S(1)} %shard_map.148._), channel_id=1, source_target_pairs={{0,64},{8,200},{16,80},{24,216},{32,96},{40,232},{48,112},{56,248}... | collective-permute-start | bytes 245768 | tf_op jit(solution)/shard_map/ppermute | solution.py:316
  33.7 2.3 %shard_map.149.part3 = bf16[64,640]{1,0:T(8,128)(2,1)S(1)} custom-call(s32[8]{0:T(128)S(1)} %copy-done.11, bf16[64,512]{1,0:T(8,128)(2,1)S(1)} %get-tuple-element.25._.query, bf16[2,2048,128]{2,1,0:T(8,128)(2,1)S(1)} %copy-done.7, bf16[2,2048,128]{2,1,0:T(8,128)(2,1)S(1)} %copy-done.8, bf16[128,128]{1,0:T(8,128)(2,1)S(1)} %get-tuple-element.29.tail_keys, ...), custom_call_target="tpu_custom_call" | custom-call | flops 3000000000 | bytes 2310176 | tf_op jit(solution)/shard_map/pallas_call | solution.py:285
  36.2 1.1 %shard_map.150 = (bf16[4,8,4608]{2,1,0:T(8,128)(2,1)S(1)}, f32[64,512]{1,0:T(8,128)S(1)}) custom-call(bf16[64,640]{1,0:T(8,128)(2,1)S(1)} %collective-permute-done.5.own_part, bf16[64,640]{1,0:T(8,128)(2,1)S(1)} %collective-permute-done.7.part1, bf16[64,640]{1,0:T(8,128)(2,1)S(1)} %collective-permute-done.9.part2, bf16[64,640]{1,0:T(8,128)(2,1)S(1)} %shard_map.149.part3, ...), custom_call_target="tpu_custom_call" | custom-call | flops 134217728 | bytes 4587520 | tf_op jit(solution)/shard_map/pallas_call | solution.py:285
  37.3 2.4 %collective-permute-start.10 = (bf16[4,8,4608]{2,1,0:T(8,128)(2,1)S(1)}, bf16[4,8,4608]{2,1,0:T(8,128)(2,1)S(1)}, u32[]{:S(2)}, u32[]{:S(2)}) collective-permute-start(bf16[4,8,4608]{2,1,0:T(8,128)(2,1)S(1)} %get-tuple-element.33), channel_id=1, source_target_pairs={{0,8},{8,0},{16,24},{24,16},{32,40},{40,32},{48,56},{56,48},{1,9},... | collective-permute-start | bytes 884744 | tf_op jit(solution)/shard_map/ppermute | solution.py:298
  39.7 0.8 %shard_map.151.keep = f32[4,8,4608]{2,1,0:T(8,128)S(1)} custom-call(f32[64,512]{1,0:T(8,128)S(1)} %get-tuple-element.32.attn, bf16[512,4096]{1,0:T(8,128)(2,1)S(1)} %copy-done, bf16[8,8,512]{2,1,0:T(8,128)(2,1)S(1)} %get-tuple-element.31.dterms), custom_call_target="tpu_custom_call" | custom-call | flops 134217728 | bytes 4390912 | tf_op jit(solution)/shard_map/pallas_call | solution.py:285
  41.0 1.5 %collective-permute-start.12 = (bf16[8,4608]{1,0:T(8,128)(2,1)S(1)}, bf16[8,4608]{1,0:T(8,128)(2,1)S(1)}, u32[]{:S(2)}, u32[]{:S(2)}) collective-permute-start(bf16[8,4608]{1,0:T(8,128)(2,1)S(1)} %get-tuple-element.36), channel_id=1, source_target_pairs={{0,32},{8,40},{16,48},{24,56},{32,0},{40,8},{48,16},{56,24},{1,33}... | collective-permute-start | bytes 221192 | tf_op jit(solution)/shard_map/ppermute | solution.py:302
  42.6 1.6 %collective-permute-start.13 = (bf16[8,4608]{1,0:T(8,128)(2,1)S(1)}, bf16[8,4608]{1,0:T(8,128)(2,1)S(1)}, u32[]{:S(2)}, u32[]{:S(2)}) collective-permute-start(bf16[8,4608]{1,0:T(8,128)(2,1)S(1)} %get-tuple-element.37), channel_id=1, source_target_pairs={{0,48},{8,56},{16,0},{24,8},{32,16},{40,24},{48,32},{56,40},{1,49}... | collective-permute-start | bytes 221192 | tf_op jit(solution)/shard_map/ppermute | solution.py:302
  44.1 3.5 %collective-permute-done.11.in1 = bf16[8,4608]{1,0:T(8,128)(2,1)S(1)} collective-permute-done((bf16[8,4608]{1,0:T(8,128)(2,1)S(1)}, bf16[8,4608]{1,0:T(8,128)(2,1)S(1)}, u32[]{:S(2)}, u32[]{:S(2)}) %collective-permute-start.11) | collective-permute-done | bytes 73760 | tf_op jit(solution)/shard_map/ppermute | solution.py:302
  47.6 0.7 %shard_map.153 = (bf16[2,4,512]{2,1,0:T(4,128)(2,1)}, bf16[8,4096]{1,0:T(8,128)(2,1)}) custom-call(f32[8,4608]{1,0:T(8,128)S(1)} %get-tuple-element.34.own, bf16[8,4608]{1,0:T(8,128)(2,1)S(1)} %collective-permute-done.11.in1, bf16[8,4608]{1,0:T(8,128)(2,1)S(1)} %collective-permute-done.12.in2, bf16[8,4608]{1,0:T(8,128)(2,1)S(1)} %collective-permute-done.13.in3), custom_call_target="tpu_custom_call" | custom-call | bytes 368640 | tf_op jit(solution)/shard_map/pallas_call | solution.py:285
  (45 shorter events, 2.6 us)
Async XLA Ops:
  0.7 5.5 %copy-start.11 = (s32[8]{0:T(128)S(1)}, s32[8]{0:T(128)}, u32[]{:S(2)}) copy-start(s32[8]{0:T(128)} %lengths.9) | copy-start | bytes 100
  0.7 5.5 %copy-start.8 = (bf16[2,2048,128]{2,1,0:T(8,128)(2,1)S(1)}, bf16[2,2048,128]{2,1,0:T(8,128)(2,1)}, u32[]{:S(2)}) copy-start(bf16[2,2048,128]{2,1,0:T(8,128)(2,1)} %values.9) | copy-start | bytes 3145732
  0.7 5.5 %copy-start.7 = (bf16[2,2048,128]{2,1,0:T(8,128)(2,1)S(1)}, bf16[2,2048,128]{2,1,0:T(8,128)(2,1)}, u32[]{:S(2)}) copy-start(bf16[2,2048,128]{2,1,0:T(8,128)(2,1)} %keys.9) | copy-start | bytes 3145732
  0.7 5.5 %copy-start = (bf16[512,4096]{1,0:T(8,128)(2,1)S(1)}, bf16[512,4096]{1,0:T(8,128)(2,1)}, u32[]{:S(2)}) copy-start(bf16[512,4096]{1,0:T(8,128)(2,1)} %w_out.5) | copy-start | bytes 12582916
  0.7 5.5 %copy-start.3 = (bf16[4096,128]{1,0:T(8,128)(2,1)S(1)}, bf16[4096,128]{1,0:T(8,128)(2,1)}, u32[]{:S(2)}) copy-start(bf16[4096,128]{1,0:T(8,128)(2,1)} %w_value.3) | copy-start | bytes 3145732
  0.7 5.5 %copy-start.2 = (bf16[4096,128]{1,0:T(8,128)(2,1)S(1)}, bf16[4096,128]{1,0:T(8,128)(2,1)}, u32[]{:S(2)}) copy-start(bf16[4096,128]{1,0:T(8,128)(2,1)} %w_key.3) | copy-start | bytes 3145732
  0.7 5.5 %copy-start.1 = (bf16[4096,512]{1,0:T(8,128)(2,1)S(1)}, bf16[4096,512]{1,0:T(8,128)(2,1)}, u32[]{:S(2)}) copy-start(bf16[4096,512]{1,0:T(8,128)(2,1)} %w_query.3) | copy-start | bytes 12582916
  0.7 5.5 %copy-start.6 = (bf16[128]{0:T(256)(128)(2,1)S(1)}, bf16[128]{0:T(256)(128)(2,1)}, u32[]{:S(2)}) copy-start(bf16[128]{0:T(256)(128)(2,1)} %param.18) | copy-start | bytes 772
  0.7 5.5 %copy-start.5 = (bf16[128]{0:T(256)(128)(2,1)S(1)}, bf16[128]{0:T(256)(128)(2,1)}, u32[]{:S(2)}) copy-start(bf16[128]{0:T(256)(128)(2,1)} %param.17) | copy-start | bytes 772
  0.7 5.5 %copy-start.10 = (bf16[2,4096]{1,0:T(2,128)(2,1)S(1)}, bf16[2,4096]{1,0:T(2,128)(2,1)}, u32[]{:S(2)}) copy-start(bf16[2,4096]{1,0:T(2,128)(2,1)} %embed.1) | copy-start | bytes 49156
  1.5 7.8 %collective-permute-start.2 = (bf16[8,4096]{1,0:T(8,128)(2,1)S(1)}, bf16[8,4096]{1,0:T(8,128)(2,1)S(1)}, u32[]{:S(2)}, u32[]{:S(2)}) collective-permute-start(bf16[8,4096]{1,0:T(8,128)(2,1)S(1)} %shard_map.141.rows0), channel_id=1, source_target_pairs={{0,48},{8,56},{16,0},{24,8},{32,16},{40,24},{48,32},{56,40},{1,49}... | collective-permute-start | bytes 196616 | tf_op jit(solution)/shard_map/ppermute | solution.py:302
  5.0 4.7 %collective-permute-start.1 = (bf16[8,4096]{1,0:T(8,128)(2,1)S(1)}, bf16[8,4096]{1,0:T(8,128)(2,1)S(1)}, u32[]{:S(2)}, u32[]{:S(2)}) collective-permute-start(bf16[8,4096]{1,0:T(8,128)(2,1)S(1)} %shard_map.141.rows0), channel_id=1, source_target_pairs={{0,32},{8,40},{16,48},{24,56},{32,0},{40,8},{48,16},{56,24},{1,33}... | collective-permute-start | bytes 196616 | tf_op jit(solution)/shard_map/ppermute | solution.py:302
  5.4 5.0 %collective-permute-start = (bf16[8,4096]{1,0:T(8,128)(2,1)S(1)}, bf16[8,4096]{1,0:T(8,128)(2,1)S(1)}, u32[]{:S(2)}, u32[]{:S(2)}) collective-permute-start(bf16[8,4096]{1,0:T(8,128)(2,1)S(1)} %shard_map.141.rows0), channel_id=1, source_target_pairs={{0,16},{8,24},{16,32},{24,40},{32,48},{40,56},{48,0},{56,8},{1,17}... | collective-permute-start | bytes 196616 | tf_op jit(solution)/shard_map/ppermute | solution.py:302
  10.6 3.4 %collective-permute-start.3 = (bf16[4,8,4096]{2,1,0:T(8,128)(2,1)S(1)}, bf16[4,8,4096]{2,1,0:T(8,128)(2,1)S(1)}, u32[]{:S(2)}, u32[]{:S(2)}) collective-permute-start(bf16[4,8,4096]{2,1,0:T(8,128)(2,1)S(1)} %get-tuple-element.22.mine), channel_id=1, source_target_pairs={{0,8},{8,0},{16,24},{24,16},{32,40},{40,32},{48,56},{56,48},{1,9},... | collective-permute-start | bytes 786440 | tf_op jit(solution)/shard_map/ppermute | solution.py:298
  15.0 5.8 %collective-permute-start.4 = (bf16[64,512]{1,0:T(8,128)(2,1)S(1)}, bf16[64,512]{1,0:T(8,128)(2,1)S(1)}, u32[]{:S(2)}, u32[]{:S(2)}) collective-permute-start(bf16[64,512]{1,0:T(8,128)(2,1)S(1)} %get-tuple-element.25._.query), channel_id=1, source_target_pairs={{192,0},{72,8},{208,16},{88,24},{224,32},{104,40},{240,48},{120,56... | collective-permute-start | bytes 196616 | tf_op jit(solution)/shard_map/ppermute | solution.py:312
  19.4 10.2 %collective-permute-start.8 = (bf16[64,512]{1,0:T(8,128)(2,1)S(1)}, bf16[64,512]{1,0:T(8,128)(2,1)S(1)}, u32[]{:S(2)}, u32[]{:S(2)}) collective-permute-start(bf16[64,512]{1,0:T(8,128)(2,1)S(1)} %get-tuple-element.25._.query), channel_id=1, source_target_pairs={{64,0},{200,8},{80,16},{216,24},{96,32},{232,40},{112,48},{248,56}... | collective-permute-start | bytes 196616 | tf_op jit(solution)/shard_map/ppermute | solution.py:312
  19.4 6.6 %collective-permute-start.6 = (bf16[64,512]{1,0:T(8,128)(2,1)S(1)}, bf16[64,512]{1,0:T(8,128)(2,1)S(1)}, u32[]{:S(2)}, u32[]{:S(2)}) collective-permute-start(bf16[64,512]{1,0:T(8,128)(2,1)S(1)} %get-tuple-element.25._.query), channel_id=1, source_target_pairs={{128,0},{136,8},{144,16},{152,24},{160,32},{168,40},{176,48},{184,... | collective-permute-start | bytes 196616 | tf_op jit(solution)/shard_map/ppermute | solution.py:312
  23.1 13.1 %collective-permute-start.5 = (bf16[64,640]{1,0:T(8,128)(2,1)S(1)}, bf16[64,640]{1,0:T(8,128)(2,1)S(1)}, u32[]{:S(2)}, u32[]{:S(2)}) collective-permute-start(bf16[64,640]{1,0:T(8,128)(2,1)S(1)} %shard_map.146._), channel_id=1, source_target_pairs={{0,192},{8,72},{16,208},{24,88},{32,224},{40,104},{48,240},{56,120... | collective-permute-start | bytes 245768 | tf_op jit(solution)/shard_map/ppermute | solution.py:316
  28.4 7.8 %collective-permute-start.7 = (bf16[64,640]{1,0:T(8,128)(2,1)S(1)}, bf16[64,640]{1,0:T(8,128)(2,1)S(1)}, u32[]{:S(2)}, u32[]{:S(2)}) collective-permute-start(bf16[64,640]{1,0:T(8,128)(2,1)S(1)} %shard_map.147._), channel_id=1, source_target_pairs={{0,128},{8,136},{16,144},{24,152},{32,160},{40,168},{48,176},{56,1... | collective-permute-start | bytes 245768 | tf_op jit(solution)/shard_map/ppermute | solution.py:316
  32.0 4.2 %collective-permute-start.9 = (bf16[64,640]{1,0:T(8,128)(2,1)S(1)}, bf16[64,640]{1,0:T(8,128)(2,1)S(1)}, u32[]{:S(2)}, u32[]{:S(2)}) collective-permute-start(bf16[64,640]{1,0:T(8,128)(2,1)S(1)} %shard_map.148._), channel_id=1, source_target_pairs={{0,64},{8,200},{16,80},{24,216},{32,96},{40,232},{48,112},{56,248}... | collective-permute-start | bytes 245768 | tf_op jit(solution)/shard_map/ppermute | solution.py:316
  37.3 3.6 %collective-permute-start.10 = (bf16[4,8,4608]{2,1,0:T(8,128)(2,1)S(1)}, bf16[4,8,4608]{2,1,0:T(8,128)(2,1)S(1)}, u32[]{:S(2)}, u32[]{:S(2)}) collective-permute-start(bf16[4,8,4608]{2,1,0:T(8,128)(2,1)S(1)} %get-tuple-element.33), channel_id=1, source_target_pairs={{0,8},{8,0},{16,24},{24,16},{32,40},{40,32},{48,56},{56,48},{1,9},... | collective-permute-start | bytes 884744 | tf_op jit(solution)/shard_map/ppermute | solution.py:298
  40.9 6.7 %collective-permute-start.11 = (bf16[8,4608]{1,0:T(8,128)(2,1)S(1)}, bf16[8,4608]{1,0:T(8,128)(2,1)S(1)}, u32[]{:S(2)}, u32[]{:S(2)}) collective-permute-start(bf16[8,4608]{1,0:T(8,128)(2,1)S(1)} %get-tuple-element.35), channel_id=1, source_target_pairs={{0,16},{8,24},{16,32},{24,40},{32,48},{40,56},{48,0},{56,8},{1,17}... | collective-permute-start | bytes 221192 | tf_op jit(solution)/shard_map/ppermute | solution.py:302
  41.0 6.6 %collective-permute-start.12 = (bf16[8,4608]{1,0:T(8,128)(2,1)S(1)}, bf16[8,4608]{1,0:T(8,128)(2,1)S(1)}, u32[]{:S(2)}, u32[]{:S(2)}) collective-permute-start(bf16[8,4608]{1,0:T(8,128)(2,1)S(1)} %get-tuple-element.36), channel_id=1, source_target_pairs={{0,32},{8,40},{16,48},{24,56},{32,0},{40,8},{48,16},{56,24},{1,33}... | collective-permute-start | bytes 221192 | tf_op jit(solution)/shard_map/ppermute | solution.py:302
  42.6 5.0 %collective-permute-start.13 = (bf16[8,4608]{1,0:T(8,128)(2,1)S(1)}, bf16[8,4608]{1,0:T(8,128)(2,1)S(1)}, u32[]{:S(2)}, u32[]{:S(2)}) collective-permute-start(bf16[8,4608]{1,0:T(8,128)(2,1)S(1)} %get-tuple-element.37), channel_id=1, source_target_pairs={{0,48},{8,56},{16,0},{24,8},{32,16},{40,24},{48,32},{56,40},{1,49}... | collective-permute-start | bytes 221192 | tf_op jit(solution)/shard_map/ppermute | solution.py:302
  (3 other events, 11.7 us)
